TPU v7x, 256 devices: a whole 4x4x8 slice. The times are simulated.
256 devices in a mesh: seq: 32 (over x, z), head: 8 (over y, core).
Axes of the slice: x: 4, y: 4, z: 8, core: 2. Of those that a mesh axis runs over, the one named last changes fastest.
Arguments:
- queries: bfloat16 [32, 768, 8192], P('seq', None, 'head'), may hold values from -20 to 20
- keys: bfloat16 [32, 768, 8192], P('seq', None, 'head'), may hold values from -2.5 to 2.5
- values: bfloat16 [32, 768, 8192], P('seq', None, 'head'), may hold values from -64 to 64
- log_decay: float32 [32, 768, 64], P('seq', None, 'head'), may hold values from -1 to 0
- gain: float32 [8192], P('head'), may hold values from 0.25 to 1.75
- parents: int32 [32], replicated, may hold values from 15 to 31, as said below
- d_out: bfloat16 [32, 768, 8192], P('seq', None, 'head'), may hold values from -6 to 6
Outputs:
- out: bfloat16 [32, 768, 8192], P('seq', None, 'head')
- d_queries: bfloat16 [32, 768, 8192], P('seq', None, 'head')
- d_keys: bfloat16 [32, 768, 8192], P('seq', None, 'head')
- d_values: bfloat16 [32, 768, 8192], P('seq', None, 'head')
Inputs may be any that keep to these rules, and one draw needn't show every extreme that they name: `parents`: every entry is the last index of some prompt, k * 16 + 15.
All inputs are finite; a program needn't handle non-finite values.
Results may differ from a plain program's by a relative error of at most 0.024.
Values may be sent and summed in bfloat16 or wider, within the bound.
No kernel may reach another device: no remote copies, remote signals or barrier semaphores. Data moves between devices by JAX's collectives and lax.ppermute only.
A program may use at most 192 MiB of HBM per device.

v0:
```python
import jax
import jax.numpy as jnp
from jax import lax
from jax.sharding import PartitionSpec as P

H = 64
HD = 128
BLK = 256
PROMPTS = 2
P_DEV = 512


epsilon = 1e-05


def entering(array, axis, combine, identity, reverse):
    devices, index = (lax.axis_size(axis), lax.axis_index(axis))
    everything = jax.tree.map(
        lambda part, kind: lax.all_gather(part.astype(kind), axis),
        array,
        (jnp.bfloat16, jnp.bfloat16),
    )
    start = jax.tree.map(
        lambda part, zero: jnp.broadcast_to(jnp.asarray(zero, part.dtype), part.shape),
        array,
        identity,
    )

    def turn(k, before):
        at = devices - 1 - k if reverse else k
        reached = at > index if reverse else at < index
        new = combine(
            before, jax.tree.map(lambda part, own: part[at].astype(own.dtype), everything, array)
        )
        return jax.tree.map(lambda a, b: jnp.where(reached, a, b), new, before)

    return lax.fori_loop(0, devices, turn, start)


def block_masks(decay_block):
    cumulative = jnp.cumsum(decay_block, axis=0)
    block_end = cumulative[-1]
    transposed = cumulative.T
    log_gaps = transposed[:, :, None] - transposed[:, None, :]
    extent = decay_block.shape[0]
    row_ids = lax.broadcasted_iota(jnp.int32, (extent, extent), 0)
    col_ids = lax.broadcasted_iota(jnp.int32, (extent, extent), 1)
    causal = (row_ids >= col_ids)[None]
    decay_mask = jnp.where(causal, jnp.exp(jnp.where(causal, log_gaps, 0.0)), 0.0)
    return (cumulative, block_end, decay_mask)


def scaled_keys(key_block, cumulative, block_end):
    return (
        key_block.astype(jnp.float32) * jnp.exp(block_end[None, :] - cumulative)[:, :, None]
    ).astype(jnp.bfloat16)


def scaled_queries(query_block, cumulative):
    return (query_block.astype(jnp.float32) * jnp.exp(cumulative)[:, :, None]).astype(jnp.bfloat16)


def state_term(key_block, value_block, cumulative, block_end):
    key_scaled = scaled_keys(key_block, cumulative, block_end)
    return jnp.einsum("uhd,uhe->hde", key_scaled, value_block, preferred_element_type=jnp.float32)


def block_output(query_block, key_block, value_block, cumulative, decay_mask, start_round):
    scores = jnp.einsum("thd,uhd->htu", query_block, key_block, preferred_element_type=jnp.float32)
    weights = (scores * decay_mask).astype(jnp.bfloat16)
    within = jnp.einsum("htu,uhe->the", weights, value_block, preferred_element_type=jnp.float32)
    query_scaled = scaled_queries(query_block, cumulative)
    across = jnp.einsum(
        "thd,hde->the", query_scaled, start_round, preferred_element_type=jnp.float32
    )
    return within + across


def block_grads(
    query_block,
    key_block,
    value_block,
    cumulative,
    block_end,
    decay_mask,
    start_round,
    grad_out,
    end_grad,
):
    scores = jnp.einsum("thd,uhd->htu", query_block, key_block, preferred_element_type=jnp.float32)
    weights = (scores * decay_mask).astype(jnp.bfloat16)
    key_scaled = scaled_keys(key_block, cumulative, block_end)
    end_round = end_grad.astype(jnp.bfloat16)
    weight_grad = jnp.einsum(
        "the,uhe->htu", grad_out, value_block, preferred_element_type=jnp.float32
    )
    score_grad = (weight_grad * decay_mask).astype(jnp.bfloat16)
    grad_values = jnp.einsum("htu,the->uhe", weights, grad_out, preferred_element_type=jnp.float32)
    grad_values = grad_values + jnp.einsum(
        "uhd,hde->uhe", key_scaled, end_round, preferred_element_type=jnp.float32
    )
    grad_queries = jnp.einsum(
        "htu,uhd->thd", score_grad, key_block, preferred_element_type=jnp.float32
    )
    grad_queries = grad_queries + jnp.exp(cumulative)[:, :, None] * jnp.einsum(
        "the,hde->thd", grad_out, start_round, preferred_element_type=jnp.float32
    )
    grad_keys = jnp.einsum(
        "htu,thd->uhd", score_grad, query_block, preferred_element_type=jnp.float32
    )
    decay_per_key = jnp.exp(block_end[None, :] - cumulative)[:, :, None]
    grad_keys = grad_keys + decay_per_key * jnp.einsum(
        "uhe,hde->uhd", value_block, end_round, preferred_element_type=jnp.float32
    )
    return (grad_queries, grad_keys, grad_values)


def link(earlier, later):
    return (earlier[0] * later[0], later[0][:, None, None] * earlier[1] + later[1])


def local(queries, keys, values, log_decay, gain, parents, d_out):
    row_count = queries.shape[1]
    columns = queries.shape[2]
    heads_here = columns // HD
    prompt_count = P_DEV // BLK
    total_count = row_count // BLK
    block_shape = (total_count, BLK, heads_here, HD)
    query_blocks = queries[0].reshape(block_shape)
    key_blocks = keys[0].reshape(block_shape)
    value_blocks = values[0].reshape(block_shape)
    decay_blocks = log_decay[0].reshape(total_count, BLK, heads_here)
    seq_count = lax.axis_size("seq")
    span = seq_count // PROMPTS
    position = lax.axis_index("seq")
    parent = lax.dynamic_index_in_dim(parents, position, 0, keepdims=False)
    last_keep = jnp.where(position % span == span - 1, 0.0, 1.0)
    first_keep = jnp.where(position % span == 0, 0.0, 1.0)
    prepared = [block_masks(decay_blocks[number]) for number in range(total_count)]
    cumulatives = [item[0] for item in prepared]
    block_ends = [item[1] for item in prepared]
    decay_masks = [item[2] for item in prepared]
    end_decays = [jnp.exp(item[1]) for item in prepared]
    state_terms = [
        state_term(
            key_blocks[number], value_blocks[number], cumulatives[number], block_ends[number]
        )
        for number in range(prompt_count)
    ]
    zero_state = jnp.zeros((heads_here, HD, HD), jnp.float32)
    summary = zero_state
    log_total = jnp.zeros((heads_here,), jnp.float32)
    for number in range(prompt_count):
        summary = end_decays[number][:, None, None] * summary + state_terms[number]
        log_total = log_total + block_ends[number]
    decay_dev = jnp.exp(log_total)
    identity = (jnp.ones((heads_here,), jnp.float32), zero_state)
    incoming = entering((decay_dev * last_keep, summary * last_keep), "seq", link, identity, False)[
        1
    ]
    starts = []
    running = incoming
    for number in range(prompt_count):
        starts.append(running.astype(jnp.bfloat16))
        running = end_decays[number][:, None, None] * running + state_terms[number]
    end_states_all = lax.all_gather(running.astype(jnp.bfloat16)[None], "seq", axis=0, tiled=True)
    response_start = lax.dynamic_index_in_dim(end_states_all, parent, 0, keepdims=False)
    running = response_start.astype(jnp.float32)
    number = 2
    starts.append(running.astype(jnp.bfloat16))
    outputs = [
        block_output(
            query_blocks[number],
            key_blocks[number],
            value_blocks[number],
            cumulatives[number],
            decay_masks[number],
            starts[number],
        )
        for number in range(total_count)
    ]
    attended = jnp.concatenate(outputs, axis=0)
    gain_cols = gain.reshape(heads_here, HD)
    weighted = gain_cols * d_out[0].reshape(row_count, heads_here, HD).astype(jnp.float32)
    squares, products = lax.psum(
        (jnp.sum(attended * attended, axis=(1, 2)), jnp.sum(weighted * attended, axis=(1, 2))),
        "head",
    )
    inverse = lax.rsqrt(squares / (H * HD) + epsilon)[:, None, None]
    out = (attended * inverse * gain_cols).astype(jnp.bfloat16).reshape(1, row_count, columns)
    grad_attended = inverse * weighted - attended * inverse * inverse * inverse * products[
        :, None, None
    ] / (H * HD)
    grad_blocks = grad_attended.astype(jnp.bfloat16).reshape(block_shape)
    grad_terms = []
    for number in range(total_count):
        query_scaled = scaled_queries(query_blocks[number], cumulatives[number])
        grad_terms.append(
            jnp.einsum(
                "thd,the->hde",
                query_scaled,
                grad_blocks[number],
                preferred_element_type=jnp.float32,
            )
        )
    gradients = [None] * total_count
    carried = zero_state
    for number in reversed(range(prompt_count, total_count)):
        gradients[number] = block_grads(
            query_blocks[number],
            key_blocks[number],
            value_blocks[number],
            cumulatives[number],
            block_ends[number],
            decay_masks[number],
            starts[number],
            grad_blocks[number],
            carried,
        )
        carried = end_decays[number][:, None, None] * carried + grad_terms[number]
    one_hot = (jnp.arange(seq_count, dtype=jnp.int32) == parent).astype(jnp.float32)
    slot_terms = one_hot[:, None, None, None] * carried[None]
    subtree_limb = lax.psum_scatter(
        slot_terms.astype(jnp.bfloat16), "seq", scatter_dimension=0, tiled=True
    ).astype(jnp.float32)[0]
    local_sum = zero_state
    for number in reversed(range(prompt_count)):
        local_sum = end_decays[number][:, None, None] * local_sum + grad_terms[number]
    element = (local_sum + decay_dev[:, None, None] * subtree_limb) * first_keep
    from_later = entering((decay_dev * first_keep, element), "seq", link, identity, True)[1]
    carried = subtree_limb + from_later
    for number in reversed(range(prompt_count)):
        gradients[number] = block_grads(
            query_blocks[number],
            key_blocks[number],
            value_blocks[number],
            cumulatives[number],
            block_ends[number],
            decay_masks[number],
            starts[number],
            grad_blocks[number],
            carried,
        )
        carried = end_decays[number][:, None, None] * carried + grad_terms[number]
    d_queries = (
        jnp.concatenate([item[0] for item in gradients], axis=0)
        .astype(jnp.bfloat16)
        .reshape(1, row_count, columns)
    )
    d_keys = (
        jnp.concatenate([item[1] for item in gradients], axis=0)
        .astype(jnp.bfloat16)
        .reshape(1, row_count, columns)
    )
    d_values = (
        jnp.concatenate([item[2] for item in gradients], axis=0)
        .astype(jnp.bfloat16)
        .reshape(1, row_count, columns)
    )
    return (out, d_queries, d_keys, d_values)


def solution(mesh):
    in_specs = (
        P("seq", None, "head"),
        P("seq", None, "head"),
        P("seq", None, "head"),
        P("seq", None, "head"),
        P("head"),
        P(),
        P("seq", None, "head"),
    )
    out_specs = (
        P("seq", None, "head"),
        P("seq", None, "head"),
        P("seq", None, "head"),
        P("seq", None, "head"),
    )
    return jax.shard_map(local, mesh=mesh, in_specs=in_specs, out_specs=out_specs, check_vma=False)
```

profile of v0, /device:TPU:32, one launch (start us, length us, event | category | flops | bytes accessed | tf_op | source)
XLA Modules:
  0.0 657.8 jit_solution(2313990045373655468)
XLA Ops:
  10.6 2.3 fusion.71
  15.1 1.2 multiply_convert_fusion.15
  17.2 40.0 %all-gather.3 = bf16[32,1,8]{2,1,0:T(2,128)(2,1)S(1)} all-gather(bf16[1,1,8]{2,1,0:T(2,128)(2,1)S(1)} %bitcast.285), channel_id=1, replica_groups=mesh['seq'=32,'head'=8] {'seq'}, dimensions={0}, use_global_device_ids=true | all-gather | bytes 528 | tf_op jit(solution)/shard_map/all_gather | solution.py:19
  57.2 58.4 %all-gather.9.cloned.1.call-done = bf16[256,128,128]{2,1,0:T(8,128)(2,1)} async-done(((bf16[8,128,128]{2,1,0:T(8,128)(2,1)}), bf16[256,128,128]{2,1,0:T(8,128)(2,1)}) %all-gather.9.cloned.1.call-update) | async-done | bytes 8388624 | tf_op jit(solution)/shard_map/all_gather | solution.py:19
  115.6 36.4 %while.30 = (s32[]{:T(128)}, f32[8,128,128]{2,1,0:T(8,128)S(1)}, s32[]{:T(128)}, bf16[32,8]{1,0:T(8,128)(2,1)S(1)}, bf16[32,8,128,128]{3,2,1,0:T(8,128)(2,1)}, /*index=5*/s32[]{:T(128)}, s32[]{:T(128)}) while((s32[]{:T(128)}, f32[8,128,128]{2,1,0:T(8,128)S(1)}, s32[]{:T(128)}, bf16[32,8]{1,0:T(8,128)(2,1)S(1)}, ...), condition=%wide.region_5.6_spmd.clone, body=%wide.region_4.5_spmd.clone.sunk | while | flops 655372 | bytes 1310913 | solution.py:37
  116.7 1.1 fusion.114
  119.0 1.1 fusion.114
  120.1 1.1 fusion.114
  121.3 1.1 fusion.114
  122.4 1.1 fusion.114
  140.6 1.1 fusion.114
  141.8 1.1 fusion.114
  142.9 1.1 fusion.114
  144.0 1.1 fusion.114
  152.0 1.9 add_convert_fusion.1
  155.7 2.6 fusion.70
  158.3 2.0 copy.293
  160.4 2.0 copy.294
  164.2 1.3 copy.292
  165.5 2.3 copy.288
  167.8 3.1 copy.221
  171.4 1.1 compare_convert_fusion
  178.0 1.5 convolution_bitcast_fusion.17
  179.4 1.5 convolution_bitcast_fusion.15
  181.2 1.4 copy.219
  182.6 1.6 fusion.16
  184.2 1.3 copy.218
  185.5 64.2 %all-gather.11.cloned.1.call-done = bf16[256,128,128]{2,1,0:T(8,128)(2,1)} async-done(((bf16[8,128,128]{2,1,0:T(8,128)(2,1)}), bf16[256,128,128]{2,1,0:T(8,128)(2,1)}) %all-gather.11.cloned.1.call-update) | async-done | bytes 8388624 | tf_op jit(solution)/shard_map/all_gather | solution.py:166
  249.7 1.8 fusion.14
  251.5 1.9 multiply_reduce_fusion.1
  253.4 1.3 copy.220
  254.7 2.5 multiply_reduce_fusion
  257.3 14.6 %all-reduce = (f32[768]{0:T(1024)S(1)}, f32[768]{0:T(1024)S(1)}) all-reduce(f32[768]{0:T(1024)S(1)} %multiply_reduce_fusion.1, f32[768]{0:T(1024)S(1)} %multiply_reduce_fusion), channel_id=1, replica_groups=mesh['seq'=32,'head'=8] {'head'}, use_global_device_ids=true, to_apply=%region_9.10 | all-reduce | flops 1536 | bytes 12288 | tf_op jit(solution)/shard_map/psum | solution.py:185
  271.9 3.3 subtract_convert_fusion
  275.6 5.5 multiply_convert_fusion
  282.1 1.1 fusion.32
  283.3 222.8 %reduce-scatter.2.cloned.1.call-done = bf16[1,8,128,128]{3,2,1,0:T(8,128)(2,1)} async-done(((bf16[32,8,128,128]{3,2,1,0:T(8,128)(2,1)}), bf16[1,8,128,128]{3,2,1,0:T(8,128)(2,1)}) %reduce-scatter.2.cloned.1.call-update) | async-done | bytes 262160 | tf_op jit(solution)/shard_map/reduce_scatter | solution.py:223
  506.1 2.3 fusion.28
  508.4 37.8 %all-gather.4 = bf16[32,1,8]{2,1,0:T(2,128)(2,1)S(1)} all-gather(bf16[1,1,8]{2,1,0:T(2,128)(2,1)S(1)} %bitcast.284), channel_id=1, replica_groups=mesh['seq'=32,'head'=8] {'seq'}, dimensions={0}, use_global_device_ids=true | all-gather | bytes 528 | tf_op jit(solution)/shard_map/all_gather | solution.py:19
  546.9 1.9 multiply_convert_fusion.2
  549.3 1.3 fusion.19
  554.8 1.2 pad_maximum_fusion.2
  556.1 2.6 copy.249
  558.7 1.7 fusion.34
  561.7 3.5 multiply_convert_fusion.1
  567.3 1.3 convolution_bitcast_fusion.10
  568.6 1.3 convolution_bitcast_fusion.11
  569.9 1.3 fusion.39
  571.2 1.3 fusion.44
  572.5 32.0 %all-gather.13.cloned.1.call-done = bf16[256,128,128]{2,1,0:T(8,128)(2,1)} async-done(((bf16[8,128,128]{2,1,0:T(8,128)(2,1)}), bf16[256,128,128]{2,1,0:T(8,128)(2,1)}) %all-gather.13.cloned.1.call-update) | async-done | bytes 8388624 | tf_op jit(solution)/shard_map/all_gather | solution.py:19
  604.5 36.7 %while.31 = (s32[]{:T(128)}, f32[8,128,128]{2,1,0:T(8,128)S(1)}, s32[]{:T(128)}, bf16[32,8]{1,0:T(8,128)(2,1)S(1)}, bf16[32,8,128,128]{3,2,1,0:T(8,128)(2,1)}, /*index=5*/s32[]{:T(128)}, s32[]{:T(128)}, s32[]{:T(128)}, s32[]{:T(128)}) while((s32[]{:T(128)}, f32[8,128,128]{2,1,0:T(8,128)S(1)}, s32[]{:T(128)}, ...), condition=%wide.region_14.15_spmd.clone, body=%wide.region_13.14_spmd.clone.sunk | while | flops 655376 | bytes 1310975 | solution.py:37
  604.6 1.1 fusion.115
  605.8 1.1 fusion.115
  606.9 1.1 fusion.115
  613.8 1.1 fusion.115
  620.7 1.1 fusion.115
  627.5 1.1 fusion.115
  628.7 1.1 fusion.115
  635.5 1.1 fusion.115
  641.3 1.4 add_convert_fusion
  644.0 1.6 copy.250
  645.6 2.5 fusion.24
  648.2 1.3 copy.247
  650.0 1.3 pad_maximum_fusion.4
  (310 shorter events, 78.5 us)
Async XLA Ops:
  7.2 108.4 %all-gather.9.cloned.1.call-start = ((), (), s32[]{:S(2)}) async-start(), calls=%async_computation.2 | async-start | bytes 8650752 | tf_op jit(solution)/shard_map/all_gather | solution.py:19
  9.6 3.3 copy-start.45
  10.5 141.5 %copy-start.53 = (f32[8]{0:T(128)}, f32[8]{0:T(128)S(1)}, u32[]{:S(2)}) copy-start(f32[8]{0:T(128)S(1)} %get-tuple-element.358) | copy-start | bytes 100
  10.5 141.5 %copy-start.57 = (f32[8]{0:T(128)}, f32[8]{0:T(128)S(1)}, u32[]{:S(2)}) copy-start(f32[8]{0:T(128)S(1)} %get-tuple-element.357) | copy-start | bytes 100
  14.1 163.8 %copy-start.4 = (bf16[1,256,1024]{1,2,0:T(8,128)(2,1)}, bf16[1,256,1024]{1,2,0:T(8,128)(2,1)S(1)}, u32[]{:S(2)}) copy-start(bf16[1,256,1024]{1,2,0:T(8,128)(2,1)S(1)} %copy.197) | copy-start | bytes 1572868
  14.5 162.9 %copy-start.10 = (bf16[1,256,1024]{1,2,0:T(8,128)(2,1)}, bf16[1,256,1024]{1,2,0:T(8,128)(2,1)S(1)}, u32[]{:S(2)}) copy-start(bf16[1,256,1024]{1,2,0:T(8,128)(2,1)S(1)} %copy.291) | copy-start | bytes 1572868
  14.7 159.6 %copy-start.7 = (bf16[1,256,1024]{1,2,0:T(8,128)(2,1)}, bf16[1,256,1024]{1,2,0:T(8,128)(2,1)S(1)}, u32[]{:S(2)}) copy-start(bf16[1,256,1024]{1,2,0:T(8,128)(2,1)S(1)} %copy.290) | copy-start | bytes 1572868
  16.3 233.4 %all-gather.11.cloned.1.call-start = ((), (), s32[]{:S(2)}) async-start(), calls=%async_computation.3 | async-start | bytes 8650752 | tf_op jit(solution)/shard_map/all_gather | solution.py:166
  152.0 2.0 copy-start.62
  154.0 352.1 %reduce-scatter.2.cloned.1.call-start = ((), (), s32[]{:S(2)}) async-start(), calls=%async_computation.1 | async-start | bytes 8650752 | tf_op jit(solution)/shard_map/reduce_scatter | solution.py:223
  155.7 7.4 %copy-start.42 = (bf16[1,256,1024]{2,1,0:T(8,128)(2,1)S(1)}, bf16[1,256,1024]{2,1,0:T(8,128)(2,1)}, u32[]{:S(2)}) copy-start(bf16[1,256,1024]{2,1,0:T(8,128)(2,1)} %get-tuple-element.349) | copy-start | bytes 1572868
  163.2 9.3 %copy-start.47 = (f32[8,2]{0,1:T(2,128)}, f32[8,2]{0,1:T(2,128)S(1)}, u32[]{:S(2)}) copy-start(f32[8,2]{0,1:T(2,128)S(1)} %slice.124) | copy-start | bytes 196
  165.5 15.4 %copy-start.13 = (bf16[1,256,1024]{1,2,0:T(8,128)(2,1)}, bf16[1,256,1024]{1,2,0:T(8,128)(2,1)S(1)}, u32[]{:S(2)}) copy-start(bf16[1,256,1024]{1,2,0:T(8,128)(2,1)S(1)} %copy.292) | copy-start | bytes 1572868
  172.8 1.5 copy-start.56
  174.1 2.0 copy-start.52
  174.3 1.0 copy-start.19
  175.1 2.3 copy-start.29
  175.3 1.1 copy-start.16
  175.4 1.3 copy-start.24
  176.1 1.8 copy-start.27
  177.4 2.0 copy-start.31
  177.4 2.0 copy-start.22
  180.9 1.7 copy-start.20
  181.2 1.4 copy-start.2
  184.2 67.3 %copy-start = (f32[256,8,128]{0,2,1:T(8,128)}, f32[256,8,128]{0,2,1:T(8,128)S(1)}, u32[]{:S(2)}) copy-start(f32[256,8,128]{0,2,1:T(8,128)S(1)} %fusion.16) | copy-start | bytes 3145732
  251.5 3.2 copy-start.1
  251.5 3.2 copy-start.46
  253.4 1.3 copy-start.3
  271.9 3.4 copy-start.17
  271.9 3.4 copy-start.63
  271.9 3.7 copy-start.59
  281.1 1.0 copy-start.14
  281.1 225.0 %copy-start.58 = (f32[8]{0:T(128)S(1)}, f32[8]{0:T(128)}, u32[]{:S(2)}) copy-start(f32[8]{0:T(128)} %copy-done.57) | copy-start | bytes 100
  281.1 225.0 %copy-start.60 = (f32[8]{0:T(128)S(1)}, f32[8]{0:T(128)}, u32[]{:S(2)}) copy-start(f32[8]{0:T(128)} %get-tuple-element.354) | copy-start | bytes 100
  281.1 225.0 %copy-start.61 = (f32[8]{0:T(128)S(1)}, f32[8]{0:T(128)}, u32[]{:S(2)}) copy-start(f32[8]{0:T(128)} %get-tuple-element.355) | copy-start | bytes 100
  281.1 227.3 %copy-start.55 = (bf16[8]{0:T(256)(128)(2,1)S(1)}, bf16[8]{0:T(256)(128)(2,1)}, u32[]{:S(2)}) copy-start(bf16[8]{0:T(256)(128)(2,1)} %get-tuple-element.310) | copy-start | bytes 52
  281.1 323.4 %all-gather.13.cloned.1.call-start = ((), (), s32[]{:S(2)}) async-start(), calls=%async_computation.4 | async-start | bytes 8650752 | tf_op jit(solution)/shard_map/all_gather | solution.py:19
  546.9 1.9 copy-start.25
  548.8 1.8 copy-start.34
  548.8 1.8 copy-start.11
  548.8 1.8 copy-start.49
  550.7 1.0 copy-start.5
  550.7 1.0 copy-start.51
  551.7 1.4 copy-start.8
  558.7 1.7 copy-start.26
  561.7 3.5 copy-start.18
  561.7 3.5 copy-start.35
  565.2 1.1 copy-start.23
  565.2 2.1 copy-start.15
  565.2 2.1 copy-start.39
  566.3 2.4 copy-start.21
  566.3 2.4 copy-start.37
  567.3 2.6 copy-start.30
  568.6 2.6 copy-start.28
  604.5 36.7 %copy-start.54 = (f32[8]{0:T(128)S(1)}, f32[8]{0:T(128)}, u32[]{:S(2)}) copy-start(f32[8]{0:T(128)} %copy-done.53) | copy-start | bytes 100
  604.5 38.1 %copy-start.6 = (bf16[1,256,1024]{1,2,0:T(8,128)(2,1)S(1)}, bf16[1,256,1024]{1,2,0:T(8,128)(2,1)}, u32[]{:S(2)}) copy-start(bf16[1,256,1024]{1,2,0:T(8,128)(2,1)} %copy-done.4) | copy-start | bytes 1572868
  641.2 1.5 copy-start.33
  641.2 1.8 copy-start.12
  641.2 1.9 copy-start.40
  641.3 1.9 copy-start.41
  642.7 1.2 copy-start.44
  644.0 1.6 copy-start.9
  645.6 3.9 copy-start.32
  648.2 1.9 copy-start.43
  (4 other events, 3.6 us)
Sparse Core Ops, SparseCore 0:
  16.4 99.1 all-gather.8
  154.1 95.5 all-gather.10
  281.2 224.8 reduce-scatter.1
  508.9 95.6 all-gather.12
where the time goes:
time: 663 us; the launch traced here: 658 us
  waiting for transfers between devices  377 us (57%)
  other arithmetic  100 us (15%)
  blocking collectives  92.5 us (14%)
  local copies, waits for them, and re-layouts  35.7 us (5%)
  matrix products  33.2 us (5%)
  between operations  16.3 us (2%)
    reduce_scatter x1, waiting for transfers between devices, local(): lax.psum_scatter(slot_terms.astype(jnp.bfloat16), 'seq', scatter_dimensio...  223 us
    all_gather x2, waiting for transfers between devices, entering(): lax.all_gather(part.astype(kind), axis)  90.4 us
    all_gather x2, blocking collectives, entering(): lax.all_gather(part.astype(kind), axis)  77.9 us
    select_n x64, other arithmetic, turn(): return jax.tree.map(lambda a, b: jnp.where(reached, a, b), new, before)  70 us
    all_gather x1, waiting for transfers between devices, local(): lax.all_gather(running.astype(jnp.bfloat16)[None], 'seq', axis=0, tiled=T...  64.2 us
    unnamed x139, local copies, waits for them, and re-layouts  16.8 us
    psum x1, blocking collectives, local(): lax.psum((jnp.sum(attended * attended, axis=(1, 2)), jnp.sum(weighted * a...  14.6 us
  transfers between devices with their start and end apart: 4, of which 4 were waited for; matrix products, arithmetic and copies ran while one was open for 8% of the time, Pallas kernels for 0%

commit v1 on v0

v1 whole, which is shorter than its diff:
```python
import jax
import jax.numpy as jnp
from jax import lax
from jax.experimental import pallas as pl
from jax.experimental.pallas import tpu as pltpu
from jax.sharding import PartitionSpec as P

H = 64
HD = 128
BLK = 256
PROMPTS = 2
P_DEV = 512
ROWS = 768
HL = 8
N_SEQ = 32
SPAN = N_SEQ // PROMPTS
COLS = HL * HD
PIECE = HL * HD // N_SEQ
EPS = 1e-05

F32 = jnp.float32
BF16 = jnp.bfloat16


def params(mib=32):
    return pltpu.CompilerParams(
        dimension_semantics=("arbitrary",), vmem_limit_bytes=mib * 1024 * 1024
    )


def dot(a, b, dims):
    return lax.dot_general(a, b, (dims, ((), ())), preferred_element_type=F32)


def mm(a, b):
    return dot(a, b, ((1,), (0,)))


def mm_nt(a, b):
    return dot(a, b, ((1,), (1,)))


def mm_tn(a, b):
    return dot(a, b, ((0,), (0,)))


def rows(number):
    return slice(number * BLK, (number + 1) * BLK)


def column(cum_ref, number, head):
    block = pltpu.roll(cum_ref[rows(number), :], lax.rem(HD - head, HD), 1)
    return block[:, 0:1]


def rounded_product(block, factor):
    return (block.astype(F32) * factor).astype(BF16)


def summary_kernel(decay_ref, keys_ref, values_ref, send_ref, term_ref, cum_ref, cum_rows_ref):
    head = pl.program_id(0)

    @pl.when(head == 0)
    def _():
        cum_ref[...] = jnp.zeros_like(cum_ref)
        for number in range(ROWS // BLK):
            total = decay_ref[0, rows(number), :]
            row_ids = lax.broadcasted_iota(jnp.int32, total.shape, 0)
            shift = 1
            while shift < BLK:
                moved = pltpu.roll(total, shift, 0)
                total = total + jnp.where(row_ids >= shift, moved, 0.0)
                shift *= 2
            cum_ref[rows(number), 0:HL] = total
        for tile in range(ROWS // HD):
            part = slice(tile * HD, (tile + 1) * HD)
            turned = cum_ref[part, :].T
            for each in range(HL):
                cum_rows_ref[each, :, part] = turned[each : each + 1, :]

    terms = []
    ends = []
    for number in range(2):
        col = column(cum_ref, number, head)
        end = col[BLK - 1 : BLK, :]
        key_scaled = rounded_product(keys_ref[0, rows(number), :], jnp.exp(end - col))
        terms.append(mm_tn(key_scaled, values_ref[0, rows(number), :]))
        ends.append(end)
    term_ref[0] = terms[0]
    summary = jnp.exp(ends[1]) * terms[0] + terms[1]
    send_ref[:, 0:PIECE, :] = summary.astype(BF16).reshape(HD // PIECE, PIECE, HD)
    decay = jnp.broadcast_to(jnp.exp(ends[0] + ends[1]), (16, HD))
    coarse = decay.astype(BF16)
    fine = (decay - coarse.astype(F32)).astype(BF16)
    row_ids = lax.broadcasted_iota(jnp.int32, (16, HD), 0)
    packed = jnp.where(
        row_ids == 0, coarse.astype(F32), jnp.where(row_ids == 1, fine.astype(F32), 0.0)
    ).astype(BF16)
    for piece in range(HD // PIECE):
        send_ref[piece, PIECE : PIECE + 16, :] = packed


def within_kernel(cum_ref, cum_rows_ref, queries_ref, keys_ref, values_ref, within_ref):
    head = pl.program_id(0)
    row_ids = lax.broadcasted_iota(jnp.int32, (BLK, BLK), 0)
    col_ids = lax.broadcasted_iota(jnp.int32, (BLK, BLK), 1)
    for number in range(ROWS // BLK):
        col = column(cum_ref, number, head)
        gaps = col - cum_rows_ref[0, :, rows(number)]
        mask = jnp.where(row_ids >= col_ids, jnp.exp(gaps), 0.0)
        scores = mm_nt(queries_ref[0, rows(number), :], keys_ref[0, rows(number), :])
        weights = (scores * mask).astype(BF16)
        within_ref[rows(number), :] = mm(weights, values_ref[0, rows(number), :])


def forward_scan_kernel(parents_ref, got_ref, send_ref, decay_ref):
    totals = []
    for prompt in range(PROMPTS):
        carry = jnp.zeros((PIECE, HD), F32)
        for index in range(prompt * SPAN, (prompt + 1) * SPAN):
            packed = got_ref[index, PIECE : PIECE + 16, :].astype(F32)
            decay = packed[0:1, :] + packed[1:2, :]
            decay_ref[index : index + 1, :] = decay
            send_ref[index, 0:PIECE, :] = carry.astype(BF16)
            carry = decay * carry + got_ref[index, 0:PIECE, :].astype(F32)
        totals.append(carry)
    for index in range(N_SEQ):
        prompt = parents_ref[index] // SPAN
        chosen = jnp.where(prompt == 0, totals[0], totals[1])
        send_ref[index, PIECE : 2 * PIECE, :] = chosen.astype(BF16)


def attend_kernel(
    cum_ref, queries_ref, d_out_ref, gain_ref, within_ref, starts_ref, term_ref,
    attended_ref, second_ref, stats_ref, squares_ref, products_ref,
):
    head = pl.program_id(0)

    @pl.when(head == 0)
    def _():
        squares_ref[...] = jnp.zeros_like(squares_ref)
        products_ref[...] = jnp.zeros_like(products_ref)

    first = starts_ref[:, 0:PIECE, :].reshape(HD, HD)
    reply = starts_ref[:, PIECE : 2 * PIECE, :].reshape(HD, HD)
    end = column(cum_ref, 0, head)[BLK - 1 : BLK, :]
    second = (jnp.exp(end) * first.astype(F32) + term_ref[0]).astype(BF16)
    second_ref[0] = second
    for number, start in enumerate((first, second, reply)):
        col = column(cum_ref, number, head)
        query_scaled = rounded_product(queries_ref[0, rows(number), :], jnp.exp(col))
        attended = within_ref[rows(number), :] + mm(query_scaled, start)
        attended_ref[rows(number), :] = attended
        weighted = gain_ref[...] * d_out_ref[0, rows(number), :].astype(F32)
        squares_ref[rows(number), :] += attended * attended
        products_ref[rows(number), :] += weighted * attended

    @pl.when(head == HL - 1)
    def _():
        stats_ref[...] = jnp.zeros_like(stats_ref)
        for tile in range(ROWS // HD):
            part = slice(tile * HD, (tile + 1) * HD)
            for base, sums_ref in ((0, squares_ref), (8, products_ref)):
                row = jnp.sum(sums_ref[part, :].T, axis=0, keepdims=True)
                stats_ref[:, base + tile : base + tile + 1, :] = jnp.broadcast_to(
                    row[None], (HL, 1, HD)
                )


def row_factors(stats_ref, inverse_ref, slope_ref):
    total = stats_ref[0]
    for source in range(1, HL):
        total = total + stats_ref[source]
    turned = jnp.concatenate([total, jnp.zeros((HD - 16, HD), F32)], axis=0).T
    for tile in range(ROWS // HD):
        part = slice(tile * HD, (tile + 1) * HD)
        squares = jnp.broadcast_to(turned[:, tile : tile + 1], (HD, HD))
        products = jnp.broadcast_to(turned[:, 8 + tile : 9 + tile], (HD, HD))
        inverse = lax.rsqrt(squares / (H * HD) + EPS)
        inverse_ref[part, :] = inverse
        if slope_ref is not None:
            slope_ref[part, :] = inverse * inverse * inverse * products / (H * HD)


def grad_kernel(
    cum_ref, queries_ref, d_out_ref, gain_ref, attended_ref, stats_ref,
    grad_ref, send_ref, term_ref, inverse_out_ref, inverse_ref, slope_ref,
):
    head = pl.program_id(0)

    @pl.when(head == 0)
    def _():
        row_factors(stats_ref, inverse_ref, slope_ref)
        inverse_out_ref[...] = inverse_ref[...]

    terms = []
    for number in range(ROWS // BLK):
        weighted = gain_ref[...] * d_out_ref[0, rows(number), :].astype(F32)
        grad = (
            inverse_ref[rows(number), :] * weighted
            - attended_ref[rows(number), :] * slope_ref[rows(number), :]
        ).astype(BF16)
        grad_ref[rows(number), :] = grad
        col = column(cum_ref, number, head)
        query_scaled = rounded_product(queries_ref[0, rows(number), :], jnp.exp(col))
        terms.append(mm_tn(query_scaled, grad))
    end = column(cum_ref, 0, head)[BLK - 1 : BLK, :]
    local_sum = jnp.exp(end) * terms[1] + terms[0]
    term_ref[0] = terms[1]
    send_ref[:, 0:PIECE, :] = local_sum.astype(BF16).reshape(HD // PIECE, PIECE, HD)
    send_ref[:, PIECE : 2 * PIECE, :] = terms[2].astype(BF16).reshape(HD // PIECE, PIECE, HD)


def backward_scan_kernel(parents_ref, got_ref, decay_ref, send_ref):
    branches = [jnp.zeros((PIECE, HD), F32) for _ in range(PROMPTS)]
    for index in range(N_SEQ):
        prompt = parents_ref[index] // SPAN
        start_grad = got_ref[index, PIECE : 2 * PIECE, :].astype(F32)
        for each in range(PROMPTS):
            branches[each] = branches[each] + jnp.where(prompt == each, start_grad, 0.0)
    for prompt in range(PROMPTS):
        carry = branches[prompt]
        for index in reversed(range(prompt * SPAN, (prompt + 1) * SPAN)):
            send_ref[index] = carry.astype(BF16)
            carry = decay_ref[index : index + 1, :] * carry + got_ref[index, 0:PIECE, :].astype(F32)


def local_grads_kernel(
    cum_ref, cum_rows_ref, queries_ref, keys_ref, values_ref, grad_ref, attended_ref, gain_ref,
    inverse_ref, starts_ref, second_ref,
    out_ref, d_queries_ref, d_keys_ref, d_values_ref, part_keys_ref, part_values_ref,
):
    head = pl.program_id(0)
    row_ids = lax.broadcasted_iota(jnp.int32, (BLK, BLK), 0)
    col_ids = lax.broadcasted_iota(jnp.int32, (BLK, BLK), 1)
    first = starts_ref[:, 0:PIECE, :].reshape(HD, HD)
    reply = starts_ref[:, PIECE : 2 * PIECE, :].reshape(HD, HD)
    for number, start in enumerate((first, second_ref[0], reply)):
        part = rows(number)
        queries = queries_ref[0, part, :]
        keys = keys_ref[0, part, :]
        values = values_ref[0, part, :]
        grad = grad_ref[part, :]
        col = column(cum_ref, number, head)
        gaps = cum_rows_ref[0, :, part] - col
        mask = jnp.where(col_ids >= row_ids, jnp.exp(gaps), 0.0)
        weights = (mm_nt(keys, queries) * mask).astype(BF16)
        score_grad = (mm_nt(values, grad) * mask).astype(BF16)
        grad_values = mm(weights, grad)
        grad_keys = mm(score_grad, queries)
        grad_queries = mm_tn(score_grad, keys) + jnp.exp(col) * mm_nt(grad, start)
        d_queries_ref[0, part, :] = grad_queries.astype(BF16)
        out_ref[0, part, :] = (
            attended_ref[part, :] * inverse_ref[part, :] * gain_ref[...]
        ).astype(BF16)
        if number < 2:
            part_keys_ref[part, :] = grad_keys
            part_values_ref[part, :] = grad_values
        else:
            d_keys_ref[0] = grad_keys.astype(BF16)
            d_values_ref[0] = grad_values.astype(BF16)


def far_grads_kernel(
    cum_ref, keys_ref, values_ref, ends_ref, term_ref, part_keys_ref, part_values_ref, _k, _v,
    d_keys_ref, d_values_ref,
):
    head = pl.program_id(0)
    cols = [column(cum_ref, number, head) for number in range(2)]
    ends = [col[BLK - 1 : BLK, :] for col in cols]
    second = ends_ref[...].reshape(HD, HD)
    first = (jnp.exp(ends[1]) * second.astype(F32) + term_ref[0]).astype(BF16)
    for number, end_grad in enumerate((first, second)):
        part = rows(number)
        factor = jnp.exp(ends[number] - cols[number])
        key_scaled = rounded_product(keys_ref[0, part, :], factor)
        grad_values = part_values_ref[part, :] + mm(key_scaled, end_grad)
        grad_keys = part_keys_ref[part, :] + factor * mm_nt(values_ref[0, part, :], end_grad)
        d_values_ref[0, part, :] = grad_values.astype(BF16)
        d_keys_ref[0, part, :] = grad_keys.astype(BF16)


def shape(dims, kind):
    return jax.ShapeDtypeStruct(dims, kind)


def whole(dims):
    return pl.BlockSpec(dims, lambda h: (0,) * len(dims))


def lead(dims):
    return pl.BlockSpec(dims, lambda h: (h,) + (0,) * (len(dims) - 1))


def cost(flops, moved):
    return pl.CostEstimate(flops=int(flops), bytes_accessed=int(moved), transcendentals=0)


FULL = pl.BlockSpec((1, ROWS, HD), lambda h: (0, 0, h))
PROMPT = pl.BlockSpec((1, P_DEV, HD), lambda h: (0, 0, h))
REPLY = pl.BlockSpec((1, BLK, HD), lambda h: (0, 2, h))
FLAT = pl.BlockSpec((ROWS, HD), lambda h: (0, h))
FLAT_PROMPT = pl.BlockSpec((P_DEV, HD), lambda h: (0, h))
LANES = pl.BlockSpec((1, HD), lambda h: (0, h))
CUM = whole((ROWS, HD))
CUM_ROWS = lead((1, 1, ROWS))
STATE = lead((1, HD, HD))
PARTS = HD // PIECE
SMEM = pl.BlockSpec(memory_space=pltpu.SMEM)
VMEM = pl.BlockSpec(memory_space=pltpu.VMEM)


def local(queries, keys, values, log_decay, gain, parents, d_out):
    gain_row = gain.reshape(1, COLS)
    mega = 1 << 20

    send, first_term, cum, cum_rows = pl.pallas_call(
        summary_kernel,
        grid=(HL,),
        in_specs=[whole((1, ROWS, HL)), PROMPT, PROMPT],
        out_specs=[lead((PARTS, PIECE + 16, HD)), STATE, CUM, whole((HL, 1, ROWS))],
        out_shape=[
            shape((N_SEQ, PIECE + 16, HD), BF16),
            shape((HL, HD, HD), F32),
            shape((ROWS, HD), F32),
            shape((HL, 1, ROWS), F32),
        ],
        compiler_params=params(),
        cost_estimate=cost(3e8, 4 * mega),
        name="summary",
    )(log_decay, keys, values)
    got = lax.all_to_all(send, "seq", 0, 0, tiled=True)

    within = pl.pallas_call(
        within_kernel,
        grid=(HL,),
        in_specs=[CUM, CUM_ROWS, FULL, FULL, FULL],
        out_specs=FLAT,
        out_shape=shape((ROWS, COLS), F32),
        compiler_params=params(),
        cost_estimate=cost(4e9, 16 * mega),
        name="within",
    )(cum, cum_rows, queries, keys, values)

    send, decays = pl.pallas_call(
        forward_scan_kernel,
        in_specs=[SMEM, VMEM],
        out_specs=[VMEM, VMEM],
        out_shape=[shape((N_SEQ, 2 * PIECE, HD), BF16), shape((N_SEQ, HD), F32)],
        compiler_params=pltpu.CompilerParams(vmem_limit_bytes=32 * mega),
        cost_estimate=cost(1e6, mega),
        name="forward_scan",
    )(parents, got)
    starts = lax.all_to_all(send, "seq", 0, 0, tiled=True)

    attended, second_start, stats = pl.pallas_call(
        attend_kernel,
        grid=(HL,),
        in_specs=[CUM, FULL, FULL, LANES, FLAT, lead((PARTS, 2 * PIECE, HD)), STATE],
        out_specs=[FLAT, STATE, whole((HL, 16, HD))],
        out_shape=[
            shape((ROWS, COLS), F32),
            shape((HL, HD, HD), BF16),
            shape((HL, 16, HD), F32),
        ],
        scratch_shapes=[pltpu.VMEM((ROWS, HD), F32), pltpu.VMEM((ROWS, HD), F32)],
        compiler_params=params(),
        cost_estimate=cost(3e8, 10 * mega),
        name="attend",
    )(cum, queries, d_out, gain_row, within, starts, first_term)
    stats = lax.all_to_all(stats, "head", 0, 0, tiled=True)

    grad, send, last_term, inverse = pl.pallas_call(
        grad_kernel,
        grid=(HL,),
        in_specs=[CUM, FULL, FULL, LANES, FLAT, whole((HL, 16, HD))],
        out_specs=[FLAT, lead((PARTS, 2 * PIECE, HD)), STATE, CUM],
        out_shape=[
            shape((ROWS, COLS), BF16),
            shape((N_SEQ, 2 * PIECE, HD), BF16),
            shape((HL, HD, HD), F32),
            shape((ROWS, HD), F32),
        ],
        scratch_shapes=[pltpu.VMEM((ROWS, HD), F32), pltpu.VMEM((ROWS, HD), F32)],
        compiler_params=params(),
        cost_estimate=cost(3e8, 10 * mega),
        name="grad",
    )(cum, queries, d_out, gain_row, attended, stats)
    got = lax.all_to_all(send, "seq", 0, 0, tiled=True)

    out, d_queries, d_keys, d_values, part_keys, part_values = pl.pallas_call(
        local_grads_kernel,
        grid=(HL,),
        in_specs=[
            CUM, CUM_ROWS, FULL, FULL, FULL, FLAT, FLAT, LANES, CUM,
            lead((PARTS, 2 * PIECE, HD)), STATE,
        ],
        out_specs=[FULL, FULL, REPLY, REPLY, FLAT_PROMPT, FLAT_PROMPT],
        out_shape=[shape((1, ROWS, COLS), BF16)] * 4 + [shape((P_DEV, COLS), F32)] * 2,
        compiler_params=params(),
        cost_estimate=cost(6e9, 24 * mega),
        name="local_grads",
    )(
        cum, cum_rows, queries, keys, values, grad, attended, gain_row, inverse, starts,
        second_start,
    )

    send = pl.pallas_call(
        backward_scan_kernel,
        in_specs=[SMEM, VMEM, VMEM],
        out_specs=VMEM,
        out_shape=shape((N_SEQ, PIECE, HD), BF16),
        compiler_params=pltpu.CompilerParams(vmem_limit_bytes=32 * mega),
        cost_estimate=cost(1e6, mega),
        name="backward_scan",
    )(parents, got, decays)
    ends = lax.all_to_all(send, "seq", 0, 0, tiled=True)

    anywhere = pl.BlockSpec(memory_space=pl.ANY)
    d_keys, d_values = pl.pallas_call(
        far_grads_kernel,
        grid=(HL,),
        in_specs=[
            CUM, PROMPT, PROMPT, lead((PARTS, PIECE, HD)), STATE, FLAT_PROMPT, FLAT_PROMPT,
            anywhere, anywhere,
        ],
        out_specs=[PROMPT, PROMPT],
        out_shape=[shape((1, ROWS, COLS), BF16)] * 2,
        input_output_aliases={7: 0, 8: 1},
        compiler_params=params(),
        cost_estimate=cost(3e8, 10 * mega),
        name="far_grads",
    )(cum, keys, values, ends, last_term, part_keys, part_values, d_keys, d_values)
    return (out, d_queries, d_keys, d_values)


def solution(mesh):
    cut = P("seq", None, "head")
    return jax.shard_map(
        local,
        mesh=mesh,
        in_specs=(cut, cut, cut, cut, P("head"), P(), cut),
        out_specs=(cut, cut, cut, cut),
        check_vma=False,
    )
```

time: 663 us -> 153 us (0.23)
  waiting for transfers between devices: 377 us -> 5.03 us
  other arithmetic: 100 us -> 0 us
  Pallas kernels: 0 us -> 46.8 us
  blocking collectives: 92.5 us -> 58.3 us
  matrix products: 33.2 us -> 0 us
  between operations: 16.3 us -> 0.84 us
  starting transfers between devices: 0.16 us -> 9.74 us
    reduce_scatter x1 -> x0, waiting for transfers between devices: 223 us -> none  [local(): lax.psum_scatter(slot_terms.astype(jnp.bfloat16), 'seq', scatter_dimensio...]
    all_gather x3 -> x0, waiting for transfers between devices: 155 us -> none  [the longest x2 90.4 us: entering(): lax.all_gather(part.astype(kind), axis)]
    all_gather x2 -> x0, blocking collectives: 77.9 us -> none  [entering(): lax.all_gather(part.astype(kind), axis)]
    select_n x64 -> x0, other arithmetic: 70 us -> none  [turn(): return jax.tree.map(lambda a, b: jnp.where(reached, a, b), new, before)]
    all_to_all x0 -> x3, blocking collectives: none -> 58.3 us  [the longest x2 48.4 us: local(): got = lax.all_to_all(send, 'seq', 0, 0, tiled=True)]
    pallas_call x0 -> x8, Pallas kernels: none -> 46.8 us  [the longest x1 13.4 us: local(): pl.pallas_call(local_grads_kernel, grid=(HL,), in_specs=[CUM, CUM_ROWS, F...]
    dot_general x35 -> x0, matrix products: 33.2 us -> none  [the longest x3 4.27 us: block_grads(): jnp.einsum('htu,the->uhe', weights, grad_out, preferred_element_type=jnp....]
    convert_element_type x71 -> x0, other arithmetic: 18.2 us -> none  [the longest x1 5.46 us: local(): slot_terms.astype(jnp.bfloat16)]
  transfers between devices with their start and end apart: 4 -> 2, of which waited for: 4 -> 1; matrix products, arithmetic and copies ran while one was open for 8% -> 0% of each run, Pallas kernels for 0% -> 13%
where the time goes in v1:
time: 153 us; the launch traced here: 151 us
  blocking collectives  58.3 us (38%)
  Pallas kernels  46.8 us (31%)
  local copies, waits for them, and re-layouts  30.2 us (20%)
  starting transfers between devices  9.74 us (6%)
  waiting for transfers between devices  5.03 us (3%)
    all_to_all x2, blocking collectives, local(): got = lax.all_to_all(send, 'seq', 0, 0, tiled=True)  48.4 us
    unnamed x71, local copies, waits for them, and re-layouts  30.2 us
    pallas_call x1, Pallas kernels, local(): pl.pallas_call(local_grads_kernel, grid=(HL,), in_specs=[CUM, CUM_ROWS, F...  13.4 us
    all_to_all x1, blocking collectives, local(): stats = lax.all_to_all(stats, 'head', 0, 0, tiled=True)  9.89 us
    pallas_call x1, Pallas kernels, local(): pl.pallas_call(attend_kernel, grid=(HL,), in_specs=[CUM, FULL, FULL, LANE...  6.97 us
    pallas_call x1, Pallas kernels, local(): pl.pallas_call(within_kernel, grid=(HL,), in_specs=[CUM, CUM_ROWS, FULL,...  6.86 us
    pallas_call x1, Pallas kernels, local(): pl.pallas_call(grad_kernel, grid=(HL,), in_specs=[CUM, FULL, FULL, LANES,...  6.55 us
    pallas_call x1, Pallas kernels, local(): pl.pallas_call(far_grads_kernel, grid=(HL,), in_specs=[CUM, PROMPT, PROMP...  6.34 us
  transfers between devices with their start and end apart: 2, of which 1 were waited for; matrix products, arithmetic and copies ran while one was open for 0% of the time, Pallas kernels for 13%

profile of v1, /device:TPU:32, one launch (start us, length us, event | category | flops | bytes accessed | tf_op | source)
XLA Modules:
  0.0 150.9 jit_solution(4670118428582797474)
XLA Ops:
  0.6 0.9 copy.13.decay_ref
  1.5 0.0 copy-start.2
  1.5 1.4 copy-done.2
  2.9 0.0 copy-start.5
  2.9 1.4 copy-done.5
  4.4 0.0 copy-start.25
  4.4 4.4 %summary.1 = (bf16[32,48,128]{2,1,0:T(8,128)(2,1)S(1)}, f32[8,128,128]{2,1,0:T(8,128)S(1)}, f32[768,128]{1,0:T(8,128)S(1)}, f32[8,1,768]{2,1,0:T(1,128)S(1)}) custom-call(f32[1,768,8]{2,1,0:T(8,128)S(1)} %copy.13.decay_ref, bf16[1,768,1024]{2,1,0:T(8,128)(2,1)S(1)} %copy-done.2, bf16[1,768,1024]{2,1,0:T(8,128)(2,1)S(1)} %copy-done.5), custom_call_target="tpu_custom_call" | custom-call | flops 300000000 | bytes 4194304 | tf_op jit(solution)/shard_map/summary/pallas_call | solution.py:317
  8.7 0.0 copy-start.20
  8.7 0.8 copy-done.20
  9.5 0.0 copy-start.32
  9.5 0.0 copy-start.1
  9.5 26.0 %all_to_all.25.got_ref = bf16[32,48,128]{2,1,0:T(8,128)(2,1)S(1)} all-to-all(bf16[32,48,128]{2,1,0:T(8,128)(2,1)S(1)} %get-tuple-element.27), channel_id=1, replica_groups=mesh['seq'=32,'head'=8] {'seq'}, dimensions={0} | all-to-all | bytes 786432 | tf_op jit(solution)/shard_map/all_to_all | solution.py:332
  35.5 0.0 copy-done.25
  35.5 1.5 %forward_scan.1 = (bf16[32,64,128]{2,1,0:T(8,128)(2,1)}, f32[32,128]{1,0:T(8,128)S(1)}) custom-call(s32[32]{0:T(128)S(1)} %copy-done.25, bf16[32,48,128]{2,1,0:T(8,128)(2,1)S(1)} %all_to_all.25.got_ref), custom_call_target="tpu_custom_call" | custom-call | flops 1000000 | bytes 1048576 | tf_op jit(solution)/shard_map/forward_scan/pallas_call | solution.py:345
  37.0 0.0 copy-start.23
  37.0 4.8 %all-to-all-start.1 = ((bf16[32,64,128]{2,1,0:T(8,128)(2,1)}), bf16[32,64,128]{2,1,0:T(8,128)(2,1)}, u32[]{:S(2)}, u32[]{:S(2)}) async-start(bf16[32,64,128]{2,1,0:T(8,128)(2,1)} %get-tuple-element.28), calls=%async_computation.1 | async-start | bytes 1048576 | tf_op jit(solution)/shard_map/all_to_all | solution.py:354
  41.9 0.0 copy-done.32
  41.9 0.0 copy-done.23
  41.9 0.0 copy-done.1
  41.9 0.0 copy-start.3
  41.9 1.4 copy-done.3
  43.3 1.4 copy-done.6
  44.7 0.7 copy-done.33
  45.5 6.9 %within.1.within_ref = f32[768,1024]{1,0:T(8,128)S(1)} custom-call(f32[768,128]{1,0:T(8,128)S(1)} %get-tuple-element.25.cum_ref, f32[8,1,768]{2,1,0:T(1,128)S(1)} %copy-done.33, bf16[1,768,1024]{2,1,0:T(8,128)(2,1)S(1)} %copy-done.1, bf16[1,768,1024]{2,1,0:T(8,128)(2,1)S(1)} %copy-done.3, bf16[1,768,1024]{2,1,0:T(8,128)(2,1)S(1)} %copy-done.6), custom_call_target="tpu_custom_call" | custom-call | flops 4000000000 | bytes 16777216 | tf_op jit(solution)/shard_map/within/pallas_call | solution.py:334
  52.3 0.0 copy-start.9
  52.4 1.6 %copy-done.9 = f32[768,1024]{1,0:T(8,128)} copy-done((f32[768,1024]{1,0:T(8,128)}, f32[768,1024]{1,0:T(8,128)S(1)}, u32[]{:S(2)}) %copy-start.9) | copy-done | bytes 3145752
  54.0 5.0 %all-to-all-done.1.starts_ref = bf16[32,64,128]{2,1,0:T(8,128)(2,1)} async-done(((bf16[32,64,128]{2,1,0:T(8,128)(2,1)}), bf16[32,64,128]{2,1,0:T(8,128)(2,1)}, u32[]{:S(2)}, u32[]{:S(2)}) %all-to-all-start.1) | async-done | bytes 524320 | tf_op jit(solution)/shard_map/all_to_all | solution.py:354
  59.0 0.0 copy-done
  59.0 0.0 copy-done.22
  59.0 1.9 %copy-done.10 = f32[768,1024]{1,0:T(8,128)S(1)} copy-done((f32[768,1024]{1,0:T(8,128)S(1)}, f32[768,1024]{1,0:T(8,128)}, u32[]{:S(2)}) %copy-start.10) | copy-done | bytes 3145752
  60.9 1.0 copy-done.21
  62.0 7.0 %attend.1 = (f32[768,1024]{1,0:T(8,128)S(1)}, bf16[8,128,128]{2,1,0:T(8,128)(2,1)S(1)}, f32[8,16,128]{2,1,0:T(8,128)S(1)}) custom-call(f32[768,128]{1,0:T(8,128)S(1)} %get-tuple-element.25.cum_ref, bf16[1,768,1024]{2,1,0:T(8,128)(2,1)S(1)} %copy-done.1, bf16[1,768,1024]{2,1,0:T(8,128)(2,1)S(1)} %copy-done, f32[1,1024]{1,0:T(1,128)S(1)} %bitcast.1, ...), custom_call_target="tpu_custom_call" | custom-call | flops 300000000 | bytes 10485760 | tf_op jit(solution)/shard_map/attend/pallas_call | solution.py:356
  68.9 0.0 copy-start.11
  68.9 0.0 copy-start.30
  69.0 9.9 %all_to_all.26.stats_ref = f32[8,16,128]{2,1,0:T(8,128)S(1)} all-to-all(f32[8,16,128]{2,1,0:T(8,128)S(1)} %get-tuple-element.31), channel_id=1, replica_groups=mesh['seq'=32,'head'=8] {'head'}, dimensions={0} | all-to-all | bytes 131072 | tf_op jit(solution)/shard_map/all_to_all | solution.py:371
  78.8 6.5 %grad.1 = (bf16[768,1024]{1,0:T(8,128)(2,1)S(1)}, bf16[32,64,128]{2,1,0:T(8,128)(2,1)S(1)}, f32[8,128,128]{2,1,0:T(8,128)S(1)}, f32[768,128]{1,0:T(8,128)S(1)}) custom-call(f32[768,128]{1,0:T(8,128)S(1)} %get-tuple-element.25.cum_ref, bf16[1,768,1024]{2,1,0:T(8,128)(2,1)S(1)} %copy-done.1, bf16[1,768,1024]{2,1,0:T(8,128)(2,1)S(1)} %copy-done, ...), custom_call_target="tpu_custom_call" | custom-call | flops 300000000 | bytes 10485760 | tf_op jit(solution)/shard_map/grad/pallas_call | solution.py:373
  85.4 0.0 copy-done.11
  85.4 0.0 copy-done.30
  85.4 0.0 copy-start.26
  85.4 1.1 copy-done.26
  86.6 22.4 %all_to_all.27.got_ref = bf16[32,64,128]{2,1,0:T(8,128)(2,1)S(1)} all-to-all(bf16[32,64,128]{2,1,0:T(8,128)(2,1)S(1)} %get-tuple-element.37), channel_id=1, replica_groups=mesh['seq'=32,'head'=8] {'seq'}, dimensions={0} | all-to-all | bytes 1048576 | tf_op jit(solution)/shard_map/all_to_all | solution.py:389
  109.0 0.0 copy-done.18
  109.0 0.0 copy-done.28
  109.0 0.0 copy-done.24
  109.0 0.9 backward_scan.1
  109.9 0.7 copy-done.17
  110.6 4.9 %all-to-all-start.4 = ((bf16[32,32,128]{2,1,0:T(8,128)(2,1)}), bf16[32,32,128]{2,1,0:T(8,128)(2,1)}, u32[]{:S(2)}, u32[]{:S(2)}) async-start(bf16[32,32,128]{2,1,0:T(8,128)(2,1)} %copy-done.17), calls=%async_computation.4 | async-start | bytes 524288 | tf_op jit(solution)/shard_map/all_to_all | solution.py:417
  115.5 0.0 copy-done.4
  115.5 0.0 copy-start.7
  115.5 1.4 copy-done.7
  116.9 1.9 %copy-done.12 = f32[768,1024]{1,0:T(8,128)S(1)} copy-done((f32[768,1024]{1,0:T(8,128)S(1)}, f32[768,1024]{1,0:T(8,128)}, u32[]{:S(2)}) %copy-start.12) | copy-done | bytes 3145752
  118.8 1.4 copy-done.27
  120.2 1.0 copy-done.29
  121.2 0.9 copy-done.31
  122.2 0.7 copy-done.34
  122.9 13.4 %local_grads.1 = (bf16[1,768,1024]{2,1,0:T(8,128)(2,1)}, bf16[1,768,1024]{2,1,0:T(8,128)(2,1)}, bf16[1,768,1024]{2,1,0:T(8,128)(2,1)}, bf16[1,768,1024]{2,1,0:T(...) custom-call(f32[768,128]{1,0:T(8,128)S(1)} %get-tuple-element.25.cum_ref, f32[8,1,768]{2,1,0:T(1,128)S(1)} %copy-done.34, ...), custom_call_target="tpu_custom_call" | custom-call | flops 6000000000 | bytes 25165824 | tf_op jit(solution)/shard_map/local_grads/pallas_call | solution.py:391
  136.3 1.4 copy-done.13
  137.6 1.3 copy-done.15
  138.9 0.0 all-to-all-done.4.ends_ref
  139.0 1.4 copy-done.8
  140.4 1.6 %copy-done.14 = f32[512,1024]{1,0:T(8,128)S(1)} copy-done((f32[512,1024]{1,0:T(8,128)S(1)}, f32[512,1024]{1,0:T(8,128)}, u32[]{:S(2)}) %copy-start.14) | copy-done | bytes 2097176
  142.0 1.6 %copy-done.16 = f32[512,1024]{1,0:T(8,128)S(1)} copy-done((f32[512,1024]{1,0:T(8,128)S(1)}, f32[512,1024]{1,0:T(8,128)}, u32[]{:S(2)}) %copy-start.16) | copy-done | bytes 2097176
  143.5 1.0 copy-done.19
  144.6 6.3 %far_grads.1 = (bf16[1,768,1024]{2,1,0:T(8,128)(2,1)}, bf16[1,768,1024]{2,1,0:T(8,128)(2,1)}) custom-call(f32[768,128]{1,0:T(8,128)S(1)} %get-tuple-element.25.cum_ref, bf16[1,768,1024]{2,1,0:T(8,128)(2,1)S(1)} %copy-done.4, bf16[1,768,1024]{2,1,0:T(8,128)(2,1)S(1)} %copy-done.8, ...), custom_call_target="tpu_custom_call", output_to_operand_aliasing={{0}: (7, {}), {1}: (8, {})} | custom-call | flops 300000000 | bytes 10485760 | tf_op jit(solution)/shard_map/far_grads/pallas_call | solution.py:420
  (22 shorter events, 0.0 us)
Async XLA Ops:
  1.5 1.4 copy-start.2
  2.9 1.4 copy-start.5
  4.4 31.2 %copy-start.25 = (s32[32]{0:T(128)S(1)}, s32[32]{0:T(128)}, u32[]{:S(2)}) copy-start(s32[32]{0:T(128)} %parents_ref.3) | copy-start | bytes 388
  8.7 0.8 copy-start.20
  9.5 32.4 %copy-start.32 = (f32[8,1,768]{2,1,0:T(1,128)}, f32[8,1,768]{2,1,0:T(1,128)S(1)}, u32[]{:S(2)}) copy-start(f32[8,1,768]{2,1,0:T(1,128)S(1)} %get-tuple-element.26.cum_rows_ref) | copy-start | bytes 73732
  9.5 32.4 %copy-start.1 = (bf16[1,768,1024]{2,1,0:T(8,128)(2,1)S(1)}, bf16[1,768,1024]{2,1,0:T(8,128)(2,1)}, u32[]{:S(2)}) copy-start(bf16[1,768,1024]{2,1,0:T(8,128)(2,1)} %queries_ref.7) | copy-start | bytes 4718596
  37.0 4.9 %copy-start.23 = (f32[32,128]{1,0:T(8,128)}, f32[32,128]{1,0:T(8,128)S(1)}, u32[]{:S(2)}) copy-start(f32[32,128]{1,0:T(8,128)S(1)} %get-tuple-element.38.decay_ref) | copy-start | bytes 49156
  37.0 22.0 %all-to-all-start.1 = ((bf16[32,64,128]{2,1,0:T(8,128)(2,1)}), bf16[32,64,128]{2,1,0:T(8,128)(2,1)}, u32[]{:S(2)}, u32[]{:S(2)}) async-start(bf16[32,64,128]{2,1,0:T(8,128)(2,1)} %get-tuple-element.28), calls=%async_computation.1 | async-start | bytes 1048576 | tf_op jit(solution)/shard_map/all_to_all | solution.py:354
  41.9 1.4 copy-start.3
  43.3 1.4 copy-start.6
  44.7 0.7 copy-start.33
  45.5 13.5 %copy-start = (bf16[1,768,1024]{2,1,0:T(8,128)(2,1)S(1)}, bf16[1,768,1024]{2,1,0:T(8,128)(2,1)}, u32[]{:S(2)}) copy-start(bf16[1,768,1024]{2,1,0:T(8,128)(2,1)} %d_out_ref.3) | copy-start | bytes 4718596
  45.5 13.5 %copy-start.22 = (f32[1024]{0:T(1024)S(1)}, f32[1024]{0:T(1024)}, u32[]{:S(2)}) copy-start(f32[1024]{0:T(1024)} %param.11) | copy-start | bytes 12292
  52.3 1.6 %copy-start.9 = (f32[768,1024]{1,0:T(8,128)}, f32[768,1024]{1,0:T(8,128)S(1)}, u32[]{:S(2)}) copy-start(f32[768,1024]{1,0:T(8,128)S(1)} %within.1.within_ref) | copy-start | bytes 9437188
  59.0 1.9 %copy-start.10 = (f32[768,1024]{1,0:T(8,128)S(1)}, f32[768,1024]{1,0:T(8,128)}, u32[]{:S(2)}) copy-start(f32[768,1024]{1,0:T(8,128)} %copy-done.9) | copy-start | bytes 9437188
  60.9 1.0 copy-start.21
  68.9 16.5 %copy-start.11 = (f32[768,1024]{1,0:T(8,128)}, f32[768,1024]{1,0:T(8,128)S(1)}, u32[]{:S(2)}) copy-start(f32[768,1024]{1,0:T(8,128)S(1)} %get-tuple-element.30.attended_ref) | copy-start | bytes 9437188
  68.9 16.5 %copy-start.30 = (bf16[8,128,128]{2,1,0:T(8,128)(2,1)}, bf16[8,128,128]{2,1,0:T(8,128)(2,1)S(1)}, u32[]{:S(2)}) copy-start(bf16[8,128,128]{2,1,0:T(8,128)(2,1)S(1)} %get-tuple-element.34.second_ref) | copy-start | bytes 786436
  78.8 30.2 %copy-start.24 = (f32[32,128]{1,0:T(8,128)S(1)}, f32[32,128]{1,0:T(8,128)}, u32[]{:S(2)}) copy-start(f32[32,128]{1,0:T(8,128)} %copy-done.23) | copy-start | bytes 49156
  85.4 1.1 copy-start.26
  86.6 22.4 %copy-start.18 = (f32[8,128,128]{2,1,0:T(8,128)}, f32[8,128,128]{2,1,0:T(8,128)S(1)}, u32[]{:S(2)}) copy-start(f32[8,128,128]{2,1,0:T(8,128)S(1)} %get-tuple-element.39.term_ref) | copy-start | bytes 1572868
  86.6 22.4 %copy-start.28 = (f32[768,128]{1,0:T(8,128)}, f32[768,128]{1,0:T(8,128)S(1)}, u32[]{:S(2)}) copy-start(f32[768,128]{1,0:T(8,128)S(1)} %get-tuple-element.33.inverse_ref) | copy-start | bytes 1179652
  86.6 28.9 %copy-start.4 = (bf16[1,768,1024]{2,1,0:T(8,128)(2,1)S(1)}, bf16[1,768,1024]{2,1,0:T(8,128)(2,1)}, u32[]{:S(2)}) copy-start(bf16[1,768,1024]{2,1,0:T(8,128)(2,1)} %keys_ref.7) | copy-start | bytes 4718596
  109.9 0.7 copy-start.17
  110.6 28.3 %all-to-all-start.4 = ((bf16[32,32,128]{2,1,0:T(8,128)(2,1)}), bf16[32,32,128]{2,1,0:T(8,128)(2,1)}, u32[]{:S(2)}, u32[]{:S(2)}) async-start(bf16[32,32,128]{2,1,0:T(8,128)(2,1)} %copy-done.17), calls=%async_computation.4 | async-start | bytes 524288 | tf_op jit(solution)/shard_map/all_to_all | solution.py:417
  115.5 1.4 copy-start.7
  116.9 1.9 %copy-start.12 = (f32[768,1024]{1,0:T(8,128)S(1)}, f32[768,1024]{1,0:T(8,128)}, u32[]{:S(2)}) copy-start(f32[768,1024]{1,0:T(8,128)} %copy-done.11) | copy-start | bytes 9437188
  118.8 1.4 copy-start.27
  120.2 1.0 copy-start.29
  121.2 0.9 copy-start.31
  122.2 0.7 copy-start.34
  136.3 1.4 copy-start.13
  137.6 1.3 copy-start.15
  139.0 1.4 copy-start.8
  140.4 1.6 %copy-start.14 = (f32[512,1024]{1,0:T(8,128)S(1)}, f32[512,1024]{1,0:T(8,128)}, u32[]{:S(2)}) copy-start(f32[512,1024]{1,0:T(8,128)} %copy-done.13) | copy-start | bytes 6291460
  142.0 1.6 %copy-start.16 = (f32[512,1024]{1,0:T(8,128)S(1)}, f32[512,1024]{1,0:T(8,128)}, u32[]{:S(2)}) copy-start(f32[512,1024]{1,0:T(8,128)} %copy-done.15) | copy-start | bytes 6291460
  143.5 1.0 copy-start.19

commit v2 on v1

v2 whole, which is shorter than its diff:
```python
import jax
import jax.numpy as jnp
from jax import lax
from jax.experimental import pallas as pl
from jax.experimental.pallas import tpu as pltpu
from jax.sharding import PartitionSpec as P

H = 64
HD = 128
BLK = 256
PROMPTS = 2
P_DEV = 512
ROWS = 768
HL = 8
N_SEQ = 32
SPAN = N_SEQ // PROMPTS
COLS = HL * HD
PIECE = HL * HD // N_SEQ
PARTS = HD // PIECE
BLOCKS = ROWS // BLK
TILES = ROWS // HD
EPS = 1e-05

F32 = jnp.float32
BF16 = jnp.bfloat16


def dot(a, b, dims):
    return lax.dot_general(a, b, (dims, ((), ())), preferred_element_type=F32)


def mm(a, b):
    return dot(a, b, ((1,), (0,)))


def mm_nt(a, b):
    return dot(a, b, ((1,), (1,)))


def mm_tn(a, b):
    return dot(a, b, ((0,), (0,)))


def rows(number):
    return slice(number * BLK, (number + 1) * BLK)


def tile_rows(tile):
    return slice(tile * HD, (tile + 1) * HD)


def column(cum_ref, number, head):
    block = pltpu.roll(cum_ref[rows(number), :], lax.rem(HD - head, HD), 1)
    return block[:, 0:1]


def rounded_product(block, factor):
    return (block.astype(F32) * factor).astype(BF16)


def lanes(head):
    return pl.ds(pl.multiple_of(head * HD, HD), HD)


def of_rows(ref, count=ROWS, first=0):
    if len(ref.shape) == 3:
        return lambda head: ref.at[0, pl.ds(first, count), lanes(head)]
    return lambda head: ref.at[pl.ds(first, count), lanes(head)]


def of_lead(ref, count=1):
    if count == 1:
        return lambda head: ref.at[head]
    return lambda head: ref.at[pl.ds(head * count, count)]


class Copies:
    def __init__(self, pairs, sems):
        self.pairs, self.sems = pairs, sems

    def each(self, head):
        return [
            pltpu.make_async_copy(src(head), dst(head), self.sems.at[number, head])
            for number, (src, dst) in enumerate(self.pairs)
        ]

    def start(self, head):
        for copy in self.each(head):
            copy.start()

    def wait(self, head):
        for copy in self.each(head):
            copy.wait()


def over_heads(fetch, body, leave=None):
    if fetch is not None:
        for head in range(HL):
            fetch.start(head)

    def step(head, carry):
        if fetch is not None:
            fetch.wait(head)
        body(head)
        if leave is not None:
            leave.start(head)
        return carry

    lax.fori_loop(0, HL, step, 0)
    if leave is not None:
        for head in range(HL):
            leave.wait(head)


def split(value):
    coarse = value.astype(BF16)
    rest = value - coarse.astype(F32)
    middle = rest.astype(BF16)
    return coarse, middle, (rest - middle.astype(F32)).astype(BF16)


def summary_kernel(
    decay_ref, keys_ref, values_ref,
    send_ref, term_ref, cum_rows_ref, ends_ref,
    keys_buf, values_buf, in_sems,
):
    fetch = Copies(
        [
            (of_rows(keys_ref, P_DEV), of_lead(keys_buf)),
            (of_rows(values_ref, P_DEV), of_lead(values_buf)),
        ],
        in_sems,
    )
    for head in range(HL):
        fetch.start(head)
    before = lax.broadcasted_iota(jnp.int32, (BLK, BLK), 0)
    after = lax.broadcasted_iota(jnp.int32, (BLK, BLK), 1)
    upper = jnp.where(before <= after, 1.0, 0.0).astype(BF16)
    stacked = jnp.concatenate(
        [decay_ref[0, :, rows(number)] for number in range(BLOCKS)], axis=0
    )
    coarse, middle, fine = (mm(part, upper) for part in split(stacked))
    cumulative = (fine + middle) + coarse
    for number in range(BLOCKS):
        total = cumulative[number * HL : (number + 1) * HL]
        cum_rows_ref[:, rows(number)] = total
        ends_ref[:, number, :] = jnp.broadcast_to(jnp.exp(total[:, BLK - 1 : BLK]), (HL, HD))
    row_ids = lax.broadcasted_iota(jnp.int32, (16, HD), 0)

    def body(head):
        terms = []
        for number in range(2):
            row = cum_rows_ref[pl.ds(head, 1), rows(number)]
            factor = jnp.exp(row[:, BLK - 1 : BLK] - row)
            turned = keys_buf[head, rows(number), :].T
            key_scaled = rounded_product(turned, factor)
            terms.append(mm(key_scaled, values_buf[head, rows(number), :]))
        term_ref[head] = terms[0]
        end_decays = ends_ref[head]
        summary = end_decays[1:2, :] * terms[0] + terms[1]
        decay = jnp.broadcast_to(end_decays[0:1, :] * end_decays[1:2, :], (16, HD))
        coarse, middle, _ = split(decay)
        packed = jnp.where(
            row_ids == 0, coarse.astype(F32), jnp.where(row_ids == 1, middle.astype(F32), 0.0)
        ).astype(BF16)
        for piece in range(PARTS):
            at = head * PARTS + piece
            send_ref[at, 0:PIECE, :] = summary[piece * PIECE : (piece + 1) * PIECE].astype(BF16)
            send_ref[at, PIECE : PIECE + 16, :] = packed

    def step(head, carry):
        fetch.wait(head)
        body(head)
        return carry

    lax.fori_loop(0, HL, step, 0)


def within_kernel(
    cum_rows_ref, queries_ref, keys_ref, values_ref, d_out_ref,
    cum_ref, within_ref, scaled_queries_ref, scaled_keys_ref, d_out_buf,
    queries_buf, keys_buf, values_buf, in_sems,
):
    fetch = Copies(
        [
            (of_rows(queries_ref), of_lead(queries_buf)),
            (of_rows(keys_ref), of_lead(keys_buf)),
            (of_rows(values_ref), of_lead(values_buf)),
            (of_rows(d_out_ref), of_lead(d_out_buf)),
        ],
        in_sems,
    )
    for head in range(HL):
        fetch.start(head)
    for tile in range(TILES):
        part = tile_rows(tile)
        padded = jnp.concatenate(
            [cum_rows_ref[:, part], jnp.zeros((HD - HL, HD), F32)], axis=0
        )
        cum_ref[part, :] = padded.T
    row_ids = lax.broadcasted_iota(jnp.int32, (BLK, BLK), 0)
    col_ids = lax.broadcasted_iota(jnp.int32, (BLK, BLK), 1)

    def body(head):
        for number in range(BLOCKS):
            part = rows(number)
            queries = queries_buf[head, part, :]
            keys = keys_buf[head, part, :]
            col = column(cum_ref, number, head)
            gaps = col - cum_rows_ref[pl.ds(head, 1), part]
            mask = jnp.where(row_ids >= col_ids, jnp.exp(gaps), 0.0)
            weights = (mm_nt(queries, keys) * mask).astype(BF16)
            within_ref[head, part, :] = mm(weights, values_buf[head, part, :])
            scaled_queries_ref[head, part, :] = rounded_product(queries, jnp.exp(col))
            if number < 2:
                factor = jnp.exp(col[BLK - 1 : BLK, :] - col)
                scaled_keys_ref[head, part, :] = rounded_product(keys, factor)

    def step(head, carry):
        fetch.wait(head)
        body(head)
        return carry

    lax.fori_loop(0, HL, step, 0)


def forward_scan_kernel(parents_ref, got_ref, send_ref, decay_ref):
    totals = []
    for prompt in range(PROMPTS):
        carry = jnp.zeros((PIECE, HD), F32)
        for index in range(prompt * SPAN, (prompt + 1) * SPAN):
            packed = got_ref[index, PIECE : PIECE + 16, :].astype(F32)
            decay = packed[0:1, :] + packed[1:2, :]
            decay_ref[index : index + 1, :] = decay
            send_ref[index, 0:PIECE, :] = carry.astype(BF16)
            carry = decay * carry + got_ref[index, 0:PIECE, :].astype(F32)
        totals.append(carry)
    for index in range(N_SEQ):
        prompt = parents_ref[index] // SPAN
        chosen = jnp.where(prompt == 0, totals[0], totals[1])
        send_ref[index, PIECE : 2 * PIECE, :] = chosen.astype(BF16)


def attend_kernel(
    ends_ref, gain_ref, queries_ref, d_out_ref, within_ref, starts_ref, term_ref,
    attended_ref, second_ref, stats_ref, squares_ref, products_ref,
):
    squares_ref[...] = jnp.zeros_like(squares_ref)
    products_ref[...] = jnp.zeros_like(products_ref)

    def body(head):
        got = starts_ref[pl.ds(head * PARTS, PARTS)]
        first = got[:, 0:PIECE, :].reshape(HD, HD)
        reply = got[:, PIECE : 2 * PIECE, :].reshape(HD, HD)
        end_decay = ends_ref[head][0:1, :]
        second = (end_decay * first.astype(F32) + term_ref[head]).astype(BF16)
        second_ref[head] = second
        gain = gain_ref[pl.ds(head, 1), :]
        for number, start in enumerate((first, second, reply)):
            part = rows(number)
            attended = within_ref[head, part, :] + mm(queries_ref[head, part, :], start)
            attended_ref[head, part, :] = attended
            weighted = gain * d_out_ref[head, part, :].astype(F32)
            squares_ref[part, :] += attended * attended
            products_ref[part, :] += weighted * attended

    over_heads(None, body)
    stats_ref[...] = jnp.zeros_like(stats_ref)
    for tile in range(TILES):
        for base, sums_ref in ((0, squares_ref), (8, products_ref)):
            row = jnp.sum(sums_ref[tile_rows(tile), :].T, axis=0, keepdims=True)
            stats_ref[:, base + tile : base + tile + 1, :] = jnp.broadcast_to(
                row[None], (HL, 1, HD)
            )


def grad_kernel(
    ends_ref, gain_ref, stats_ref, queries_ref, d_out_ref, attended_ref,
    grad_ref, send_ref, term_ref, inverse_ref, slope_ref,
):
    total = stats_ref[0]
    for source in range(1, HL):
        total = total + stats_ref[source]
    turned = jnp.concatenate([total, jnp.zeros((HD - 16, HD), F32)], axis=0).T
    for tile in range(TILES):
        squares = turned[:, tile : tile + 1]
        products = turned[:, 8 + tile : 9 + tile]
        inverse = lax.rsqrt(squares / (H * HD) + EPS)
        slope = inverse * inverse * inverse * products / (H * HD)
        inverse_ref[tile_rows(tile), :] = jnp.broadcast_to(inverse, (HD, HD))
        slope_ref[tile_rows(tile), :] = jnp.broadcast_to(slope, (HD, HD))

    def body(head):
        gain = gain_ref[pl.ds(head, 1), :]
        terms = []
        for number in range(BLOCKS):
            part = rows(number)
            weighted = gain * d_out_ref[head, part, :].astype(F32)
            grad = (
                inverse_ref[part, :] * weighted
                - attended_ref[head, part, :] * slope_ref[part, :]
            ).astype(BF16)
            grad_ref[head, part, :] = grad
            terms.append(mm_tn(queries_ref[head, part, :], grad))
        local_sum = ends_ref[head][0:1, :] * terms[1] + terms[0]
        term_ref[head] = terms[1]
        for piece in range(PARTS):
            at = head * PARTS + piece
            part = slice(piece * PIECE, (piece + 1) * PIECE)
            send_ref[at, 0:PIECE, :] = local_sum[part].astype(BF16)
            send_ref[at, PIECE : 2 * PIECE, :] = terms[2][part].astype(BF16)

    over_heads(None, body)


def backward_scan_kernel(parents_ref, got_ref, decay_ref, send_ref):
    branches = [jnp.zeros((PIECE, HD), F32) for _ in range(PROMPTS)]
    for index in range(N_SEQ):
        prompt = parents_ref[index] // SPAN
        start_grad = got_ref[index, PIECE : 2 * PIECE, :].astype(F32)
        for each in range(PROMPTS):
            branches[each] = branches[each] + jnp.where(prompt == each, start_grad, 0.0)
    for prompt in range(PROMPTS):
        carry = branches[prompt]
        for index in reversed(range(prompt * SPAN, (prompt + 1) * SPAN)):
            send_ref[index] = carry.astype(BF16)
            carry = decay_ref[index : index + 1, :] * carry + got_ref[index, 0:PIECE, :].astype(F32)


def local_grads_kernel(
    cum_ref, cum_rows_ref, inverse_ref, gain_ref,
    queries_ref, keys_ref, values_ref, grad_ref, attended_ref, starts_ref, second_ref,
    out_ref, d_queries_ref, part_keys_ref, part_values_ref, d_keys_ref, d_values_ref, values_buf,
    queries_buf, keys_buf, out_buf, d_queries_buf, d_keys_buf, d_values_buf, in_sems, out_sems,
):
    fetch = Copies(
        [
            (of_rows(queries_ref), of_lead(queries_buf)),
            (of_rows(keys_ref), of_lead(keys_buf)),
            (of_rows(values_ref), of_lead(values_buf)),
        ],
        in_sems,
    )
    leave = Copies(
        [
            (of_lead(out_buf), of_rows(out_ref)),
            (of_lead(d_queries_buf), of_rows(d_queries_ref)),
            (of_lead(d_keys_buf), of_rows(d_keys_ref, BLK, P_DEV)),
            (of_lead(d_values_buf), of_rows(d_values_ref, BLK, P_DEV)),
        ],
        out_sems,
    )
    row_ids = lax.broadcasted_iota(jnp.int32, (BLK, BLK), 0)
    col_ids = lax.broadcasted_iota(jnp.int32, (BLK, BLK), 1)

    def body(head):
        got = starts_ref[pl.ds(head * PARTS, PARTS)]
        first = got[:, 0:PIECE, :].reshape(HD, HD)
        reply = got[:, PIECE : 2 * PIECE, :].reshape(HD, HD)
        gain = gain_ref[pl.ds(head, 1), :]
        for number, start in enumerate((first, second_ref[head], reply)):
            part = rows(number)
            queries = queries_buf[head, part, :]
            keys = keys_buf[head, part, :]
            values = values_buf[head, part, :]
            grad = grad_ref[head, part, :]
            col = column(cum_ref, number, head)
            gaps = cum_rows_ref[pl.ds(head, 1), part] - col
            mask = jnp.where(col_ids >= row_ids, jnp.exp(gaps), 0.0)
            weights = (mm_nt(keys, queries) * mask).astype(BF16)
            score_grad = (mm_nt(values, grad) * mask).astype(BF16)
            grad_values = mm(weights, grad)
            grad_keys = mm(score_grad, queries)
            grad_queries = mm_tn(score_grad, keys) + jnp.exp(col) * mm_nt(grad, start)
            d_queries_buf[head, part, :] = grad_queries.astype(BF16)
            out_buf[head, part, :] = (
                attended_ref[head, part, :] * inverse_ref[part, :] * gain
            ).astype(BF16)
            if number < 2:
                part_keys_ref[head, part, :] = grad_keys
                part_values_ref[head, part, :] = grad_values
            else:
                d_keys_buf[head] = grad_keys.astype(BF16)
                d_values_buf[head] = grad_values.astype(BF16)

    over_heads(fetch, body, leave)


def far_grads_kernel(
    cum_ref, ends_ref, far_ref, term_ref, scaled_keys_ref, values_ref,
    part_keys_ref, part_values_ref, _k, _v,
    d_keys_ref, d_values_ref, d_keys_buf, d_values_buf, out_sems,
):
    leave = Copies(
        [
            (of_lead(d_keys_buf), of_rows(d_keys_ref, P_DEV)),
            (of_lead(d_values_buf), of_rows(d_values_ref, P_DEV)),
        ],
        out_sems,
    )

    def body(head):
        second = far_ref[pl.ds(head * PARTS, PARTS)].reshape(HD, HD)
        first = (ends_ref[head][1:2, :] * second.astype(F32) + term_ref[head]).astype(BF16)
        for number, end_grad in enumerate((first, second)):
            part = rows(number)
            col = column(cum_ref, number, head)
            factor = jnp.exp(col[BLK - 1 : BLK, :] - col)
            grad_values = part_values_ref[head, part, :] + mm(scaled_keys_ref[head, part, :], end_grad)
            grad_keys = part_keys_ref[head, part, :] + factor * mm_nt(
                values_ref[head, part, :], end_grad
            )
            d_values_buf[head, part, :] = grad_values.astype(BF16)
            d_keys_buf[head, part, :] = grad_keys.astype(BF16)

    over_heads(None, body, leave)


def shape(dims, kind):
    return jax.ShapeDtypeStruct(dims, kind)


HBM = pl.BlockSpec(memory_space=pltpu.HBM)
SMEM = pl.BlockSpec(memory_space=pltpu.SMEM)
VMEM = pl.BlockSpec(memory_space=pltpu.VMEM)
WIDE = shape((1, ROWS, COLS), BF16)
HEAD_ROWS = (HL, ROWS, HD)
HEAD_PROMPT = (HL, P_DEV, HD)
HEAD_REPLY = (HL, BLK, HD)
STATE = (HL, HD, HD)
PIECES = (N_SEQ, PIECE, HD)
TWO_PIECES = (N_SEQ, 2 * PIECE, HD)
SENT_PIECES = (N_SEQ, PIECE + 16, HD)
CUM = (ROWS, HD)


def call(kernel, name, in_specs, outs, scratch, semaphores, mib, flops, moved, aliases=None):
    return pl.pallas_call(
        kernel,
        in_specs=in_specs,
        out_specs=[spec for spec, _ in outs],
        out_shape=[made for _, made in outs],
        scratch_shapes=[pltpu.VMEM(dims, kind) for dims, kind in scratch]
        + [pltpu.SemaphoreType.DMA((count, HL)) for count in semaphores],
        input_output_aliases=aliases or {},
        compiler_params=pltpu.CompilerParams(vmem_limit_bytes=mib << 20),
        cost_estimate=pl.CostEstimate(
            flops=int(flops), bytes_accessed=int(moved) << 20, transcendentals=0
        ),
        name=name,
    )


def summarize(decay_rows, keys, values):
    return call(
        summary_kernel, "summary", [VMEM, HBM, HBM],
        [
            (VMEM, shape(SENT_PIECES, BF16)), (VMEM, shape(STATE, F32)),
            (VMEM, shape((HL, ROWS), F32)), (VMEM, shape((HL, 8, HD), F32)),
        ],
        [(HEAD_PROMPT, BF16), (HEAD_PROMPT, BF16)], [2], 52, 3e8, 4,
    )(decay_rows, keys, values)


def inside(cum_rows, queries, keys, values, d_out):
    return call(
        within_kernel, "within", [VMEM] + [HBM] * 4,
        [
            (VMEM, shape(CUM, F32)), (VMEM, shape(HEAD_ROWS, F32)), (VMEM, shape(HEAD_ROWS, BF16)),
            (VMEM, shape(HEAD_PROMPT, BF16)), (VMEM, shape(HEAD_ROWS, BF16)),
        ],
        [(HEAD_ROWS, BF16)] * 3, [4], 20, 4e9, 16,
    )(cum_rows, queries, keys, values, d_out)


def forward_scan(parents, got):
    return call(
        forward_scan_kernel, "forward_scan", [SMEM, VMEM],
        [(VMEM, shape(TWO_PIECES, BF16)), (VMEM, shape((N_SEQ, HD), F32))],
        [], [], 12, 1e6, 1,
    )(parents, got)


def attend(ends, gains, scaled_queries, d_out, within, starts, term):
    return call(
        attend_kernel, "attend", [VMEM] * 7,
        [
            (VMEM, shape(HEAD_ROWS, F32)), (VMEM, shape(STATE, BF16)),
            (VMEM, shape((HL, 16, HD), F32)),
        ],
        [(CUM, F32), (CUM, F32)], [], 20, 3e8, 10,
    )(ends, gains, scaled_queries, d_out, within, starts, term)


def grads(ends, gains, stats, scaled_queries, d_out, attended):
    return call(
        grad_kernel, "grad", [VMEM] * 6,
        [
            (VMEM, shape(HEAD_ROWS, BF16)), (VMEM, shape(TWO_PIECES, BF16)),
            (VMEM, shape(STATE, F32)), (VMEM, shape(CUM, F32)),
        ],
        [(CUM, F32)], [], 20, 3e8, 10,
    )(ends, gains, stats, scaled_queries, d_out, attended)


def local_grads(
    cum, cum_rows, inverse, gains, queries, keys, values, grad, attended, starts, second
):
    return call(
        local_grads_kernel, "local_grads", [VMEM] * 4 + [HBM] * 3 + [VMEM] * 4,
        [
            (HBM, WIDE), (HBM, WIDE), (VMEM, shape(HEAD_PROMPT, F32)),
            (VMEM, shape(HEAD_PROMPT, F32)), (HBM, WIDE), (HBM, WIDE),
            (VMEM, shape(HEAD_ROWS, BF16)),
        ],
        [(HEAD_ROWS, BF16)] * 4 + [(HEAD_REPLY, BF16)] * 2, [3, 4], 28, 6e9, 24,
    )(cum, cum_rows, inverse, gains, queries, keys, values, grad, attended, starts, second)


def far_grads(cum, ends, far, term, scaled_keys, values, part_keys, part_values, d_keys, d_values):
    return call(
        far_grads_kernel, "far_grads", [VMEM] * 8 + [HBM] * 2,
        [(HBM, WIDE), (HBM, WIDE)],
        [(HEAD_PROMPT, BF16), (HEAD_PROMPT, BF16)], [2], 20, 3e8, 10, {8: 0, 9: 1},
    )(cum, ends, far, term, scaled_keys, values, part_keys, part_values, d_keys, d_values)


def backward_scan(parents, got, decays):
    return call(
        backward_scan_kernel, "backward_scan", [SMEM, VMEM, VMEM],
        [(VMEM, shape(PIECES, BF16))], [], [], 12, 1e6, 1,
    )(parents, got, decays)[0]


def everyone(array, axis):
    return lax.all_to_all(array, axis, 0, 0, tiled=True)


def local(queries, keys, values, log_decay, gain, parents, d_out):
    gains = gain.reshape(HL, HD)
    decay_rows = jnp.swapaxes(log_decay, 1, 2)
    send, first_term, cum_rows, block_ends = summarize(decay_rows, keys, values)
    got = everyone(send, "seq")
    cum, within, scaled_queries, scaled_keys, d_out_heads = inside(
        cum_rows, queries, keys, values, d_out
    )
    send, decays = forward_scan(parents, got)
    starts = everyone(send, "seq")
    attended, second, stats = attend(
        block_ends, gains, scaled_queries, d_out_heads, within, starts, first_term
    )
    stats = everyone(stats, "head")
    grad, send, last_term, inverse = grads(
        block_ends, gains, stats, scaled_queries, d_out_heads, attended
    )
    got = everyone(send, "seq")
    out, d_queries, part_keys, part_values, d_keys, d_values, value_heads = local_grads(
        cum, cum_rows, inverse, gains, queries, keys, values, grad, attended, starts, second
    )
    far = everyone(backward_scan(parents, got, decays), "seq")
    d_keys, d_values = far_grads(
        cum, block_ends, far, last_term, scaled_keys, value_heads, part_keys, part_values,
        d_keys, d_values,
    )
    return (out, d_queries, d_keys, d_values)


def solution(mesh):
    cut = P("seq", None, "head")
    return jax.shard_map(
        local,
        mesh=mesh,
        in_specs=(cut, cut, cut, cut, P("head"), P(), cut),
        out_specs=(cut, cut, cut, cut),
        check_vma=False,
    )
```

time: 153 us -> 144 us (0.941)
  Pallas kernels: 46.8 us -> 36.4 us
  waiting for transfers between devices: 5.03 us -> 0.51 us
  blocking collectives: 58.3 us -> 62.4 us
  local copies, waits for them, and re-layouts: 30.2 us -> 32.6 us
    pallas_call x8, Pallas kernels: 46.8 us -> 36.4 us  [the longest x1 12.9 us: local_grads(): call(local_grads_kernel, 'local_grads', [VMEM] * 4 + [HBM] * 3 + [VMEM] *...]
    all_to_all x2, waiting for transfers between devices: 5.03 us -> 0.51 us  [everyone(): return lax.all_to_all(array, axis, 0, 0, tiled=True)]
    all_to_all x3, blocking collectives: 58.3 us -> 62.4 us  [everyone(): return lax.all_to_all(array, axis, 0, 0, tiled=True)]
    unnamed x71 -> x66, local copies, waits for them, and re-layouts: 30.2 us -> 32.6 us
  transfers between devices with their start and end apart: 2 -> 2, of which waited for: 1 -> 1; matrix products, arithmetic and copies ran while one was open for 0% -> 0% of each run, Pallas kernels for 13% -> 14%
where the time goes in v2:
time: 144 us; the launch traced here: 142 us
  blocking collectives  62.4 us (43%)
  Pallas kernels  36.4 us (25%)
  local copies, waits for them, and re-layouts  32.6 us (23%)
  starting transfers between devices  9.69 us (7%)
    all_to_all x3, blocking collectives, everyone(): return lax.all_to_all(array, axis, 0, 0, tiled=True)  62.4 us
    unnamed x66, local copies, waits for them, and re-layouts  32.6 us
    pallas_call x1, Pallas kernels, local_grads(): call(local_grads_kernel, 'local_grads', [VMEM] * 4 + [HBM] * 3 + [VMEM] *...  12.9 us
    all_to_all x2, starting transfers between devices, everyone(): return lax.all_to_all(array, axis, 0, 0, tiled=True)  9.69 us
    pallas_call x1, Pallas kernels, inside(): call(within_kernel, 'within', [VMEM] + [HBM] * 4, [(VMEM, shape(CUM, F32)...  7.61 us
    pallas_call x1, Pallas kernels, far_grads(): call(far_grads_kernel, 'far_grads', [VMEM] * 8 + [HBM] * 2, [(HBM, WIDE),...  3.68 us
    pallas_call x1, Pallas kernels, attend(): call(attend_kernel, 'attend', [VMEM] * 7, [(VMEM, shape(HEAD_ROWS, F32)),...  3.19 us
    pallas_call x1, Pallas kernels, summarize(): call(summary_kernel, 'summary', [VMEM, HBM, HBM], [(VMEM, shape(SENT_PIEC...  3.17 us
  transfers between devices with their start and end apart: 2, of which 1 were waited for; matrix products, arithmetic and copies ran while one was open for 0% of the time, Pallas kernels for 14%

profile of v2, /device:TPU:32, one launch (start us, length us, event | category | flops | bytes accessed | tf_op | source)
XLA Modules:
  0.0 142.4 jit_solution(613891549486951742)
XLA Ops:
  0.6 0.0 copy-start.21
  0.6 0.7 copy-done.21
  1.4 0.0 copy-start.23
  1.4 3.2 %summary.1 = (bf16[32,48,128]{2,1,0:T(8,128)(2,1)S(1)}, f32[8,128,128]{2,1,0:T(8,128)S(1)}, f32[8,768]{1,0:T(8,128)S(1)}, f32[8,8,128]{2,1,0:T(8,128)S(1)}) custom-call(f32[1,8,768]{2,1,0:T(8,128)S(1)} %bitcast.2, bf16[1,768,1024]{2,1,0:T(8,128)(2,1)} %keys_ref.5, bf16[1,768,1024]{2,1,0:T(8,128)(2,1)} %values_ref.5), custom_call_target="tpu_custom_call" | custom-call | flops 300000000 | bytes 4194304 | tf_op jit(solution)/shard_map/summary/pallas_call | solution.py:455
  4.5 0.0 copy-start.16
  4.6 25.9 %all_to_all.25.got_ref = bf16[32,48,128]{2,1,0:T(8,128)(2,1)S(1)} all-to-all(bf16[32,48,128]{2,1,0:T(8,128)(2,1)S(1)} %get-tuple-element.37), channel_id=1, replica_groups=mesh['seq'=32,'head'=8] {'seq'}, dimensions={0} | all-to-all | bytes 786432 | tf_op jit(solution)/shard_map/all_to_all | solution.py:536
  30.4 0.0 copy-done.23
  30.4 1.5 %forward_scan.1 = (bf16[32,64,128]{2,1,0:T(8,128)(2,1)}, f32[32,128]{1,0:T(8,128)S(1)}) custom-call(s32[32]{0:T(128)S(1)} %copy-done.23, bf16[32,48,128]{2,1,0:T(8,128)(2,1)S(1)} %all_to_all.25.got_ref), custom_call_target="tpu_custom_call" | custom-call | flops 1000000 | bytes 1048576 | tf_op jit(solution)/shard_map/forward_scan/pallas_call | solution.py:477
  31.9 0.0 copy-done.16
  31.9 4.8 %all-to-all-start.1 = ((bf16[32,64,128]{2,1,0:T(8,128)(2,1)}), bf16[32,64,128]{2,1,0:T(8,128)(2,1)}, u32[]{:S(2)}, u32[]{:S(2)}) async-start(bf16[32,64,128]{2,1,0:T(8,128)(2,1)} %get-tuple-element.38), calls=%async_computation.1 | async-start | bytes 1048576 | tf_op jit(solution)/shard_map/all_to_all | solution.py:536
  36.8 0.0 copy-start.6
  36.8 1.4 copy-done.6
  38.2 0.0 copy-start.8
  38.2 1.4 copy-done.8
  39.6 0.0 copy-start.24
  39.6 1.4 copy-done.24
  41.0 0.0 copy-start.25
  41.0 1.4 copy-done.25
  42.4 0.0 copy-start.22
  42.4 7.6 %within.1 = (f32[768,128]{1,0:T(8,128)S(1)}, f32[8,768,128]{2,1,0:T(8,128)S(1)}, bf16[8,768,128]{2,1,0:T(8,128)(2,1)S(1)}, bf16[8,512,128]{2,1,0:T(8,128)(2,1)S(1)}, bf16[8,768,128]{2,1,0:T(8,128)(2,1)S(1)}) custom-call(f32[8,768]{1,0:T(8,128)S(1)} %get-tuple-element.31.cum_rows_ref, bf16[1,768,1024]{2,1,0:T(8,128)(2,1)S(1)} %copy-done.25, ...), custom_call_target="tpu_custom_call" | custom-call | flops 4000000000 | bytes 16777216 | tf_op jit(solution)/shard_map/within/pallas_call | solution.py:466
  50.1 0.0 copy-start
  50.1 1.6 %copy-done = f32[8,768,128]{2,1,0:T(8,128)} copy-done((f32[8,768,128]{2,1,0:T(8,128)}, f32[8,768,128]{2,1,0:T(8,128)S(1)}, u32[]{:S(2)}) %copy-start) | copy-done | bytes 3145752
  51.7 0.0 copy-start.12
  51.7 1.0 copy-done.12
  52.7 0.0 copy-start.18
  52.7 0.7 copy-done.18
  53.4 0.5 all-to-all-done.1.starts_ref
  53.9 0.0 copy-done.22
  53.9 1.9 %copy-done.1 = f32[8,768,128]{2,1,0:T(8,128)S(1)} copy-done((f32[8,768,128]{2,1,0:T(8,128)S(1)}, f32[8,768,128]{2,1,0:T(8,128)}, u32[]{:S(2)}) %copy-start.1) | copy-done | bytes 3145752
  55.8 1.0 copy-done.17
  56.9 3.2 %attend.1 = (f32[8,768,128]{2,1,0:T(8,128)S(1)}, bf16[8,128,128]{2,1,0:T(8,128)(2,1)S(1)}, f32[8,16,128]{2,1,0:T(8,128)S(1)}) custom-call(f32[8,8,128]{2,1,0:T(8,128)S(1)} %get-tuple-element.33.ends_ref, f32[8,128]{1,0:T(8,128)S(1)} %bitcast.3, bf16[8,768,128]{2,1,0:T(8,128)(2,1)S(1)} %get-tuple-element.34.queries_ref, ...), custom_call_target="tpu_custom_call" | custom-call | flops 300000000 | bytes 10485760 | tf_op jit(solution)/shard_map/attend/pallas_call | solution.py:485
  60.1 0.0 copy-start.2
  60.1 0.0 copy-start.31
  60.1 9.9 %all_to_all.26.stats_ref = f32[8,16,128]{2,1,0:T(8,128)S(1)} all-to-all(f32[8,16,128]{2,1,0:T(8,128)S(1)} %get-tuple-element.40), channel_id=1, replica_groups=mesh['seq'=32,'head'=8] {'head'}, dimensions={0} | all-to-all | bytes 131072 | tf_op jit(solution)/shard_map/all_to_all | solution.py:536
  70.0 2.7 %grad.1 = (bf16[8,768,128]{2,1,0:T(8,128)(2,1)S(1)}, bf16[32,64,128]{2,1,0:T(8,128)(2,1)S(1)}, f32[8,128,128]{2,1,0:T(8,128)S(1)}, f32[768,128]{1,0:T(8,128)S(1)}) custom-call(f32[8,8,128]{2,1,0:T(8,128)S(1)} %get-tuple-element.33.ends_ref, f32[8,128]{1,0:T(8,128)S(1)} %bitcast.4, f32[8,16,128]{2,1,0:T(8,128)S(1)} %all_to_all.26.stats_ref, ...), custom_call_target="tpu_custom_call" | custom-call | flops 300000000 | bytes 10485760 | tf_op jit(solution)/shard_map/grad/pallas_call | solution.py:496
  72.7 0.0 copy-done.2
  72.7 0.0 copy-done.31
  72.7 0.0 copy-start.14
  72.8 0.8 copy-done.14
  73.6 1.1 copy-done.27
  74.7 26.6 %all_to_all.27.got_ref = bf16[32,64,128]{2,1,0:T(8,128)(2,1)S(1)} all-to-all(bf16[32,64,128]{2,1,0:T(8,128)(2,1)S(1)} %get-tuple-element.47), channel_id=1, replica_groups=mesh['seq'=32,'head'=8] {'seq'}, dimensions={0} | all-to-all | bytes 1048576 | tf_op jit(solution)/shard_map/all_to_all | solution.py:536
  101.3 0.0 copy-done.29
  101.3 1.6 %backward_scan.1 = bf16[32,32,128]{2,1,0:T(8,128)(2,1)} custom-call(s32[32]{0:T(128)S(1)} %copy-done.23, bf16[32,64,128]{2,1,0:T(8,128)(2,1)S(1)} %all_to_all.27.got_ref, f32[32,128]{1,0:T(8,128)S(1)} %get-tuple-element.48.decay_ref), custom_call_target="tpu_custom_call" | custom-call | flops 1000000 | bytes 1048576 | tf_op jit(solution)/shard_map/backward_scan/pallas_call | solution.py:529
  102.9 4.8 %all-to-all-start.4 = ((bf16[32,32,128]{2,1,0:T(8,128)(2,1)}), bf16[32,32,128]{2,1,0:T(8,128)(2,1)S(1)}, u32[]{:S(2)}, u32[]{:S(2)}) async-start(bf16[32,32,128]{2,1,0:T(8,128)(2,1)} %backward_scan.1), calls=%async_computation.4 | async-start | bytes 524288 | tf_op jit(solution)/shard_map/all_to_all | solution.py:536
  107.7 0.0 copy-start.3
  107.8 1.9 %copy-done.3 = f32[8,768,128]{2,1,0:T(8,128)S(1)} copy-done((f32[8,768,128]{2,1,0:T(8,128)S(1)}, f32[8,768,128]{2,1,0:T(8,128)}, u32[]{:S(2)}) %copy-start.3) | copy-done | bytes 3145752
  109.6 1.4 copy-done.7
  111.0 1.4 copy-done.9
  112.5 1.0 copy-done.19
  113.5 1.4 copy-done.26
  114.9 1.4 copy-done.28
  116.3 1.0 copy-done.30
  117.3 0.9 copy-done.32
  118.2 12.9 %local_grads.1 = (bf16[1,768,1024]{2,1,0:T(8,128)(2,1)}, bf16[1,768,1024]{2,1,0:T(8,128)(2,1)}, f32[8,512,128]{2,1,0:T(8,128)S(1)}, f32[8,512,128]{2,1,0:T(8,128...) custom-call(f32[768,128]{1,0:T(8,128)S(1)} %copy-done.19, ...), custom_call_target="tpu_custom_call" | custom-call | flops 6000000000 | bytes 25165824 | tf_op jit(solution)/shard_map/local_grads/pallas_call | solution.py:509
  131.1 0.0 copy-start.4
  131.1 1.4 copy-done.4
  132.5 1.2 copy-done.10
  133.7 0.0 all-to-all-done.4.far_ref
  133.7 0.0 copy-done.13
  133.7 1.6 %copy-done.5 = f32[8,512,128]{2,1,0:T(8,128)S(1)} copy-done((f32[8,512,128]{2,1,0:T(8,128)S(1)}, f32[8,512,128]{2,1,0:T(8,128)}, u32[]{:S(2)}) %copy-start.5) | copy-done | bytes 2097176
  135.3 1.4 copy-done.11
  136.7 1.0 copy-done.15
  137.7 1.0 copy-done.20
  138.7 3.7 %far_grads.1 = (bf16[1,768,1024]{2,1,0:T(8,128)(2,1)}, bf16[1,768,1024]{2,1,0:T(8,128)(2,1)}) custom-call(f32[768,128]{1,0:T(8,128)S(1)} %copy-done.20, f32[8,8,128]{2,1,0:T(8,128)S(1)} %get-tuple-element.33.ends_ref, bf16[32,32,128]{2,1,0:T(8,128)(2,1)S(1)} %all-to-all-done.4.far_ref, ...), custom_call_target="tpu_custom_call", output_to_operand_aliasing={{0}: (8, {}), {1}: (9, {})} | custom-call | flops 300000000 | bytes 10485760 | tf_op jit(solution)/shard_map/far_grads/pallas_call | solution.py:521
  (17 shorter events, 0.0 us)
Async XLA Ops:
  0.6 0.7 copy-start.21
  1.4 29.1 %copy-start.23 = (s32[32]{0:T(128)S(1)}, s32[32]{0:T(128)}, u32[]{:S(2)}) copy-start(s32[32]{0:T(128)} %parents_ref.3) | copy-start | bytes 388
  4.5 27.4 %copy-start.16 = (f32[8,128,128]{2,1,0:T(8,128)}, f32[8,128,128]{2,1,0:T(8,128)S(1)}, u32[]{:S(2)}) copy-start(f32[8,128,128]{2,1,0:T(8,128)S(1)} %get-tuple-element.39.term_ref) | copy-start | bytes 1572868
  31.9 22.0 %all-to-all-start.1 = ((bf16[32,64,128]{2,1,0:T(8,128)(2,1)}), bf16[32,64,128]{2,1,0:T(8,128)(2,1)}, u32[]{:S(2)}, u32[]{:S(2)}) async-start(bf16[32,64,128]{2,1,0:T(8,128)(2,1)} %get-tuple-element.38), calls=%async_computation.1 | async-start | bytes 1048576 | tf_op jit(solution)/shard_map/all_to_all | solution.py:536
  36.8 1.4 copy-start.6
  38.2 1.4 copy-start.8
  39.6 1.4 copy-start.24
  41.0 1.4 copy-start.25
  42.4 11.5 %copy-start.22 = (f32[1024]{0:T(1024)S(1)}, f32[1024]{0:T(1024)}, u32[]{:S(2)}) copy-start(f32[1024]{0:T(1024)} %param.11) | copy-start | bytes 12292
  50.1 1.6 %copy-start = (f32[8,768,128]{2,1,0:T(8,128)}, f32[8,768,128]{2,1,0:T(8,128)S(1)}, u32[]{:S(2)}) copy-start(f32[8,768,128]{2,1,0:T(8,128)S(1)} %get-tuple-element.36.within_ref) | copy-start | bytes 9437188
  51.7 1.0 copy-start.12
  52.7 0.7 copy-start.18
  53.9 1.9 %copy-start.1 = (f32[8,768,128]{2,1,0:T(8,128)S(1)}, f32[8,768,128]{2,1,0:T(8,128)}, u32[]{:S(2)}) copy-start(f32[8,768,128]{2,1,0:T(8,128)} %copy-done) | copy-start | bytes 9437188
  55.8 1.0 copy-start.17
  60.1 12.7 %copy-start.2 = (f32[8,768,128]{2,1,0:T(8,128)}, f32[8,768,128]{2,1,0:T(8,128)S(1)}, u32[]{:S(2)}) copy-start(f32[8,768,128]{2,1,0:T(8,128)S(1)} %get-tuple-element.41.attended_ref) | copy-start | bytes 9437188
  60.1 12.7 %copy-start.31 = (bf16[8,128,128]{2,1,0:T(8,128)(2,1)}, bf16[8,128,128]{2,1,0:T(8,128)(2,1)S(1)}, u32[]{:S(2)}) copy-start(bf16[8,128,128]{2,1,0:T(8,128)(2,1)S(1)} %get-tuple-element.44.second_ref) | copy-start | bytes 786436
  72.7 0.8 copy-start.14
  73.6 1.1 copy-start.27
  74.7 26.6 %copy-start.29 = (f32[768,128]{1,0:T(8,128)}, f32[768,128]{1,0:T(8,128)S(1)}, u32[]{:S(2)}) copy-start(f32[768,128]{1,0:T(8,128)S(1)} %get-tuple-element.42.inverse_ref) | copy-start | bytes 1179652
  102.9 30.8 %all-to-all-start.4 = ((bf16[32,32,128]{2,1,0:T(8,128)(2,1)}), bf16[32,32,128]{2,1,0:T(8,128)(2,1)S(1)}, u32[]{:S(2)}, u32[]{:S(2)}) async-start(bf16[32,32,128]{2,1,0:T(8,128)(2,1)} %backward_scan.1), calls=%async_computation.4 | async-start | bytes 524288 | tf_op jit(solution)/shard_map/all_to_all | solution.py:536
  107.7 1.9 %copy-start.3 = (f32[8,768,128]{2,1,0:T(8,128)S(1)}, f32[8,768,128]{2,1,0:T(8,128)}, u32[]{:S(2)}) copy-start(f32[8,768,128]{2,1,0:T(8,128)} %copy-done.2) | copy-start | bytes 9437188
  109.6 1.4 copy-start.7
  111.0 1.4 copy-start.9
  112.5 1.0 copy-start.19
  113.4 1.4 copy-start.26
  114.9 1.4 copy-start.28
  116.3 1.0 copy-start.30
  117.3 0.9 copy-start.32
  118.2 15.5 %copy-start.13 = (bf16[8,512,128]{2,1,0:T(8,128)(2,1)S(1)}, bf16[8,512,128]{2,1,0:T(8,128)(2,1)}, u32[]{:S(2)}) copy-start(bf16[8,512,128]{2,1,0:T(8,128)(2,1)} %copy-done.12) | copy-start | bytes 3145732
  131.1 1.4 copy-start.4
  132.5 1.2 copy-start.10
  133.7 1.6 %copy-start.5 = (f32[8,512,128]{2,1,0:T(8,128)S(1)}, f32[8,512,128]{2,1,0:T(8,128)}, u32[]{:S(2)}) copy-start(f32[8,512,128]{2,1,0:T(8,128)} %copy-done.4) | copy-start | bytes 6291460
  135.3 1.4 copy-start.11
  136.7 1.0 copy-start.15
  137.7 1.0 copy-start.20

commit v3 on v2

--- a/solution.py
+++ b/solution.py
@@ -177,18 +177,26 @@
 
 
 def within_kernel(
-    cum_rows_ref, queries_ref, keys_ref, values_ref, d_out_ref,
-    cum_ref, within_ref, scaled_queries_ref, scaled_keys_ref, d_out_buf,
-    queries_buf, keys_buf, values_buf, in_sems,
+    cum_rows_ref, queries_ref, keys_ref, values_ref,
+    cum_ref, within_ref, scaled_queries_ref, scaled_keys_ref, done_ref,
+    queries_buf, keys_buf, values_buf, within_buf, scaled_queries_buf, scaled_keys_buf,
+    in_sems, out_sems,
 ):
     fetch = Copies(
         [
             (of_rows(queries_ref), of_lead(queries_buf)),
             (of_rows(keys_ref), of_lead(keys_buf)),
             (of_rows(values_ref), of_lead(values_buf)),
-            (of_rows(d_out_ref), of_lead(d_out_buf)),
         ],
         in_sems,
+    )
+    leave = Copies(
+        [
+            (of_lead(within_buf), of_lead(within_ref)),
+            (of_lead(scaled_queries_buf), of_lead(scaled_queries_ref)),
+            (of_lead(scaled_keys_buf), of_lead(scaled_keys_ref)),
+        ],
+        out_sems,
     )
     for head in range(HL):
         fetch.start(head)
@@ -198,6 +206,7 @@
             [cum_rows_ref[:, part], jnp.zeros((HD - HL, HD), F32)], axis=0
         )
         cum_ref[part, :] = padded.T
+    done_ref[...] = jnp.zeros_like(done_ref)
     row_ids = lax.broadcasted_iota(jnp.int32, (BLK, BLK), 0)
     col_ids = lax.broadcasted_iota(jnp.int32, (BLK, BLK), 1)
 
@@ -210,21 +219,24 @@
             gaps = col - cum_rows_ref[pl.ds(head, 1), part]
             mask = jnp.where(row_ids >= col_ids, jnp.exp(gaps), 0.0)
             weights = (mm_nt(queries, keys) * mask).astype(BF16)
-            within_ref[head, part, :] = mm(weights, values_buf[head, part, :])
-            scaled_queries_ref[head, part, :] = rounded_product(queries, jnp.exp(col))
+            within_buf[head, part, :] = mm(weights, values_buf[head, part, :])
+            scaled_queries_buf[head, part, :] = rounded_product(queries, jnp.exp(col))
             if number < 2:
                 factor = jnp.exp(col[BLK - 1 : BLK, :] - col)
-                scaled_keys_ref[head, part, :] = rounded_product(keys, factor)
+                scaled_keys_buf[head, part, :] = rounded_product(keys, factor)
 
     def step(head, carry):
         fetch.wait(head)
         body(head)
+        leave.start(head)
         return carry
 
     lax.fori_loop(0, HL, step, 0)
-
-
-def forward_scan_kernel(parents_ref, got_ref, send_ref, decay_ref):
+    for head in range(HL):
+        leave.wait(head)
+
+
+def forward_scan_kernel(parents_ref, got_ref, _after, send_ref, decay_ref):
     totals = []
     for prompt in range(PROMPTS):
         carry = jnp.zeros((PIECE, HD), F32)
@@ -260,7 +272,7 @@
             part = rows(number)
             attended = within_ref[head, part, :] + mm(queries_ref[head, part, :], start)
             attended_ref[head, part, :] = attended
-            weighted = gain * d_out_ref[head, part, :].astype(F32)
+            weighted = gain * d_out_ref[0, part, lanes(head)].astype(F32)
             squares_ref[part, :] += attended * attended
             products_ref[part, :] += weighted * attended
 
@@ -274,10 +286,7 @@
             )
 
 
-def grad_kernel(
-    ends_ref, gain_ref, stats_ref, queries_ref, d_out_ref, attended_ref,
-    grad_ref, send_ref, term_ref, inverse_ref, slope_ref,
-):
+def row_factors(stats_ref, inverse_ref, slope_ref):
     total = stats_ref[0]
     for source in range(1, HL):
         total = total + stats_ref[source]
@@ -290,20 +299,25 @@
         inverse_ref[tile_rows(tile), :] = jnp.broadcast_to(inverse, (HD, HD))
         slope_ref[tile_rows(tile), :] = jnp.broadcast_to(slope, (HD, HD))
 
+
+def grad_kernel(
+    ends_ref, gain_ref, stats_ref, queries_ref, d_out_ref, attended_ref,
+    send_ref, inverse_ref, slope_ref,
+):
+    row_factors(stats_ref, inverse_ref, slope_ref)
+
     def body(head):
         gain = gain_ref[pl.ds(head, 1), :]
         terms = []
         for number in range(BLOCKS):
             part = rows(number)
-            weighted = gain * d_out_ref[head, part, :].astype(F32)
+            weighted = gain * d_out_ref[0, part, lanes(head)].astype(F32)
             grad = (
                 inverse_ref[part, :] * weighted
                 - attended_ref[head, part, :] * slope_ref[part, :]
             ).astype(BF16)
-            grad_ref[head, part, :] = grad
             terms.append(mm_tn(queries_ref[head, part, :], grad))
         local_sum = ends_ref[head][0:1, :] * terms[1] + terms[0]
-        term_ref[head] = terms[1]
         for piece in range(PARTS):
             at = head * PARTS + piece
             part = slice(piece * PIECE, (piece + 1) * PIECE)
@@ -313,7 +327,7 @@
     over_heads(None, body)
 
 
-def backward_scan_kernel(parents_ref, got_ref, decay_ref, send_ref):
+def backward_scan_kernel(parents_ref, got_ref, decay_ref, _after, send_ref):
     branches = [jnp.zeros((PIECE, HD), F32) for _ in range(PROMPTS)]
     for index in range(N_SEQ):
         prompt = parents_ref[index] // SPAN
@@ -328,16 +342,22 @@
 
 
 def local_grads_kernel(
-    cum_ref, cum_rows_ref, inverse_ref, gain_ref,
-    queries_ref, keys_ref, values_ref, grad_ref, attended_ref, starts_ref, second_ref,
-    out_ref, d_queries_ref, part_keys_ref, part_values_ref, d_keys_ref, d_values_ref, values_buf,
-    queries_buf, keys_buf, out_buf, d_queries_buf, d_keys_buf, d_values_buf, in_sems, out_sems,
+    cum_ref, cum_rows_ref, stats_ref, gain_ref,
+    queries_ref, keys_ref, values_ref, d_out_ref, attended_ref, starts_ref, second_ref,
+    out_ref, d_queries_ref, part_keys_ref, part_values_ref, d_keys_ref, d_values_ref, term_ref,
+    done_ref, queries_buf, keys_buf, values_buf, d_out_buf, attended_buf, starts_buf, second_buf,
+    out_buf, d_queries_buf, part_keys_buf, part_values_buf, d_keys_buf, d_values_buf, term_buf,
+    inverse_ref, slope_ref, in_sems, out_sems,
 ):
     fetch = Copies(
         [
+            (of_rows(d_out_ref), of_lead(d_out_buf)),
+            (of_lead(attended_ref), of_lead(attended_buf)),
             (of_rows(queries_ref), of_lead(queries_buf)),
             (of_rows(keys_ref), of_lead(keys_buf)),
             (of_rows(values_ref), of_lead(values_buf)),
+            (of_lead(starts_ref, PARTS), of_lead(starts_buf, PARTS)),
+            (of_lead(second_ref), of_lead(second_buf)),
         ],
         in_sems,
     )
@@ -345,25 +365,36 @@
         [
             (of_lead(out_buf), of_rows(out_ref)),
             (of_lead(d_queries_buf), of_rows(d_queries_ref)),
+            (of_lead(part_keys_buf), of_lead(part_keys_ref)),
+            (of_lead(part_values_buf), of_lead(part_values_ref)),
             (of_lead(d_keys_buf), of_rows(d_keys_ref, BLK, P_DEV)),
             (of_lead(d_values_buf), of_rows(d_values_ref, BLK, P_DEV)),
+            (of_lead(term_buf), of_lead(term_ref)),
         ],
         out_sems,
     )
+    for head in range(HL):
+        fetch.start(head)
+    done_ref[...] = jnp.zeros_like(done_ref)
+    row_factors(stats_ref, inverse_ref, slope_ref)
     row_ids = lax.broadcasted_iota(jnp.int32, (BLK, BLK), 0)
     col_ids = lax.broadcasted_iota(jnp.int32, (BLK, BLK), 1)
 
     def body(head):
-        got = starts_ref[pl.ds(head * PARTS, PARTS)]
+        got = starts_buf[pl.ds(head * PARTS, PARTS)]
         first = got[:, 0:PIECE, :].reshape(HD, HD)
         reply = got[:, PIECE : 2 * PIECE, :].reshape(HD, HD)
         gain = gain_ref[pl.ds(head, 1), :]
-        for number, start in enumerate((first, second_ref[head], reply)):
+        for number, start in enumerate((first, second_buf[head], reply)):
             part = rows(number)
             queries = queries_buf[head, part, :]
             keys = keys_buf[head, part, :]
             values = values_buf[head, part, :]
-            grad = grad_ref[head, part, :]
+            attended = attended_buf[head, part, :]
+            inverse = inverse_ref[part, :]
+            weighted = gain * d_out_buf[head, part, :].astype(F32)
+            grad = (inverse * weighted - attended * slope_ref[part, :]).astype(BF16)
+            out_buf[head, part, :] = (attended * inverse * gain).astype(BF16)
             col = column(cum_ref, number, head)
             gaps = cum_rows_ref[pl.ds(head, 1), part] - col
             mask = jnp.where(col_ids >= row_ids, jnp.exp(gaps), 0.0)
@@ -371,19 +402,27 @@
             score_grad = (mm_nt(values, grad) * mask).astype(BF16)
             grad_values = mm(weights, grad)
             grad_keys = mm(score_grad, queries)
-            grad_queries = mm_tn(score_grad, keys) + jnp.exp(col) * mm_nt(grad, start)
+            growth = jnp.exp(col)
+            grad_queries = mm_tn(score_grad, keys) + growth * mm_nt(grad, start)
             d_queries_buf[head, part, :] = grad_queries.astype(BF16)
-            out_buf[head, part, :] = (
-                attended_ref[head, part, :] * inverse_ref[part, :] * gain
-            ).astype(BF16)
+            if number == 1:
+                term_buf[head] = mm_tn(rounded_product(queries, growth), grad)
             if number < 2:
-                part_keys_ref[head, part, :] = grad_keys
-                part_values_ref[head, part, :] = grad_values
+                part_keys_buf[head, part, :] = grad_keys
+                part_values_buf[head, part, :] = grad_values
             else:
                 d_keys_buf[head] = grad_keys.astype(BF16)
                 d_values_buf[head] = grad_values.astype(BF16)
 
-    over_heads(fetch, body, leave)
+    def step(head, carry):
+        fetch.wait(head)
+        body(head)
+        leave.start(head)
+        return carry
+
+    lax.fori_loop(0, HL, step, 0)
+    for head in range(HL):
+        leave.wait(head)
 
 
 def far_grads_kernel(
@@ -408,7 +447,7 @@
             factor = jnp.exp(col[BLK - 1 : BLK, :] - col)
             grad_values = part_values_ref[head, part, :] + mm(scaled_keys_ref[head, part, :], end_grad)
             grad_keys = part_keys_ref[head, part, :] + factor * mm_nt(
-                values_ref[head, part, :], end_grad
+                values_ref[0, part, lanes(head)], end_grad
             )
             d_values_buf[head, part, :] = grad_values.astype(BF16)
             d_keys_buf[head, part, :] = grad_keys.astype(BF16)
@@ -462,23 +501,24 @@
     )(decay_rows, keys, values)
 
 
-def inside(cum_rows, queries, keys, values, d_out):
-    return call(
-        within_kernel, "within", [VMEM] + [HBM] * 4,
-        [
-            (VMEM, shape(CUM, F32)), (VMEM, shape(HEAD_ROWS, F32)), (VMEM, shape(HEAD_ROWS, BF16)),
-            (VMEM, shape(HEAD_PROMPT, BF16)), (VMEM, shape(HEAD_ROWS, BF16)),
-        ],
-        [(HEAD_ROWS, BF16)] * 3, [4], 20, 4e9, 16,
-    )(cum_rows, queries, keys, values, d_out)
-
-
-def forward_scan(parents, got):
-    return call(
-        forward_scan_kernel, "forward_scan", [SMEM, VMEM],
+def inside(cum_rows, queries, keys, values):
+    return call(
+        within_kernel, "within", [VMEM] + [HBM] * 3,
+        [
+            (VMEM, shape(CUM, F32)), (HBM, shape(HEAD_ROWS, F32)), (HBM, shape(HEAD_ROWS, BF16)),
+            (HBM, shape(HEAD_PROMPT, BF16)), (VMEM, shape((8, HD), F32)),
+        ],
+        [(HEAD_ROWS, BF16)] * 3 + [(HEAD_ROWS, F32), (HEAD_ROWS, BF16), (HEAD_PROMPT, BF16)],
+        [3, 3], 56, 4e9, 16,
+    )(cum_rows, queries, keys, values)
+
+
+def forward_scan(parents, got, after):
+    return call(
+        forward_scan_kernel, "forward_scan", [SMEM, VMEM, HBM],
         [(VMEM, shape(TWO_PIECES, BF16)), (VMEM, shape((N_SEQ, HD), F32))],
         [], [], 12, 1e6, 1,
-    )(parents, got)
+    )(parents, got, after)
 
 
 def attend(ends, gains, scaled_queries, d_out, within, starts, term):
@@ -494,42 +534,41 @@
 
 def grads(ends, gains, stats, scaled_queries, d_out, attended):
     return call(
-        grad_kernel, "grad", [VMEM] * 6,
-        [
-            (VMEM, shape(HEAD_ROWS, BF16)), (VMEM, shape(TWO_PIECES, BF16)),
-            (VMEM, shape(STATE, F32)), (VMEM, shape(CUM, F32)),
-        ],
-        [(CUM, F32)], [], 20, 3e8, 10,
-    )(ends, gains, stats, scaled_queries, d_out, attended)
+        grad_kernel, "grad", [VMEM] * 6, [(VMEM, shape(TWO_PIECES, BF16))],
+        [(CUM, F32), (CUM, F32)], [], 20, 3e8, 10,
+    )(ends, gains, stats, scaled_queries, d_out, attended)[0]
 
 
 def local_grads(
-    cum, cum_rows, inverse, gains, queries, keys, values, grad, attended, starts, second
+    cum, cum_rows, stats, gains, queries, keys, values, d_out, attended, starts, second
 ):
     return call(
-        local_grads_kernel, "local_grads", [VMEM] * 4 + [HBM] * 3 + [VMEM] * 4,
-        [
-            (HBM, WIDE), (HBM, WIDE), (VMEM, shape(HEAD_PROMPT, F32)),
-            (VMEM, shape(HEAD_PROMPT, F32)), (HBM, WIDE), (HBM, WIDE),
-            (VMEM, shape(HEAD_ROWS, BF16)),
-        ],
-        [(HEAD_ROWS, BF16)] * 4 + [(HEAD_REPLY, BF16)] * 2, [3, 4], 28, 6e9, 24,
-    )(cum, cum_rows, inverse, gains, queries, keys, values, grad, attended, starts, second)
+        local_grads_kernel, "local_grads", [VMEM] * 4 + [HBM] * 7,
+        [
+            (HBM, WIDE), (HBM, WIDE), (HBM, shape(HEAD_PROMPT, F32)),
+            (HBM, shape(HEAD_PROMPT, F32)), (HBM, WIDE), (HBM, WIDE), (HBM, shape(STATE, F32)),
+            (VMEM, shape((8, HD), F32)),
+        ],
+        [(HEAD_ROWS, BF16)] * 4 + [(HEAD_ROWS, F32), (TWO_PIECES, BF16), (STATE, BF16)]
+        + [(HEAD_ROWS, BF16)] * 2 + [(HEAD_PROMPT, F32)] * 2 + [(HEAD_REPLY, BF16)] * 2
+        + [(STATE, F32), (CUM, F32), (CUM, F32)],
+        [7, 7], 56, 6e9, 24,
+    )(cum, cum_rows, stats, gains, queries, keys, values, d_out, attended, starts, second)
 
 
 def far_grads(cum, ends, far, term, scaled_keys, values, part_keys, part_values, d_keys, d_values):
     return call(
         far_grads_kernel, "far_grads", [VMEM] * 8 + [HBM] * 2,
         [(HBM, WIDE), (HBM, WIDE)],
-        [(HEAD_PROMPT, BF16), (HEAD_PROMPT, BF16)], [2], 20, 3e8, 10, {8: 0, 9: 1},
+        [(HEAD_PROMPT, BF16), (HEAD_PROMPT, BF16)], [2], 24, 3e8, 10, {8: 0, 9: 1},
     )(cum, ends, far, term, scaled_keys, values, part_keys, part_values, d_keys, d_values)
 
 
-def backward_scan(parents, got, decays):
-    return call(
-        backward_scan_kernel, "backward_scan", [SMEM, VMEM, VMEM],
+def backward_scan(parents, got, decays, after):
+    return call(
+        backward_scan_kernel, "backward_scan", [SMEM, VMEM, VMEM, HBM],
         [(VMEM, shape(PIECES, BF16))], [], [], 12, 1e6, 1,
-    )(parents, got, decays)[0]
+    )(parents, got, decays, after)[0]
 
 
 def everyone(array, axis):
@@ -541,25 +580,21 @@
     decay_rows = jnp.swapaxes(log_decay, 1, 2)
     send, first_term, cum_rows, block_ends = summarize(decay_rows, keys, values)
     got = everyone(send, "seq")
-    cum, within, scaled_queries, scaled_keys, d_out_heads = inside(
-        cum_rows, queries, keys, values, d_out
-    )
-    send, decays = forward_scan(parents, got)
+    cum, within, scaled_queries, scaled_keys, done = inside(cum_rows, queries, keys, values)
+    send, decays = forward_scan(parents, got, done)
     starts = everyone(send, "seq")
     attended, second, stats = attend(
-        block_ends, gains, scaled_queries, d_out_heads, within, starts, first_term
+        block_ends, gains, scaled_queries, d_out, within, starts, first_term
     )
     stats = everyone(stats, "head")
-    grad, send, last_term, inverse = grads(
-        block_ends, gains, stats, scaled_queries, d_out_heads, attended
-    )
+    send = grads(block_ends, gains, stats, scaled_queries, d_out, attended)
     got = everyone(send, "seq")
-    out, d_queries, part_keys, part_values, d_keys, d_values, value_heads = local_grads(
-        cum, cum_rows, inverse, gains, queries, keys, values, grad, attended, starts, second
-    )
-    far = everyone(backward_scan(parents, got, decays), "seq")
+    out, d_queries, part_keys, part_values, d_keys, d_values, last_term, done = local_grads(
+        cum, cum_rows, stats, gains, queries, keys, values, d_out, attended, starts, second
+    )
+    far = everyone(backward_scan(parents, got, decays, done), "seq")
     d_keys, d_values = far_grads(
-        cum, block_ends, far, last_term, scaled_keys, value_heads, part_keys, part_values,
+        cum, block_ends, far, last_term, scaled_keys, values, part_keys, part_values,
         d_keys, d_values,
     )
     return (out, d_queries, d_keys, d_values)

time: 144 us -> 129 us (0.90)
  local copies, waits for them, and re-layouts: 32.6 us -> 14.2 us
  blocking collectives: 62.4 us -> 49.6 us
  waiting for transfers between devices: 0.51 us -> 8.54 us
  starting transfers between devices: 9.69 us -> 16 us
  Pallas kernels: 36.4 us -> 38.8 us
    unnamed x66 -> x46, local copies, waits for them, and re-layouts: 32.6 us -> 14.2 us
    all_to_all x3, blocking collectives: 62.4 us -> 49.6 us  [everyone(): return lax.all_to_all(array, axis, 0, 0, tiled=True)]
    all_to_all x2, waiting for transfers between devices: 0.51 us -> 8.54 us  [everyone(): return lax.all_to_all(array, axis, 0, 0, tiled=True)]
    all_to_all x2, starting transfers between devices: 9.69 us -> 16 us  [everyone(): return lax.all_to_all(array, axis, 0, 0, tiled=True)]
    pallas_call x5, Pallas kernels: 26.4 us -> 29 us  [the longest x1 14.3 us: local_grads(): call(local_grads_kernel, 'local_grads', [VMEM] * 4 + [HBM] * 7, [(HBM, WI...]
  transfers between devices with their start and end apart: 2 -> 2, of which waited for: 1 -> 2; matrix products, arithmetic and copies ran while one was open for 0% -> 0% of each run, Pallas kernels for 14% -> 19%
where the time goes in v3:
time: 129 us; the launch traced here: 128 us
  blocking collectives  49.6 us (38%)
  Pallas kernels  38.8 us (30%)
  starting transfers between devices  16 us (12%)
  local copies, waits for them, and re-layouts  14.2 us (11%)
  waiting for transfers between devices  8.54 us (7%)
    all_to_all x3, blocking collectives, everyone(): return lax.all_to_all(array, axis, 0, 0, tiled=True)  49.6 us
    all_to_all x2, starting transfers between devices, everyone(): return lax.all_to_all(array, axis, 0, 0, tiled=True)  16 us
    pallas_call x1, Pallas kernels, local_grads(): call(local_grads_kernel, 'local_grads', [VMEM] * 4 + [HBM] * 7, [(HBM, WI...  14.3 us
    unnamed x46, local copies, waits for them, and re-layouts  14.2 us
    pallas_call x1, Pallas kernels, inside(): call(within_kernel, 'within', [VMEM] + [HBM] * 3, [(VMEM, shape(CUM, F32)...  9.5 us
    all_to_all x2, waiting for transfers between devices, everyone(): return lax.all_to_all(array, axis, 0, 0, tiled=True)  8.54 us
    pallas_call x1, Pallas kernels, summarize(): call(summary_kernel, 'summary', [VMEM, HBM, HBM], [(VMEM, shape(SENT_PIEC...  3.9 us
    pallas_call x1, Pallas kernels, far_grads(): call(far_grads_kernel, 'far_grads', [VMEM] * 8 + [HBM] * 2, [(HBM, WIDE),...  3.77 us
  transfers between devices with their start and end apart: 2, of which 2 were waited for; matrix products, arithmetic and copies ran while one was open for 0% of the time, Pallas kernels for 19%

profile of v3, /device:TPU:32, one launch (start us, length us, event | category | flops | bytes accessed | tf_op | source)
XLA Modules:
  0.0 128.0 jit_solution(16768274668981386796)
XLA Ops:
  0.6 0.0 copy-start.15
  0.6 0.7 copy-done.15
  1.4 3.9 %summary.1 = (bf16[32,48,128]{2,1,0:T(8,128)(2,1)}, f32[8,128,128]{2,1,0:T(8,128)S(1)}, f32[8,768]{1,0:T(8,128)S(1)}, f32[8,8,128]{2,1,0:T(8,128)S(1)}) custom-call(f32[1,8,768]{2,1,0:T(8,128)S(1)} %bitcast.2, bf16[1,768,1024]{2,1,0:T(8,128)(2,1)} %keys_ref.5, bf16[1,768,1024]{2,1,0:T(8,128)(2,1)} %values_ref.7), custom_call_target="tpu_custom_call" | custom-call | flops 300000000 | bytes 4194304 | tf_op jit(solution)/shard_map/summary/pallas_call | solution.py:494
  5.3 0.0 copy-start.22
  5.3 0.6 copy-done.22
  5.9 0.0 copy-start.12
  5.9 11.2 %all-to-all-start = ((bf16[32,48,128]{2,1,0:T(8,128)(2,1)}), bf16[32,48,128]{2,1,0:T(8,128)(2,1)S(1)}, u32[]{:S(2)}, u32[]{:S(2)}) async-start(bf16[32,48,128]{2,1,0:T(8,128)(2,1)} %get-tuple-element.33), calls=%async_computation | async-start | bytes 786432 | tf_op jit(solution)/shard_map/all_to_all | solution.py:575
  17.1 0.0 copy-start.19
  17.1 0.0 copy-start
  17.1 0.0 copy-start.16
  17.1 9.5 %within.1 = (f32[768,128]{1,0:T(8,128)}, f32[8,768,128]{2,1,0:T(8,128)}, bf16[8,768,128]{2,1,0:T(8,128)(2,1)}, bf16[8,512,128]{2,1,0:T(8,128)(2,1)}, f32[8,128]{1,0:T(8,128)}) custom-call(f32[8,768]{1,0:T(8,128)} %copy-done.22, bf16[1,768,1024]{2,1,0:T(8,128)(2,1)} %queries_ref.3, bf16[1,768,1024]{2,1,0:T(8,128)(2,1)} %keys_ref.5, ...), custom_call_target="tpu_custom_call" | custom-call | flops 4000000000 | bytes 16777216 | tf_op jit(solution)/shard_map/within/pallas_call | solution.py:505
  26.6 5.3 %all-to-all-done.got_ref = bf16[32,48,128]{2,1,0:T(8,128)(2,1)S(1)} async-done(((bf16[32,48,128]{2,1,0:T(8,128)(2,1)}), bf16[32,48,128]{2,1,0:T(8,128)(2,1)S(1)}, u32[]{:S(2)}, u32[]{:S(2)}) %all-to-all-start) | async-done | bytes 393248 | tf_op jit(solution)/shard_map/all_to_all | solution.py:575
  32.0 0.0 copy-done.19
  32.0 0.0 copy-start.18
  32.0 0.7 copy-done.18
  32.7 0.7 forward_scan.1
  33.4 21.7 %all_to_all.25.starts_ref = bf16[32,64,128]{2,1,0:T(8,128)(2,1)S(1)} all-to-all(bf16[32,64,128]{2,1,0:T(8,128)(2,1)S(1)} %get-tuple-element.35), channel_id=1, replica_groups=mesh['seq'=32,'head'=8] {'seq'}, dimensions={0} | all-to-all | bytes 1048576 | tf_op jit(solution)/shard_map/all_to_all | solution.py:575
  55.1 0.0 copy-start.6
  55.1 0.0 copy-done
  55.1 0.0 copy-done.16
  55.1 0.0 copy-start.1
  55.1 1.6 %copy-done.1 = bf16[8,768,128]{2,1,0:T(8,128)(2,1)S(1)} copy-done((bf16[8,768,128]{2,1,0:T(8,128)(2,1)S(1)}, bf16[8,768,128]{2,1,0:T(8,128)(2,1)}, u32[]{:S(2)}) %copy-start.1) | copy-done | bytes 1572888
  56.7 0.0 copy-start.5
  56.7 1.9 %copy-done.5 = f32[8,768,128]{2,1,0:T(8,128)S(1)} copy-done((f32[8,768,128]{2,1,0:T(8,128)S(1)}, f32[8,768,128]{2,1,0:T(8,128)}, u32[]{:S(2)}) %copy-start.5) | copy-done | bytes 3145752
  58.5 0.0 copy-start.2
  58.6 2.2 %attend.1 = (f32[8,768,128]{2,1,0:T(8,128)S(1)}, bf16[8,128,128]{2,1,0:T(8,128)(2,1)S(1)}, f32[8,16,128]{2,1,0:T(8,128)S(1)}) custom-call(f32[8,8,128]{2,1,0:T(8,128)S(1)} %get-tuple-element.30.ends_ref, f32[8,128]{1,0:T(8,128)S(1)} %bitcast.4, bf16[8,768,128]{2,1,0:T(8,128)(2,1)S(1)} %copy-done.1, bf16[1,768,1024]{2,1,0:T(8,128)(2,1)S(1)} %copy-done, ...), custom_call_target="tpu_custom_call" | custom-call | flops 300000000 | bytes 10485760 | tf_op jit(solution)/shard_map/attend/pallas_call | solution.py:525
  60.7 0.0 copy-done.6
  60.7 0.0 copy-start.21
  60.7 0.7 copy-done.21
  61.4 9.9 %all_to_all.26.stats_ref = f32[8,16,128]{2,1,0:T(8,128)S(1)} all-to-all(f32[8,16,128]{2,1,0:T(8,128)S(1)} %get-tuple-element.37), channel_id=1, replica_groups=mesh['seq'=32,'head'=8] {'head'}, dimensions={0} | all-to-all | bytes 131072 | tf_op jit(solution)/shard_map/all_to_all | solution.py:575
  71.3 0.0 copy-start.14
  71.3 0.0 copy-done.12
  71.3 0.0 copy-done.2
  71.3 3.6 %grad.1 = bf16[32,64,128]{2,1,0:T(8,128)(2,1)} custom-call(f32[8,8,128]{2,1,0:T(8,128)S(1)} %get-tuple-element.30.ends_ref, f32[8,128]{1,0:T(8,128)S(1)} %bitcast.5, f32[8,16,128]{2,1,0:T(8,128)S(1)} %all_to_all.26.stats_ref, bf16[8,768,128]{2,1,0:T(8,128)(2,1)S(1)} %copy-done.2, bf16[1,768,1024]{2,1,0:T(8,128)(2,1)S(1)} %copy-done, ...), custom_call_target="tpu_custom_call" | custom-call | flops 300000000 | bytes 10485760 | tf_op jit(solution)/shard_map/grad/pallas_call | solution.py:536
  74.9 0.0 copy-done.14
  74.9 0.0 copy-start.4
  74.9 1.6 %copy-done.4 = f32[8,768,128]{2,1,0:T(8,128)} copy-done((f32[8,768,128]{2,1,0:T(8,128)}, f32[8,768,128]{2,1,0:T(8,128)S(1)}, u32[]{:S(2)}) %copy-start.4) | copy-done | bytes 3145752
  76.6 4.8 %all-to-all-start.3 = ((bf16[32,64,128]{2,1,0:T(8,128)(2,1)}), bf16[32,64,128]{2,1,0:T(8,128)(2,1)S(1)}, u32[]{:S(2)}, u32[]{:S(2)}) async-start(bf16[32,64,128]{2,1,0:T(8,128)(2,1)} %grad.1), calls=%async_computation.3 | async-start | bytes 1048576 | tf_op jit(solution)/shard_map/all_to_all | solution.py:575
  81.4 0.0 copy-start.3
  81.4 0.0 copy-start.11
  81.4 14.3 %local_grads.1 = (bf16[1,768,1024]{2,1,0:T(8,128)(2,1)}, bf16[1,768,1024]{2,1,0:T(8,128)(2,1)}, f32[8,512,128]{2,1,0:T(8,128)}, f32[8,512,128]{2,1,0:T(8,128)}, ...) custom-call(f32[768,128]{1,0:T(8,128)} %get-tuple-element.29.cum_ref, ...), custom_call_target="tpu_custom_call" | custom-call | flops 6000000000 | bytes 25165824 | tf_op jit(solution)/shard_map/local_grads/pallas_call | solution.py:545
  95.7 0.0 copy-start.9
  95.7 3.2 %all-to-all-done.3.got_ref = bf16[32,64,128]{2,1,0:T(8,128)(2,1)S(1)} async-done(((bf16[32,64,128]{2,1,0:T(8,128)(2,1)}), bf16[32,64,128]{2,1,0:T(8,128)(2,1)S(1)}, u32[]{:S(2)}, u32[]{:S(2)}) %all-to-all-start.3) | async-done | bytes 524320 | tf_op jit(solution)/shard_map/all_to_all | solution.py:575
  98.9 0.0 copy-start.17
  99.0 0.7 copy-done.17
  99.6 0.0 copy-start.20
  99.6 0.7 copy-done.20
  100.3 0.9 backward_scan.1
  101.1 18.1 %all_to_all.27.far_ref = bf16[32,32,128]{2,1,0:T(8,128)(2,1)S(1)} all-to-all(bf16[32,32,128]{2,1,0:T(8,128)(2,1)S(1)} %backward_scan.1), channel_id=1, replica_groups=mesh['seq'=32,'head'=8] {'seq'}, dimensions={0} | all-to-all | bytes 524288 | tf_op jit(solution)/shard_map/all_to_all | solution.py:575
  119.2 0.0 copy-done.3
  119.3 0.0 copy-done.11
  119.3 0.0 copy-done.9
  119.3 0.0 copy-start.7
  119.3 1.6 %copy-done.7 = f32[8,512,128]{2,1,0:T(8,128)S(1)} copy-done((f32[8,512,128]{2,1,0:T(8,128)S(1)}, f32[8,512,128]{2,1,0:T(8,128)}, u32[]{:S(2)}) %copy-start.7) | copy-done | bytes 2097176
  120.9 0.0 copy-start.8
  120.9 1.6 %copy-done.8 = f32[8,512,128]{2,1,0:T(8,128)S(1)} copy-done((f32[8,512,128]{2,1,0:T(8,128)S(1)}, f32[8,512,128]{2,1,0:T(8,128)}, u32[]{:S(2)}) %copy-start.8) | copy-done | bytes 2097176
  122.4 0.0 copy-start.10
  122.4 1.0 copy-done.10
  123.5 0.0 copy-start.13
  123.5 0.8 copy-done.13
  124.2 3.8 %far_grads.1 = (bf16[1,768,1024]{2,1,0:T(8,128)(2,1)}, bf16[1,768,1024]{2,1,0:T(8,128)(2,1)}) custom-call(f32[768,128]{1,0:T(8,128)S(1)} %copy-done.11, f32[8,8,128]{2,1,0:T(8,128)S(1)} %copy-done.13, bf16[32,32,128]{2,1,0:T(8,128)(2,1)S(1)} %all_to_all.27.far_ref, f32[8,128,128]{2,1,0:T(8,128)S(1)} %copy-done.10, ...), custom_call_target="tpu_custom_call", output_to_operand_aliasing={{0}: (8, {}), {1}: (9, {})} | custom-call | flops 300000000 | bytes 10485760 | tf_op jit(solution)/shard_map/far_grads/pallas_call | solution.py:560
Async XLA Ops:
  0.6 0.7 copy-start.15
  5.3 0.6 copy-start.22
  5.9 65.4 %copy-start.12 = (f32[8,8,128]{2,1,0:T(8,128)}, f32[8,8,128]{2,1,0:T(8,128)S(1)}, u32[]{:S(2)}) copy-start(f32[8,8,128]{2,1,0:T(8,128)S(1)} %get-tuple-element.30.ends_ref) | copy-start | bytes 98308
  5.9 26.1 %all-to-all-start = ((bf16[32,48,128]{2,1,0:T(8,128)(2,1)}), bf16[32,48,128]{2,1,0:T(8,128)(2,1)S(1)}, u32[]{:S(2)}, u32[]{:S(2)}) async-start(bf16[32,48,128]{2,1,0:T(8,128)(2,1)} %get-tuple-element.33), calls=%async_computation | async-start | bytes 786432 | tf_op jit(solution)/shard_map/all_to_all | solution.py:575
  17.1 14.9 %copy-start.19 = (s32[32]{0:T(128)S(1)}, s32[32]{0:T(128)}, u32[]{:S(2)}) copy-start(s32[32]{0:T(128)} %parents_ref.3) | copy-start | bytes 388
  17.1 38.0 %copy-start = (bf16[1,768,1024]{2,1,0:T(8,128)(2,1)S(1)}, bf16[1,768,1024]{2,1,0:T(8,128)(2,1)}, u32[]{:S(2)}) copy-start(bf16[1,768,1024]{2,1,0:T(8,128)(2,1)} %d_out_ref.5) | copy-start | bytes 4718596
  17.1 38.0 %copy-start.16 = (f32[1024]{0:T(1024)S(1)}, f32[1024]{0:T(1024)}, u32[]{:S(2)}) copy-start(f32[1024]{0:T(1024)} %param.11) | copy-start | bytes 12292
  32.0 0.7 copy-start.18
  55.1 5.7 %copy-start.6 = (bf16[32,64,128]{2,1,0:T(8,128)(2,1)}, bf16[32,64,128]{2,1,0:T(8,128)(2,1)S(1)}, u32[]{:S(2)}) copy-start(bf16[32,64,128]{2,1,0:T(8,128)(2,1)S(1)} %all_to_all.25.starts_ref) | copy-start | bytes 1572868
  55.1 1.6 %copy-start.1 = (bf16[8,768,128]{2,1,0:T(8,128)(2,1)S(1)}, bf16[8,768,128]{2,1,0:T(8,128)(2,1)}, u32[]{:S(2)}) copy-start(bf16[8,768,128]{2,1,0:T(8,128)(2,1)} %get-tuple-element.31.queries_ref) | copy-start | bytes 4718596
  56.7 1.9 %copy-start.5 = (f32[8,768,128]{2,1,0:T(8,128)S(1)}, f32[8,768,128]{2,1,0:T(8,128)}, u32[]{:S(2)}) copy-start(f32[8,768,128]{2,1,0:T(8,128)} %get-tuple-element.32.within_ref) | copy-start | bytes 9437188
  58.5 12.8 %copy-start.2 = (bf16[8,768,128]{2,1,0:T(8,128)(2,1)S(1)}, bf16[8,768,128]{2,1,0:T(8,128)(2,1)}, u32[]{:S(2)}) copy-start(bf16[8,768,128]{2,1,0:T(8,128)(2,1)} %get-tuple-element.31.queries_ref) | copy-start | bytes 4718596
  60.7 0.7 copy-start.21
  71.3 3.6 %copy-start.14 = (f32[8,16,128]{2,1,0:T(8,128)}, f32[8,16,128]{2,1,0:T(8,128)S(1)}, u32[]{:S(2)}) copy-start(f32[8,16,128]{2,1,0:T(8,128)S(1)} %all_to_all.26.stats_ref) | copy-start | bytes 196612
  74.9 1.6 %copy-start.4 = (f32[8,768,128]{2,1,0:T(8,128)}, f32[8,768,128]{2,1,0:T(8,128)S(1)}, u32[]{:S(2)}) copy-start(f32[8,768,128]{2,1,0:T(8,128)S(1)} %get-tuple-element.38.attended_ref) | copy-start | bytes 9437188
  76.6 22.4 %all-to-all-start.3 = ((bf16[32,64,128]{2,1,0:T(8,128)(2,1)}), bf16[32,64,128]{2,1,0:T(8,128)(2,1)S(1)}, u32[]{:S(2)}, u32[]{:S(2)}) async-start(bf16[32,64,128]{2,1,0:T(8,128)(2,1)} %grad.1), calls=%async_computation.3 | async-start | bytes 1048576 | tf_op jit(solution)/shard_map/all_to_all | solution.py:575
  81.4 37.8 %copy-start.3 = (bf16[1,768,1024]{2,1,0:T(8,128)(2,1)S(1)}, bf16[1,768,1024]{2,1,0:T(8,128)(2,1)}, u32[]{:S(2)}) copy-start(bf16[1,768,1024]{2,1,0:T(8,128)(2,1)} %values_ref.7) | copy-start | bytes 4718596
  81.4 37.8 %copy-start.11 = (f32[768,128]{1,0:T(8,128)S(1)}, f32[768,128]{1,0:T(8,128)}, u32[]{:S(2)}) copy-start(f32[768,128]{1,0:T(8,128)} %get-tuple-element.29.cum_ref) | copy-start | bytes 1179652
  95.7 23.5 %copy-start.9 = (bf16[8,512,128]{2,1,0:T(8,128)(2,1)S(1)}, bf16[8,512,128]{2,1,0:T(8,128)(2,1)}, u32[]{:S(2)}) copy-start(bf16[8,512,128]{2,1,0:T(8,128)(2,1)} %get-tuple-element.45.scaled_keys_ref) | copy-start | bytes 3145732
  98.9 0.7 copy-start.17
  99.6 0.7 copy-start.20
  119.3 1.6 %copy-start.7 = (f32[8,512,128]{2,1,0:T(8,128)S(1)}, f32[8,512,128]{2,1,0:T(8,128)}, u32[]{:S(2)}) copy-start(f32[8,512,128]{2,1,0:T(8,128)} %get-tuple-element.46.part_keys_ref) | copy-start | bytes 6291460
  120.9 1.6 %copy-start.8 = (f32[8,512,128]{2,1,0:T(8,128)S(1)}, f32[8,512,128]{2,1,0:T(8,128)}, u32[]{:S(2)}) copy-start(f32[8,512,128]{2,1,0:T(8,128)} %get-tuple-element.47.part_values_ref) | copy-start | bytes 6291460
  122.4 1.0 copy-start.10
  123.5 0.8 copy-start.13

commit v4 on v3

--- a/solution.py
+++ b/solution.py
@@ -49,9 +49,12 @@
     return slice(tile * HD, (tile + 1) * HD)
 
 
-def column(cum_ref, number, head):
-    block = pltpu.roll(cum_ref[rows(number), :], lax.rem(HD - head, HD), 1)
-    return block[:, 0:1]
+def down(row):
+    return jnp.broadcast_to(row, (HD, BLK)).T
+
+
+def twice(block):
+    return jnp.concatenate([block, block], axis=1)
 
 
 def rounded_product(block, factor):
@@ -68,9 +71,9 @@
     return lambda head: ref.at[pl.ds(first, count), lanes(head)]
 
 
-def of_lead(ref, count=1):
+def of_lead(ref, count=1, first=0):
     if count == 1:
-        return lambda head: ref.at[head]
+        return lambda head: ref.at[head + first]
     return lambda head: ref.at[pl.ds(head * count, count)]
 
 
@@ -93,8 +96,8 @@
             copy.wait()
 
 
-def over_heads(fetch, body, leave=None):
-    if fetch is not None:
+def over_heads(fetch, body, leave=None, started=False):
+    if fetch is not None and not started:
         for head in range(HL):
             fetch.start(head)
 
@@ -178,7 +181,7 @@
 
 def within_kernel(
     cum_rows_ref, queries_ref, keys_ref, values_ref,
-    cum_ref, within_ref, scaled_queries_ref, scaled_keys_ref, done_ref,
+    within_ref, scaled_keys_ref, done_ref,
     queries_buf, keys_buf, values_buf, within_buf, scaled_queries_buf, scaled_keys_buf,
     in_sems, out_sems,
 ):
@@ -193,19 +196,11 @@
     leave = Copies(
         [
             (of_lead(within_buf), of_lead(within_ref)),
-            (of_lead(scaled_queries_buf), of_lead(scaled_queries_ref)),
+            (of_lead(scaled_queries_buf), of_lead(within_ref, first=HL)),
             (of_lead(scaled_keys_buf), of_lead(scaled_keys_ref)),
         ],
         out_sems,
     )
-    for head in range(HL):
-        fetch.start(head)
-    for tile in range(TILES):
-        part = tile_rows(tile)
-        padded = jnp.concatenate(
-            [cum_rows_ref[:, part], jnp.zeros((HD - HL, HD), F32)], axis=0
-        )
-        cum_ref[part, :] = padded.T
     done_ref[...] = jnp.zeros_like(done_ref)
     row_ids = lax.broadcasted_iota(jnp.int32, (BLK, BLK), 0)
     col_ids = lax.broadcasted_iota(jnp.int32, (BLK, BLK), 1)
@@ -215,25 +210,17 @@
             part = rows(number)
             queries = queries_buf[head, part, :]
             keys = keys_buf[head, part, :]
-            col = column(cum_ref, number, head)
-            gaps = col - cum_rows_ref[pl.ds(head, 1), part]
+            row = cum_rows_ref[pl.ds(head, 1), part]
+            gaps = twice(down(row)) - row
             mask = jnp.where(row_ids >= col_ids, jnp.exp(gaps), 0.0)
             weights = (mm_nt(queries, keys) * mask).astype(BF16)
-            within_buf[head, part, :] = mm(weights, values_buf[head, part, :])
-            scaled_queries_buf[head, part, :] = rounded_product(queries, jnp.exp(col))
+            within_buf[head, part, :] = mm(weights, values_buf[head, part, :]).astype(BF16)
+            scaled_queries_buf[head, part, :] = rounded_product(queries, down(jnp.exp(row)))
             if number < 2:
-                factor = jnp.exp(col[BLK - 1 : BLK, :] - col)
+                factor = down(jnp.exp(row[:, BLK - 1 : BLK] - row))
                 scaled_keys_buf[head, part, :] = rounded_product(keys, factor)
 
-    def step(head, carry):
-        fetch.wait(head)
-        body(head)
-        leave.start(head)
-        return carry
-
-    lax.fori_loop(0, HL, step, 0)
-    for head in range(HL):
-        leave.wait(head)
+    over_heads(fetch, body, leave)
 
 
 def forward_scan_kernel(parents_ref, got_ref, _after, send_ref, decay_ref):
@@ -250,13 +237,31 @@
     for index in range(N_SEQ):
         prompt = parents_ref[index] // SPAN
         chosen = jnp.where(prompt == 0, totals[0], totals[1])
+        decay_ref[N_SEQ + index : N_SEQ + index + 1, :] = jnp.full((1, HD), prompt, F32)
         send_ref[index, PIECE : 2 * PIECE, :] = chosen.astype(BF16)
 
 
 def attend_kernel(
-    ends_ref, gain_ref, queries_ref, d_out_ref, within_ref, starts_ref, term_ref,
-    attended_ref, second_ref, stats_ref, squares_ref, products_ref,
+    ends_ref, gain_ref, d_out_ref, starts_ref, term_ref, within_ref,
+    queries_ref, attended_ref, stats_ref, kept_ref, states_ref,
+    within_buf, states_buf, squares_ref, products_ref, in_sems, out_sems,
 ):
+    fetch = Copies(
+        [
+            (of_lead(within_ref, first=HL), of_lead(queries_ref)),
+            (of_lead(within_ref), of_lead(within_buf)),
+        ],
+        in_sems,
+    )
+    leave = Copies(
+        [
+            (of_lead(attended_ref), of_lead(kept_ref)),
+            (of_lead(states_buf, BLOCKS), of_lead(states_ref, BLOCKS)),
+        ],
+        out_sems,
+    )
+    for head in range(HL):
+        fetch.start(head)
     squares_ref[...] = jnp.zeros_like(squares_ref)
     products_ref[...] = jnp.zeros_like(products_ref)
 
@@ -266,17 +271,19 @@
         reply = got[:, PIECE : 2 * PIECE, :].reshape(HD, HD)
         end_decay = ends_ref[head][0:1, :]
         second = (end_decay * first.astype(F32) + term_ref[head]).astype(BF16)
-        second_ref[head] = second
         gain = gain_ref[pl.ds(head, 1), :]
         for number, start in enumerate((first, second, reply)):
             part = rows(number)
-            attended = within_ref[head, part, :] + mm(queries_ref[head, part, :], start)
-            attended_ref[head, part, :] = attended
+            states_buf[head * BLOCKS + number] = start
+            attended = within_buf[head, part, :].astype(F32) + mm(
+                queries_ref[head, part, :], start
+            )
+            attended_ref[head, part, :] = attended.astype(BF16)
             weighted = gain * d_out_ref[0, part, lanes(head)].astype(F32)
             squares_ref[part, :] += attended * attended
             products_ref[part, :] += weighted * attended
 
-    over_heads(None, body)
+    over_heads(fetch, body, leave, started=True)
     stats_ref[...] = jnp.zeros_like(stats_ref)
     for tile in range(TILES):
         for base, sums_ref in ((0, squares_ref), (8, products_ref)):
@@ -314,7 +321,7 @@
             weighted = gain * d_out_ref[0, part, lanes(head)].astype(F32)
             grad = (
                 inverse_ref[part, :] * weighted
-                - attended_ref[head, part, :] * slope_ref[part, :]
+                - attended_ref[head, part, :].astype(F32) * slope_ref[part, :]
             ).astype(BF16)
             terms.append(mm_tn(queries_ref[head, part, :], grad))
         local_sum = ends_ref[head][0:1, :] * terms[1] + terms[0]
@@ -327,10 +334,10 @@
     over_heads(None, body)
 
 
-def backward_scan_kernel(parents_ref, got_ref, decay_ref, _after, send_ref):
+def backward_scan_kernel(got_ref, decay_ref, _after, send_ref):
     branches = [jnp.zeros((PIECE, HD), F32) for _ in range(PROMPTS)]
     for index in range(N_SEQ):
-        prompt = parents_ref[index] // SPAN
+        prompt = decay_ref[N_SEQ + index : N_SEQ + index + 1, :]
         start_grad = got_ref[index, PIECE : 2 * PIECE, :].astype(F32)
         for each in range(PROMPTS):
             branches[each] = branches[each] + jnp.where(prompt == each, start_grad, 0.0)
@@ -342,11 +349,11 @@
 
 
 def local_grads_kernel(
-    cum_ref, cum_rows_ref, stats_ref, gain_ref,
-    queries_ref, keys_ref, values_ref, d_out_ref, attended_ref, starts_ref, second_ref,
-    out_ref, d_queries_ref, part_keys_ref, part_values_ref, d_keys_ref, d_values_ref, term_ref,
-    done_ref, queries_buf, keys_buf, values_buf, d_out_buf, attended_buf, starts_buf, second_buf,
-    out_buf, d_queries_buf, part_keys_buf, part_values_buf, d_keys_buf, d_values_buf, term_buf,
+    cum_rows_ref, stats_ref, gain_ref,
+    queries_ref, keys_ref, values_ref, d_out_ref, attended_ref, states_ref,
+    out_ref, d_queries_ref, d_keys_ref, d_values_ref, term_ref, done_ref,
+    queries_buf, keys_buf, values_buf, d_out_buf, attended_buf, states_buf,
+    out_buf, d_queries_buf, d_keys_buf, d_values_buf, term_buf,
     inverse_ref, slope_ref, in_sems, out_sems,
 ):
     fetch = Copies(
@@ -356,8 +363,7 @@
             (of_rows(queries_ref), of_lead(queries_buf)),
             (of_rows(keys_ref), of_lead(keys_buf)),
             (of_rows(values_ref), of_lead(values_buf)),
-            (of_lead(starts_ref, PARTS), of_lead(starts_buf, PARTS)),
-            (of_lead(second_ref), of_lead(second_buf)),
+            (of_lead(states_ref, BLOCKS), of_lead(states_buf, BLOCKS)),
         ],
         in_sems,
     )
@@ -365,10 +371,8 @@
         [
             (of_lead(out_buf), of_rows(out_ref)),
             (of_lead(d_queries_buf), of_rows(d_queries_ref)),
-            (of_lead(part_keys_buf), of_lead(part_keys_ref)),
-            (of_lead(part_values_buf), of_lead(part_values_ref)),
-            (of_lead(d_keys_buf), of_rows(d_keys_ref, BLK, P_DEV)),
-            (of_lead(d_values_buf), of_rows(d_values_ref, BLK, P_DEV)),
+            (of_lead(d_keys_buf), of_rows(d_keys_ref)),
+            (of_lead(d_values_buf), of_rows(d_values_ref)),
             (of_lead(term_buf), of_lead(term_ref)),
         ],
         out_sems,
@@ -381,55 +385,47 @@
     col_ids = lax.broadcasted_iota(jnp.int32, (BLK, BLK), 1)
 
     def body(head):
-        got = starts_buf[pl.ds(head * PARTS, PARTS)]
-        first = got[:, 0:PIECE, :].reshape(HD, HD)
-        reply = got[:, PIECE : 2 * PIECE, :].reshape(HD, HD)
         gain = gain_ref[pl.ds(head, 1), :]
-        for number, start in enumerate((first, second_buf[head], reply)):
+        for number in range(BLOCKS):
             part = rows(number)
             queries = queries_buf[head, part, :]
             keys = keys_buf[head, part, :]
             values = values_buf[head, part, :]
-            attended = attended_buf[head, part, :]
+            attended = attended_buf[head, part, :].astype(F32)
             inverse = inverse_ref[part, :]
             weighted = gain * d_out_buf[head, part, :].astype(F32)
             grad = (inverse * weighted - attended * slope_ref[part, :]).astype(BF16)
             out_buf[head, part, :] = (attended * inverse * gain).astype(BF16)
-            col = column(cum_ref, number, head)
-            gaps = cum_rows_ref[pl.ds(head, 1), part] - col
+            row = cum_rows_ref[pl.ds(head, 1), part]
+            gaps = row - twice(down(row))
             mask = jnp.where(col_ids >= row_ids, jnp.exp(gaps), 0.0)
             weights = (mm_nt(keys, queries) * mask).astype(BF16)
             score_grad = (mm_nt(values, grad) * mask).astype(BF16)
-            grad_values = mm(weights, grad)
-            grad_keys = mm(score_grad, queries)
-            growth = jnp.exp(col)
+            growth = down(jnp.exp(row))
+            start = states_buf[head * BLOCKS + number]
             grad_queries = mm_tn(score_grad, keys) + growth * mm_nt(grad, start)
             d_queries_buf[head, part, :] = grad_queries.astype(BF16)
             if number == 1:
                 term_buf[head] = mm_tn(rounded_product(queries, growth), grad)
-            if number < 2:
-                part_keys_buf[head, part, :] = grad_keys
-                part_values_buf[head, part, :] = grad_values
-            else:
-                d_keys_buf[head] = grad_keys.astype(BF16)
-                d_values_buf[head] = grad_values.astype(BF16)
-
-    def step(head, carry):
-        fetch.wait(head)
-        body(head)
-        leave.start(head)
-        return carry
-
-    lax.fori_loop(0, HL, step, 0)
-    for head in range(HL):
-        leave.wait(head)
+            d_keys_buf[head, part, :] = mm(score_grad, queries).astype(BF16)
+            d_values_buf[head, part, :] = mm(weights, grad).astype(BF16)
+
+    over_heads(fetch, body, leave, started=True)
 
 
 def far_grads_kernel(
-    cum_ref, ends_ref, far_ref, term_ref, scaled_keys_ref, values_ref,
-    part_keys_ref, part_values_ref, _k, _v,
-    d_keys_ref, d_values_ref, d_keys_buf, d_values_buf, out_sems,
+    cum_rows_ref, ends_ref, far_ref, scaled_keys_ref, values_ref, term_ref,
+    near_keys_ref, near_values_ref, d_keys_ref, d_values_ref,
+    term_buf, near_keys_buf, near_values_buf, d_keys_buf, d_values_buf, in_sems, out_sems,
 ):
+    fetch = Copies(
+        [
+            (of_lead(term_ref), of_lead(term_buf)),
+            (of_rows(near_keys_ref, P_DEV), of_lead(near_keys_buf)),
+            (of_rows(near_values_ref, P_DEV), of_lead(near_values_buf)),
+        ],
+        in_sems,
+    )
     leave = Copies(
         [
             (of_lead(d_keys_buf), of_rows(d_keys_ref, P_DEV)),
@@ -440,19 +436,21 @@
 
     def body(head):
         second = far_ref[pl.ds(head * PARTS, PARTS)].reshape(HD, HD)
-        first = (ends_ref[head][1:2, :] * second.astype(F32) + term_ref[head]).astype(BF16)
+        first = (ends_ref[head][1:2, :] * second.astype(F32) + term_buf[head]).astype(BF16)
         for number, end_grad in enumerate((first, second)):
             part = rows(number)
-            col = column(cum_ref, number, head)
-            factor = jnp.exp(col[BLK - 1 : BLK, :] - col)
-            grad_values = part_values_ref[head, part, :] + mm(scaled_keys_ref[head, part, :], end_grad)
-            grad_keys = part_keys_ref[head, part, :] + factor * mm_nt(
+            row = cum_rows_ref[pl.ds(head, 1), part]
+            factor = down(jnp.exp(row[:, BLK - 1 : BLK] - row))
+            grad_values = near_values_buf[head, part, :].astype(F32) + mm(
+                scaled_keys_ref[head, part, :], end_grad
+            )
+            grad_keys = near_keys_buf[head, part, :].astype(F32) + factor * mm_nt(
                 values_ref[0, part, lanes(head)], end_grad
             )
             d_values_buf[head, part, :] = grad_values.astype(BF16)
             d_keys_buf[head, part, :] = grad_keys.astype(BF16)
 
-    over_heads(None, body, leave)
+    over_heads(fetch, body, leave)
 
 
 def shape(dims, kind):
@@ -471,6 +469,7 @@
 TWO_PIECES = (N_SEQ, 2 * PIECE, HD)
 SENT_PIECES = (N_SEQ, PIECE + 16, HD)
 CUM = (ROWS, HD)
+FAR = 160
 
 
 def call(kernel, name, in_specs, outs, scratch, semaphores, mib, flops, moved, aliases=None):
@@ -505,31 +504,32 @@
     return call(
         within_kernel, "within", [VMEM] + [HBM] * 3,
         [
-            (VMEM, shape(CUM, F32)), (HBM, shape(HEAD_ROWS, F32)), (HBM, shape(HEAD_ROWS, BF16)),
-            (HBM, shape(HEAD_PROMPT, BF16)), (VMEM, shape((8, HD), F32)),
-        ],
-        [(HEAD_ROWS, BF16)] * 3 + [(HEAD_ROWS, F32), (HEAD_ROWS, BF16), (HEAD_PROMPT, BF16)],
-        [3, 3], 56, 4e9, 16,
+            (HBM, shape((FAR, ROWS, HD), BF16)), (HBM, shape(HEAD_PROMPT, BF16)),
+            (VMEM, shape((8, HD), F32)),
+        ],
+        [(HEAD_ROWS, BF16)] * 5 + [(HEAD_PROMPT, BF16)], [3, 3], 52, 4e9, 16,
     )(cum_rows, queries, keys, values)
 
 
 def forward_scan(parents, got, after):
     return call(
         forward_scan_kernel, "forward_scan", [SMEM, VMEM, HBM],
-        [(VMEM, shape(TWO_PIECES, BF16)), (VMEM, shape((N_SEQ, HD), F32))],
+        [(VMEM, shape(TWO_PIECES, BF16)), (VMEM, shape((2 * N_SEQ, HD), F32))],
         [], [], 12, 1e6, 1,
     )(parents, got, after)
 
 
-def attend(ends, gains, scaled_queries, d_out, within, starts, term):
-    return call(
-        attend_kernel, "attend", [VMEM] * 7,
-        [
-            (VMEM, shape(HEAD_ROWS, F32)), (VMEM, shape(STATE, BF16)),
-            (VMEM, shape((HL, 16, HD), F32)),
-        ],
-        [(CUM, F32), (CUM, F32)], [], 20, 3e8, 10,
-    )(ends, gains, scaled_queries, d_out, within, starts, term)
+def attend(ends, gains, d_out, starts, term, within):
+    return call(
+        attend_kernel, "attend", [VMEM] * 5 + [HBM],
+        [
+            (VMEM, shape(HEAD_ROWS, BF16)), (VMEM, shape(HEAD_ROWS, BF16)),
+            (VMEM, shape((HL, 16, HD), F32)), (HBM, shape((FAR, ROWS, HD), BF16)),
+            (HBM, shape((6 * FAR, HD, HD), BF16)),
+        ],
+        [(HEAD_ROWS, BF16), ((HL * BLOCKS, HD, HD), BF16), (CUM, F32), (CUM, F32)],
+        [2, 2], 36, 3e8, 10,
+    )(ends, gains, d_out, starts, term, within)
 
 
 def grads(ends, gains, stats, scaled_queries, d_out, attended):
@@ -539,36 +539,32 @@
     )(ends, gains, stats, scaled_queries, d_out, attended)[0]
 
 
-def local_grads(
-    cum, cum_rows, stats, gains, queries, keys, values, d_out, attended, starts, second
-):
-    return call(
-        local_grads_kernel, "local_grads", [VMEM] * 4 + [HBM] * 7,
-        [
-            (HBM, WIDE), (HBM, WIDE), (HBM, shape(HEAD_PROMPT, F32)),
-            (HBM, shape(HEAD_PROMPT, F32)), (HBM, WIDE), (HBM, WIDE), (HBM, shape(STATE, F32)),
-            (VMEM, shape((8, HD), F32)),
-        ],
-        [(HEAD_ROWS, BF16)] * 4 + [(HEAD_ROWS, F32), (TWO_PIECES, BF16), (STATE, BF16)]
-        + [(HEAD_ROWS, BF16)] * 2 + [(HEAD_PROMPT, F32)] * 2 + [(HEAD_REPLY, BF16)] * 2
+def local_grads(cum_rows, stats, gains, queries, keys, values, d_out, attended, states):
+    return call(
+        local_grads_kernel, "local_grads", [VMEM] * 3 + [HBM] * 6,
+        [
+            (HBM, WIDE), (HBM, WIDE), (HBM, WIDE), (HBM, WIDE),
+            (HBM, shape((4 * FAR, HD, HD), F32)), (VMEM, shape((8, HD), F32)),
+        ],
+        [(HEAD_ROWS, BF16)] * 5 + [((HL * BLOCKS, HD, HD), BF16)] + [(HEAD_ROWS, BF16)] * 4
         + [(STATE, F32), (CUM, F32), (CUM, F32)],
-        [7, 7], 56, 6e9, 24,
-    )(cum, cum_rows, stats, gains, queries, keys, values, d_out, attended, starts, second)
-
-
-def far_grads(cum, ends, far, term, scaled_keys, values, part_keys, part_values, d_keys, d_values):
-    return call(
-        far_grads_kernel, "far_grads", [VMEM] * 8 + [HBM] * 2,
+        [6, 5], 53, 6e9, 24,
+    )(cum_rows, stats, gains, queries, keys, values, d_out, attended, states)
+
+
+def far_grads(cum_rows, ends, far, scaled_keys, values, term, near_keys, near_values):
+    return call(
+        far_grads_kernel, "far_grads", [VMEM] * 5 + [HBM] * 3,
         [(HBM, WIDE), (HBM, WIDE)],
-        [(HEAD_PROMPT, BF16), (HEAD_PROMPT, BF16)], [2], 24, 3e8, 10, {8: 0, 9: 1},
-    )(cum, ends, far, term, scaled_keys, values, part_keys, part_values, d_keys, d_values)
-
-
-def backward_scan(parents, got, decays, after):
-    return call(
-        backward_scan_kernel, "backward_scan", [SMEM, VMEM, VMEM, HBM],
+        [(STATE, F32)] + [(HEAD_PROMPT, BF16)] * 4, [3, 2], 36, 3e8, 10, {6: 0, 7: 1},
+    )(cum_rows, ends, far, scaled_keys, values, term, near_keys, near_values)
+
+
+def backward_scan(got, decays, after):
+    return call(
+        backward_scan_kernel, "backward_scan", [VMEM, VMEM, HBM],
         [(VMEM, shape(PIECES, BF16))], [], [], 12, 1e6, 1,
-    )(parents, got, decays, after)[0]
+    )(got, decays, after)[0]
 
 
 def everyone(array, axis):
@@ -580,22 +576,21 @@
     decay_rows = jnp.swapaxes(log_decay, 1, 2)
     send, first_term, cum_rows, block_ends = summarize(decay_rows, keys, values)
     got = everyone(send, "seq")
-    cum, within, scaled_queries, scaled_keys, done = inside(cum_rows, queries, keys, values)
+    within, scaled_keys, done = inside(cum_rows, queries, keys, values)
     send, decays = forward_scan(parents, got, done)
     starts = everyone(send, "seq")
-    attended, second, stats = attend(
-        block_ends, gains, scaled_queries, d_out, within, starts, first_term
+    near_queries, attended, stats, kept, states = attend(
+        block_ends, gains, d_out, starts, first_term, within
     )
     stats = everyone(stats, "head")
-    send = grads(block_ends, gains, stats, scaled_queries, d_out, attended)
+    send = grads(block_ends, gains, stats, near_queries, d_out, attended)
     got = everyone(send, "seq")
-    out, d_queries, part_keys, part_values, d_keys, d_values, last_term, done = local_grads(
-        cum, cum_rows, stats, gains, queries, keys, values, d_out, attended, starts, second
-    )
-    far = everyone(backward_scan(parents, got, decays, done), "seq")
+    out, d_queries, d_keys, d_values, last_term, done = local_grads(
+        cum_rows, stats, gains, queries, keys, values, d_out, kept, states
+    )
+    far = everyone(backward_scan(got, decays, done), "seq")
     d_keys, d_values = far_grads(
-        cum, block_ends, far, last_term, scaled_keys, values, part_keys, part_values,
-        d_keys, d_values,
+        cum_rows, block_ends, far, scaled_keys, values, last_term, d_keys, d_values
     )
     return (out, d_queries, d_keys, d_values)
 

time: 129 us -> 116 us (0.90)
  local copies, waits for them, and re-layouts: 14.2 us -> 1.74 us
    unnamed x46 -> x14, local copies, waits for them, and re-layouts: 14.2 us -> 1.74 us
where the time goes in v4:
time: 116 us; the launch traced here: 115 us
  blocking collectives  48.8 us (42%)
  Pallas kernels  38.4 us (33%)
  starting transfers between devices  16 us (14%)
  waiting for transfers between devices  9.56 us (8%)
  local copies, waits for them, and re-layouts  1.74 us (2%)
    all_to_all x3, blocking collectives, everyone(): return lax.all_to_all(array, axis, 0, 0, tiled=True)  48.8 us
    all_to_all x2, starting transfers between devices, everyone(): return lax.all_to_all(array, axis, 0, 0, tiled=True)  16 us
    pallas_call x1, Pallas kernels, local_grads(): call(local_grads_kernel, 'local_grads', [VMEM] * 3 + [HBM] * 6, [(HBM, WI...  13.4 us
    all_to_all x2, waiting for transfers between devices, everyone(): return lax.all_to_all(array, axis, 0, 0, tiled=True)  9.56 us
    pallas_call x1, Pallas kernels, inside(): call(within_kernel, 'within', [VMEM] + [HBM] * 3, [(HBM, shape((FAR, ROWS...  8.4 us
    pallas_call x1, Pallas kernels, attend(): call(attend_kernel, 'attend', [VMEM] * 5 + [HBM], [(VMEM, shape(HEAD_ROWS...  4.19 us
    pallas_call x1, Pallas kernels, far_grads(): call(far_grads_kernel, 'far_grads', [VMEM] * 5 + [HBM] * 3, [(HBM, WIDE),...  3.94 us
    pallas_call x1, Pallas kernels, summarize(): call(summary_kernel, 'summary', [VMEM, HBM, HBM], [(VMEM, shape(SENT_PIEC...  3.9 us
  transfers between devices with their start and end apart: 2, of which 2 were waited for; matrix products, arithmetic and copies ran while one was open for 0% of the time, Pallas kernels for 19%

profile of v4, /device:TPU:32, one launch (start us, length us, event | category | flops | bytes accessed | tf_op | source)
XLA Modules:
  0.0 115.3 jit_solution(12238998679378783139)
XLA Ops:
  0.6 0.0 copy-start.5
  0.6 0.7 copy-done.5
  1.4 3.9 %summary.1 = (bf16[32,48,128]{2,1,0:T(8,128)(2,1)}, f32[8,128,128]{2,1,0:T(8,128)S(1)}, f32[8,768]{1,0:T(8,128)S(1)}, f32[8,8,128]{2,1,0:T(8,128)S(1)}) custom-call(f32[1,8,768]{2,1,0:T(8,128)S(1)} %bitcast.5, bf16[1,768,1024]{2,1,0:T(8,128)(2,1)} %keys_ref.5, bf16[1,768,1024]{2,1,0:T(8,128)(2,1)} %values_ref.7), custom_call_target="tpu_custom_call" | custom-call | flops 300000000 | bytes 4194304 | tf_op jit(solution)/shard_map/summary/pallas_call | solution.py:493
  5.3 11.2 %all-to-all-start = ((bf16[32,48,128]{2,1,0:T(8,128)(2,1)}), bf16[32,48,128]{2,1,0:T(8,128)(2,1)S(1)}, u32[]{:S(2)}, u32[]{:S(2)}) async-start(bf16[32,48,128]{2,1,0:T(8,128)(2,1)} %get-tuple-element.28), calls=%async_computation | async-start | bytes 786432 | tf_op jit(solution)/shard_map/all_to_all | solution.py:571
  16.5 0.0 copy-start.6
  16.5 0.0 copy-start.1
  16.5 0.0 copy-start.4
  16.5 8.4 %within.1 = (bf16[160,768,128]{2,1,0:T(8,128)(2,1)}, bf16[8,512,128]{2,1,0:T(8,128)(2,1)S(1)}, f32[8,128]{1,0:T(8,128)S(1)}) custom-call(f32[8,768]{1,0:T(8,128)S(1)} %get-tuple-element.26.cum_rows_ref, bf16[1,768,1024]{2,1,0:T(8,128)(2,1)} %queries_ref.3, bf16[1,768,1024]{2,1,0:T(8,128)(2,1)} %keys_ref.5, bf16[1,768,1024]{2,1,0:T(8,128)(2,1)} %values_ref.7), custom_call_target="tpu_custom_call" | custom-call | flops 4000000000 | bytes 16777216 | tf_op jit(solution)/shard_map/within/pallas_call | solution.py:504
  24.9 0.0 copy-start.2
  24.9 1.0 copy-done.2
  25.9 5.5 %all-to-all-done.got_ref = bf16[32,48,128]{2,1,0:T(8,128)(2,1)S(1)} async-done(((bf16[32,48,128]{2,1,0:T(8,128)(2,1)}), bf16[32,48,128]{2,1,0:T(8,128)(2,1)S(1)}, u32[]{:S(2)}, u32[]{:S(2)}) %all-to-all-start) | async-done | bytes 393248 | tf_op jit(solution)/shard_map/all_to_all | solution.py:571
  31.4 0.0 copy-done.6
  31.4 0.7 forward_scan.1
  32.1 21.7 %all_to_all.25.starts_ref = bf16[32,64,128]{2,1,0:T(8,128)(2,1)S(1)} all-to-all(bf16[32,64,128]{2,1,0:T(8,128)(2,1)S(1)} %get-tuple-element.30), channel_id=1, replica_groups=mesh['seq'=32,'head'=8] {'seq'}, dimensions={0} | all-to-all | bytes 1048576 | tf_op jit(solution)/shard_map/all_to_all | solution.py:571
  53.8 0.0 copy-done.1
  53.8 0.0 copy-done.4
  53.8 4.2 %attend.1 = (bf16[8,768,128]{2,1,0:T(8,128)(2,1)S(1)}, bf16[8,768,128]{2,1,0:T(8,128)(2,1)S(1)}, f32[8,16,128]{2,1,0:T(8,128)S(1)}, bf16[160,768,128]{2,1,0:T(8,128)(2,1)}, bf16[960,128,128]{2,1,0:T(8,128)(2,1)}) custom-call(f32[8,8,128]{2,1,0:T(8,128)S(1)} %get-tuple-element.27.ends_ref, f32[8,128]{1,0:T(8,128)S(1)} %bitcast.2, ...), custom_call_target="tpu_custom_call" | custom-call | flops 300000000 | bytes 10485760 | tf_op jit(solution)/shard_map/attend/pallas_call | solution.py:523
  58.0 9.9 %all_to_all.26.stats_ref = f32[8,16,128]{2,1,0:T(8,128)S(1)} all-to-all(f32[8,16,128]{2,1,0:T(8,128)S(1)} %get-tuple-element.33), channel_id=1, replica_groups=mesh['seq'=32,'head'=8] {'head'}, dimensions={0} | all-to-all | bytes 131072 | tf_op jit(solution)/shard_map/all_to_all | solution.py:571
  67.9 3.6 %grad.1 = bf16[32,64,128]{2,1,0:T(8,128)(2,1)} custom-call(f32[8,8,128]{2,1,0:T(8,128)S(1)} %get-tuple-element.27.ends_ref, f32[8,128]{1,0:T(8,128)S(1)} %bitcast.3, f32[8,16,128]{2,1,0:T(8,128)S(1)} %all_to_all.26.stats_ref, bf16[8,768,128]{2,1,0:T(8,128)(2,1)S(1)} %get-tuple-element.38.queries_ref, bf16[1,768,1024]{2,1,0:T(8,128)(2,1)S(1)} %copy-done.1, ...), custom_call_target="tpu_custom_call" | custom-call | flops 300000000 | bytes 10485760 | tf_op jit(solution)/shard_map/grad/pallas_call | solution.py:536
  71.5 4.8 %all-to-all-start.3 = ((bf16[32,64,128]{2,1,0:T(8,128)(2,1)}), bf16[32,64,128]{2,1,0:T(8,128)(2,1)S(1)}, u32[]{:S(2)}, u32[]{:S(2)}) async-start(bf16[32,64,128]{2,1,0:T(8,128)(2,1)} %grad.1), calls=%async_computation.3 | async-start | bytes 1048576 | tf_op jit(solution)/shard_map/all_to_all | solution.py:571
  76.3 0.0 copy-start
  76.3 13.4 %local_grads.1 = (bf16[1,768,1024]{2,1,0:T(8,128)(2,1)}, bf16[1,768,1024]{2,1,0:T(8,128)(2,1)}, bf16[1,768,1024]{2,1,0:T(8,128)(2,1)}, bf16[1,768,1024]{2,1,0:T(...) custom-call(f32[8,768]{1,0:T(8,128)S(1)} %get-tuple-element.26.cum_rows_ref, ...), custom_call_target="tpu_custom_call" | custom-call | flops 6000000000 | bytes 25165824 | tf_op jit(solution)/shard_map/local_grads/pallas_call | solution.py:543
  89.7 0.0 copy-start.3
  89.7 4.1 %all-to-all-done.3.got_ref = bf16[32,64,128]{2,1,0:T(8,128)(2,1)S(1)} async-done(((bf16[32,64,128]{2,1,0:T(8,128)(2,1)}), bf16[32,64,128]{2,1,0:T(8,128)(2,1)S(1)}, u32[]{:S(2)}, u32[]{:S(2)}) %all-to-all-start.3) | async-done | bytes 524320 | tf_op jit(solution)/shard_map/all_to_all | solution.py:571
  93.8 0.2 backward_scan.1
  94.1 17.2 %all_to_all.27.far_ref = bf16[32,32,128]{2,1,0:T(8,128)(2,1)S(1)} all-to-all(bf16[32,32,128]{2,1,0:T(8,128)(2,1)S(1)} %backward_scan.1), channel_id=1, replica_groups=mesh['seq'=32,'head'=8] {'seq'}, dimensions={0} | all-to-all | bytes 524288 | tf_op jit(solution)/shard_map/all_to_all | solution.py:571
  111.3 0.0 copy-done
  111.3 0.0 copy-done.3
  111.3 3.9 %far_grads.1 = (bf16[1,768,1024]{2,1,0:T(8,128)(2,1)}, bf16[1,768,1024]{2,1,0:T(8,128)(2,1)}) custom-call(f32[8,768]{1,0:T(8,128)S(1)} %get-tuple-element.26.cum_rows_ref, f32[8,8,128]{2,1,0:T(8,128)S(1)} %get-tuple-element.27.ends_ref, bf16[32,32,128]{2,1,0:T(8,128)(2,1)S(1)} %all_to_all.27.far_ref, ...), custom_call_target="tpu_custom_call", output_to_operand_aliasing={{0}: (6, {}), {1}: (7, {})} | custom-call | flops 300000000 | bytes 10485760 | tf_op jit(solution)/shard_map/far_grads/pallas_call | solution.py:556
Async XLA Ops:
  0.6 0.7 copy-start.5
  5.3 26.1 %all-to-all-start = ((bf16[32,48,128]{2,1,0:T(8,128)(2,1)}), bf16[32,48,128]{2,1,0:T(8,128)(2,1)S(1)}, u32[]{:S(2)}, u32[]{:S(2)}) async-start(bf16[32,48,128]{2,1,0:T(8,128)(2,1)} %get-tuple-element.28), calls=%async_computation | async-start | bytes 786432 | tf_op jit(solution)/shard_map/all_to_all | solution.py:571
  16.5 14.9 %copy-start.6 = (s32[32]{0:T(128)S(1)}, s32[32]{0:T(128)}, u32[]{:S(2)}) copy-start(s32[32]{0:T(128)} %parents_ref.1) | copy-start | bytes 388
  16.5 37.3 %copy-start.1 = (bf16[1,768,1024]{2,1,0:T(8,128)(2,1)S(1)}, bf16[1,768,1024]{2,1,0:T(8,128)(2,1)}, u32[]{:S(2)}) copy-start(bf16[1,768,1024]{2,1,0:T(8,128)(2,1)} %d_out_ref.5) | copy-start | bytes 4718596
  16.5 37.3 %copy-start.4 = (f32[1024]{0:T(1024)S(1)}, f32[1024]{0:T(1024)}, u32[]{:S(2)}) copy-start(f32[1024]{0:T(1024)} %param.11) | copy-start | bytes 12292
  24.9 1.0 copy-start.2
  71.5 22.4 %all-to-all-start.3 = ((bf16[32,64,128]{2,1,0:T(8,128)(2,1)}), bf16[32,64,128]{2,1,0:T(8,128)(2,1)S(1)}, u32[]{:S(2)}, u32[]{:S(2)}) async-start(bf16[32,64,128]{2,1,0:T(8,128)(2,1)} %grad.1), calls=%async_computation.3 | async-start | bytes 1048576 | tf_op jit(solution)/shard_map/all_to_all | solution.py:571
  76.3 35.0 %copy-start = (bf16[1,768,1024]{2,1,0:T(8,128)(2,1)S(1)}, bf16[1,768,1024]{2,1,0:T(8,128)(2,1)}, u32[]{:S(2)}) copy-start(bf16[1,768,1024]{2,1,0:T(8,128)(2,1)} %values_ref.7) | copy-start | bytes 4718596
  89.7 21.6 %copy-start.3 = (bf16[8,512,128]{2,1,0:T(8,128)(2,1)S(1)}, bf16[8,512,128]{2,1,0:T(8,128)(2,1)}, u32[]{:S(2)}) copy-start(bf16[8,512,128]{2,1,0:T(8,128)(2,1)} %copy-done.2) | copy-start | bytes 3145732

commit v5 on v4

--- a/solution.py
+++ b/solution.py
@@ -1,3 +1,5 @@
+import functools
+
 import jax
 import jax.numpy as jnp
 from jax import lax
@@ -15,8 +17,9 @@
 N_SEQ = 32
 SPAN = N_SEQ // PROMPTS
 COLS = HL * HD
-PIECE = HL * HD // N_SEQ
-PARTS = HD // PIECE
+RING = 8
+RINGS = N_SEQ // RING
+PACK = 16
 BLOCKS = ROWS // BLK
 TILES = ROWS // HD
 EPS = 1e-05
@@ -75,6 +78,10 @@
     if count == 1:
         return lambda head: ref.at[head + first]
     return lambda head: ref.at[pl.ds(head * count, count)]
+
+
+def of_head_rows(ref, count, first):
+    return lambda head: ref.at[head, pl.ds(first, count)]
 
 
 class Copies:
@@ -122,6 +129,19 @@
     return coarse, middle, (rest - middle.astype(F32)).astype(BF16)
 
 
+def packed(decay):
+    coarse, middle, _ = split(jnp.broadcast_to(decay, (PACK, HD)))
+    row_ids = lax.broadcasted_iota(jnp.int32, (PACK, HD), 0)
+    return jnp.where(
+        row_ids == 0, coarse.astype(F32), jnp.where(row_ids == 1, middle.astype(F32), 0.0)
+    ).astype(BF16)
+
+
+def unpacked(block):
+    both = block.astype(F32)
+    return both[0:1, :] + both[1:2, :]
+
+
 def summary_kernel(
     decay_ref, keys_ref, values_ref,
     send_ref, term_ref, cum_rows_ref, ends_ref,
@@ -148,7 +168,6 @@
         total = cumulative[number * HL : (number + 1) * HL]
         cum_rows_ref[:, rows(number)] = total
         ends_ref[:, number, :] = jnp.broadcast_to(jnp.exp(total[:, BLK - 1 : BLK]), (HL, HD))
-    row_ids = lax.broadcasted_iota(jnp.int32, (16, HD), 0)
 
     def body(head):
         terms = []
@@ -161,15 +180,9 @@
         term_ref[head] = terms[0]
         end_decays = ends_ref[head]
         summary = end_decays[1:2, :] * terms[0] + terms[1]
-        decay = jnp.broadcast_to(end_decays[0:1, :] * end_decays[1:2, :], (16, HD))
-        coarse, middle, _ = split(decay)
-        packed = jnp.where(
-            row_ids == 0, coarse.astype(F32), jnp.where(row_ids == 1, middle.astype(F32), 0.0)
-        ).astype(BF16)
-        for piece in range(PARTS):
-            at = head * PARTS + piece
-            send_ref[at, 0:PIECE, :] = summary[piece * PIECE : (piece + 1) * PIECE].astype(BF16)
-            send_ref[at, PIECE : PIECE + 16, :] = packed
+        decay = end_decays[0:1, :] * end_decays[1:2, :]
+        send_ref[head, 0:HD, :] = summary.astype(BF16)
+        send_ref[head, HD : HD + PACK, :] = packed(decay)
 
     def step(head, carry):
         fetch.wait(head)
@@ -223,22 +236,46 @@
     over_heads(fetch, body, leave)
 
 
-def forward_scan_kernel(parents_ref, got_ref, _after, send_ref, decay_ref):
-    totals = []
-    for prompt in range(PROMPTS):
-        carry = jnp.zeros((PIECE, HD), F32)
-        for index in range(prompt * SPAN, (prompt + 1) * SPAN):
-            packed = got_ref[index, PIECE : PIECE + 16, :].astype(F32)
-            decay = packed[0:1, :] + packed[1:2, :]
-            decay_ref[index : index + 1, :] = decay
-            send_ref[index, 0:PIECE, :] = carry.astype(BF16)
-            carry = decay * carry + got_ref[index, 0:PIECE, :].astype(F32)
-        totals.append(carry)
-    for index in range(N_SEQ):
-        prompt = parents_ref[index] // SPAN
-        chosen = jnp.where(prompt == 0, totals[0], totals[1])
-        decay_ref[N_SEQ + index : N_SEQ + index + 1, :] = jnp.full((1, HD), prompt, F32)
-        send_ref[index, PIECE : 2 * PIECE, :] = chosen.astype(BF16)
+def ring_place():
+    ring = lax.axis_index("seq") // RING
+    return ring, ring % 2 == 1, ring // 2
+
+
+def ring_prefix_kernel(got_ref, _after, part_ref, decay_ref, send_ref):
+    carry = jnp.zeros((HD, HD), F32)
+    before = jnp.ones((1, HD), F32)
+    for place in range(RING):
+        decay = unpacked(got_ref[place, HD : HD + PACK, :])
+        decay_ref[place : place + 1, :] = decay
+        decay_ref[RING + place : RING + place + 1, :] = before
+        part_ref[place] = carry
+        carry = decay * carry + got_ref[place, 0:HD, :].astype(F32)
+        before = before * decay
+    part_ref[RING] = carry
+    decay_ref[2 * RING : 3 * RING, :] = jnp.broadcast_to(before, (RING, HD))
+    send_ref[0:HD, :] = carry.astype(BF16)
+    send_ref[HD : HD + PACK, :] = packed(before)
+
+
+def ring_starts_kernel(
+    parents_ref, part_ref, decay_ref, mate_ref, same_ref, cross_ref, send_ref, mate_decay_ref
+):
+    ring, upper, prompt = ring_place()
+    own, own_decay = part_ref[RING], decay_ref[2 * RING : 2 * RING + 1, :]
+    (mate, mate_decay), (same, same_decay), (cross, cross_decay) = (
+        (ref[0:HD, :].astype(F32), unpacked(ref[HD : HD + PACK, :]))
+        for ref in (mate_ref, same_ref, cross_ref)
+    )
+    mate_decay_ref[...] = jnp.broadcast_to(mate_decay, mate_decay_ref.shape)
+    here = jnp.where(upper, own_decay * mate + own, mate_decay * own + mate)
+    there = jnp.where(upper, same_decay * cross + same, cross_decay * same + cross)
+    totals = (jnp.where(prompt == 0, here, there), jnp.where(prompt == 0, there, here))
+    carry = jnp.where(upper, mate, 0.0)
+    for place in range(RING):
+        start = decay_ref[RING + place : RING + place + 1, :] * carry + part_ref[place]
+        parent = parents_ref[ring * RING + place] // SPAN
+        send_ref[place, 0:HD, :] = start.astype(BF16)
+        send_ref[place, HD : 2 * HD, :] = jnp.where(parent == 0, totals[0], totals[1]).astype(BF16)
 
 
 def attend_kernel(
@@ -266,9 +303,8 @@
     products_ref[...] = jnp.zeros_like(products_ref)
 
     def body(head):
-        got = starts_ref[pl.ds(head * PARTS, PARTS)]
-        first = got[:, 0:PIECE, :].reshape(HD, HD)
-        reply = got[:, PIECE : 2 * PIECE, :].reshape(HD, HD)
+        first = starts_ref[head, 0:HD, :]
+        reply = starts_ref[head, HD : 2 * HD, :]
         end_decay = ends_ref[head][0:1, :]
         second = (end_decay * first.astype(F32) + term_ref[head]).astype(BF16)
         gain = gain_ref[pl.ds(head, 1), :]
@@ -325,58 +361,85 @@
             ).astype(BF16)
             terms.append(mm_tn(queries_ref[head, part, :], grad))
         local_sum = ends_ref[head][0:1, :] * terms[1] + terms[0]
-        for piece in range(PARTS):
-            at = head * PARTS + piece
-            part = slice(piece * PIECE, (piece + 1) * PIECE)
-            send_ref[at, 0:PIECE, :] = local_sum[part].astype(BF16)
-            send_ref[at, PIECE : 2 * PIECE, :] = terms[2][part].astype(BF16)
+        send_ref[head, 0:HD, :] = local_sum.astype(BF16)
+        send_ref[head, HD : 2 * HD, :] = terms[2].astype(BF16)
 
     over_heads(None, body)
 
 
-def backward_scan_kernel(got_ref, decay_ref, _after, send_ref):
-    branches = [jnp.zeros((PIECE, HD), F32) for _ in range(PROMPTS)]
-    for index in range(N_SEQ):
-        prompt = decay_ref[N_SEQ + index : N_SEQ + index + 1, :]
-        start_grad = got_ref[index, PIECE : 2 * PIECE, :].astype(F32)
-        for each in range(PROMPTS):
-            branches[each] = branches[each] + jnp.where(prompt == each, start_grad, 0.0)
-    for prompt in range(PROMPTS):
-        carry = branches[prompt]
-        for index in reversed(range(prompt * SPAN, (prompt + 1) * SPAN)):
-            send_ref[index] = carry.astype(BF16)
-            carry = decay_ref[index : index + 1, :] * carry + got_ref[index, 0:PIECE, :].astype(F32)
+def ring_suffix_kernel(
+    parents_ref, got_ref, decay_ref, _after, part_ref, later_ref, mate_send_ref, far_send_ref
+):
+    ring, _, prompt = ring_place()
+    carry = jnp.zeros((HD, HD), F32)
+    after = jnp.ones((1, HD), F32)
+    mine = jnp.zeros((HD, HD), F32)
+    theirs = jnp.zeros((HD, HD), F32)
+    for place in reversed(range(RING)):
+        decay = decay_ref[place : place + 1, :]
+        part_ref[place] = carry
+        later_ref[place : place + 1, :] = after
+        carry = decay * carry + got_ref[place, 0:HD, :].astype(F32)
+        after = after * decay
+        start_grad = got_ref[place, HD : 2 * HD, :].astype(F32)
+        ours = parents_ref[ring * RING + place] // SPAN == prompt
+        mine = mine + jnp.where(ours, start_grad, 0.0)
+        theirs = theirs + jnp.where(ours, 0.0, start_grad)
+    part_ref[RING] = mine
+    mate_send_ref[0:HD, :] = carry.astype(BF16)
+    mate_send_ref[HD : 2 * HD, :] = mine.astype(BF16)
+    far_send_ref[...] = theirs.astype(BF16)
+
+
+def ring_ends_kernel(
+    part_ref, later_ref, mate_decay_ref, mate_ref, same_ref, cross_ref, _after, send_ref
+):
+    _, upper, _ = ring_place()
+    branch = (
+        part_ref[RING]
+        + mate_ref[HD : 2 * HD, :].astype(F32)
+        + (same_ref[...].astype(F32) + cross_ref[...].astype(F32))
+    )
+    above = mate_decay_ref[0:1, :] * branch + mate_ref[0:HD, :].astype(F32)
+    carry = jnp.where(upper, branch, above)
+    for place in range(RING):
+        send_ref[place] = (later_ref[place : place + 1, :] * carry + part_ref[place]).astype(BF16)
 
 
 def local_grads_kernel(
-    cum_rows_ref, stats_ref, gain_ref,
-    queries_ref, keys_ref, values_ref, d_out_ref, attended_ref, states_ref,
-    out_ref, d_queries_ref, d_keys_ref, d_values_ref, term_ref, done_ref,
-    queries_buf, keys_buf, values_buf, d_out_buf, attended_buf, states_buf,
-    out_buf, d_queries_buf, d_keys_buf, d_values_buf, term_buf,
-    inverse_ref, slope_ref, in_sems, out_sems,
-):
+    blocks, cum_rows_ref, stats_ref, gain_ref,
+    queries_ref, keys_ref, values_ref, d_out_ref, attended_ref, states_ref, *refs
+):
+    first, count = blocks[0] * BLK, len(blocks) * BLK
+    if first:
+        refs = refs[4:]
+    out_ref, d_queries_ref, d_keys_ref, d_values_ref = refs[:4]
+    term_ref = None if first else refs[4]
+    (
+        done_ref, queries_buf, keys_buf, values_buf, d_out_buf, attended_buf, states_buf,
+        out_buf, d_queries_buf, d_keys_buf, d_values_buf, term_buf,
+        inverse_ref, slope_ref, in_sems, out_sems,
+    ) = refs[-16:]
     fetch = Copies(
         [
-            (of_rows(d_out_ref), of_lead(d_out_buf)),
-            (of_lead(attended_ref), of_lead(attended_buf)),
-            (of_rows(queries_ref), of_lead(queries_buf)),
-            (of_rows(keys_ref), of_lead(keys_buf)),
-            (of_rows(values_ref), of_lead(values_buf)),
+            (of_rows(d_out_ref, count, first), of_lead(d_out_buf)),
+            (of_head_rows(attended_ref, count, first), of_lead(attended_buf)),
+            (of_rows(queries_ref, count, first), of_lead(queries_buf)),
+            (of_rows(keys_ref, count, first), of_lead(keys_buf)),
+            (of_rows(values_ref, count, first), of_lead(values_buf)),
             (of_lead(states_ref, BLOCKS), of_lead(states_buf, BLOCKS)),
         ],
         in_sems,
     )
-    leave = Copies(
-        [
-            (of_lead(out_buf), of_rows(out_ref)),
-            (of_lead(d_queries_buf), of_rows(d_queries_ref)),
-            (of_lead(d_keys_buf), of_rows(d_keys_ref)),
-            (of_lead(d_values_buf), of_rows(d_values_ref)),
-            (of_lead(term_buf), of_lead(term_ref)),
-        ],
-        out_sems,
-    )
+    leaving = [
+        (of_lead(out_buf), of_rows(out_ref, count, first)),
+        (of_lead(d_queries_buf), of_rows(d_queries_ref, count, first)),
+        (of_lead(d_keys_buf), of_rows(d_keys_ref, count, first)),
+        (of_lead(d_values_buf), of_rows(d_values_ref, count, first)),
+    ]
+    if not first:
+        leaving.append((of_lead(term_buf), of_lead(term_ref)))
+    leave = Copies(leaving, out_sems)
     for head in range(HL):
         fetch.start(head)
     done_ref[...] = jnp.zeros_like(done_ref)
@@ -386,17 +449,18 @@
 
     def body(head):
         gain = gain_ref[pl.ds(head, 1), :]
-        for number in range(BLOCKS):
-            part = rows(number)
+        for number in blocks:
+            part = rows(number - blocks[0])
+            whole = rows(number)
             queries = queries_buf[head, part, :]
             keys = keys_buf[head, part, :]
             values = values_buf[head, part, :]
             attended = attended_buf[head, part, :].astype(F32)
-            inverse = inverse_ref[part, :]
+            inverse = inverse_ref[whole, :]
             weighted = gain * d_out_buf[head, part, :].astype(F32)
-            grad = (inverse * weighted - attended * slope_ref[part, :]).astype(BF16)
+            grad = (inverse * weighted - attended * slope_ref[whole, :]).astype(BF16)
             out_buf[head, part, :] = (attended * inverse * gain).astype(BF16)
-            row = cum_rows_ref[pl.ds(head, 1), part]
+            row = cum_rows_ref[pl.ds(head, 1), whole]
             gaps = row - twice(down(row))
             mask = jnp.where(col_ids >= row_ids, jnp.exp(gaps), 0.0)
             weights = (mm_nt(keys, queries) * mask).astype(BF16)
@@ -435,7 +499,7 @@
     )
 
     def body(head):
-        second = far_ref[pl.ds(head * PARTS, PARTS)].reshape(HD, HD)
+        second = far_ref[head]
         first = (ends_ref[head][1:2, :] * second.astype(F32) + term_buf[head]).astype(BF16)
         for number, end_grad in enumerate((first, second)):
             part = rows(number)
@@ -465,9 +529,9 @@
 HEAD_PROMPT = (HL, P_DEV, HD)
 HEAD_REPLY = (HL, BLK, HD)
 STATE = (HL, HD, HD)
-PIECES = (N_SEQ, PIECE, HD)
-TWO_PIECES = (N_SEQ, 2 * PIECE, HD)
-SENT_PIECES = (N_SEQ, PIECE + 16, HD)
+TWO_STATES = (HL, 2 * HD, HD)
+SENT_STATE = (HL, HD + PACK, HD)
+PART = (RING + 1, HD, HD)
 CUM = (ROWS, HD)
 FAR = 160
 
@@ -493,7 +557,7 @@
     return call(
         summary_kernel, "summary", [VMEM, HBM, HBM],
         [
-            (VMEM, shape(SENT_PIECES, BF16)), (VMEM, shape(STATE, F32)),
+            (VMEM, shape(SENT_STATE, BF16)), (VMEM, shape(STATE, F32)),
             (VMEM, shape((HL, ROWS), F32)), (VMEM, shape((HL, 8, HD), F32)),
         ],
         [(HEAD_PROMPT, BF16), (HEAD_PROMPT, BF16)], [2], 52, 3e8, 4,
@@ -511,12 +575,41 @@
     )(cum_rows, queries, keys, values)
 
 
-def forward_scan(parents, got, after):
-    return call(
-        forward_scan_kernel, "forward_scan", [SMEM, VMEM, HBM],
-        [(VMEM, shape(TWO_PIECES, BF16)), (VMEM, shape((2 * N_SEQ, HD), F32))],
+def ring_prefix(got, after):
+    return call(
+        ring_prefix_kernel, "ring_prefix", [VMEM, HBM],
+        [
+            (VMEM, shape(PART, F32)), (VMEM, shape((3 * RING, HD), F32)),
+            (VMEM, shape((HD + PACK, HD), BF16)),
+        ],
         [], [], 12, 1e6, 1,
-    )(parents, got, after)
+    )(got, after)
+
+
+def ring_starts(parents, part, decays, mate, same, cross):
+    return call(
+        ring_starts_kernel, "ring_starts", [SMEM] + [VMEM] * 5,
+        [(VMEM, shape(TWO_STATES, BF16)), (VMEM, shape((8, HD), F32))],
+        [], [], 12, 1e6, 1,
+    )(parents, part, decays, mate, same, cross)
+
+
+def ring_suffix(parents, got, decays, after):
+    return call(
+        ring_suffix_kernel, "ring_suffix", [SMEM, VMEM, VMEM, HBM],
+        [
+            (VMEM, shape(PART, F32)), (VMEM, shape((RING, HD), F32)),
+            (VMEM, shape((2 * HD, HD), BF16)), (VMEM, shape((HD, HD), BF16)),
+        ],
+        [], [], 12, 1e6, 1,
+    )(parents, got, decays, after)
+
+
+def ring_ends(part, later, mate_decay, mate, same, cross, after):
+    return call(
+        ring_ends_kernel, "ring_ends", [VMEM] * 6 + [HBM],
+        [(VMEM, shape(STATE, BF16))], [], [], 12, 1e6, 1,
+    )(part, later, mate_decay, mate, same, cross, after)[0]
 
 
 def attend(ends, gains, d_out, starts, term, within):
@@ -534,22 +627,26 @@
 
 def grads(ends, gains, stats, scaled_queries, d_out, attended):
     return call(
-        grad_kernel, "grad", [VMEM] * 6, [(VMEM, shape(TWO_PIECES, BF16))],
+        grad_kernel, "grad", [VMEM] * 6, [(VMEM, shape(TWO_STATES, BF16))],
         [(CUM, F32), (CUM, F32)], [], 20, 3e8, 10,
     )(ends, gains, stats, scaled_queries, d_out, attended)[0]
 
 
-def local_grads(cum_rows, stats, gains, queries, keys, values, d_out, attended, states):
-    return call(
-        local_grads_kernel, "local_grads", [VMEM] * 3 + [HBM] * 6,
-        [
-            (HBM, WIDE), (HBM, WIDE), (HBM, WIDE), (HBM, WIDE),
-            (HBM, shape((4 * FAR, HD, HD), F32)), (VMEM, shape((8, HD), F32)),
-        ],
-        [(HEAD_ROWS, BF16)] * 5 + [((HL * BLOCKS, HD, HD), BF16)] + [(HEAD_ROWS, BF16)] * 4
+def local_grads(
+    blocks, cum_rows, stats, gains, queries, keys, values, d_out, attended, states, *partly
+):
+    some = (HL, len(blocks) * BLK, HD)
+    term = [] if partly else [(HBM, shape((4 * FAR, HD, HD), F32))]
+    left = 4 + len(term)
+    return call(
+        functools.partial(local_grads_kernel, blocks), "reply_grads" if partly else "local_grads",
+        [VMEM] * 3 + [HBM] * (6 + len(partly)),
+        [(HBM, WIDE)] * 4 + term + [(VMEM, shape((8, HD), F32))],
+        [(some, BF16)] * 5 + [((HL * BLOCKS, HD, HD), BF16)] + [(some, BF16)] * 4
         + [(STATE, F32), (CUM, F32), (CUM, F32)],
-        [6, 5], 53, 6e9, 24,
-    )(cum_rows, stats, gains, queries, keys, values, d_out, attended, states)
+        [6, left], 53, 2e9 * len(blocks), 8 * len(blocks),
+        {9 + number: number for number in range(len(partly))},
+    )(cum_rows, stats, gains, queries, keys, values, d_out, attended, states, *partly)
 
 
 def far_grads(cum_rows, ends, far, scaled_keys, values, term, near_keys, near_values):
@@ -560,35 +657,43 @@
     )(cum_rows, ends, far, scaled_keys, values, term, near_keys, near_values)
 
 
-def backward_scan(got, decays, after):
-    return call(
-        backward_scan_kernel, "backward_scan", [VMEM, VMEM, HBM],
-        [(VMEM, shape(PIECES, BF16))], [], [], 12, 1e6, 1,
-    )(got, decays, after)[0]
-
-
-def everyone(array, axis):
-    return lax.all_to_all(array, axis, 0, 0, tiled=True)
+def around(array):
+    groups = [[ring * RING + place for place in range(RING)] for ring in range(RINGS)]
+    return lax.all_to_all(array, "seq", 0, 0, axis_index_groups=groups, tiled=True)
+
+
+def across(array, step):
+    pairs = [(index, index ^ (step * RING)) for index in range(N_SEQ)]
+    return lax.ppermute(array, "seq", pairs)
+
+
+def everyone(array):
+    return lax.all_to_all(array, "head", 0, 0, tiled=True)
 
 
 def local(queries, keys, values, log_decay, gain, parents, d_out):
     gains = gain.reshape(HL, HD)
     decay_rows = jnp.swapaxes(log_decay, 1, 2)
     send, first_term, cum_rows, block_ends = summarize(decay_rows, keys, values)
-    got = everyone(send, "seq")
+    got = around(send)
     within, scaled_keys, done = inside(cum_rows, queries, keys, values)
-    send, decays = forward_scan(parents, got, done)
-    starts = everyone(send, "seq")
+    part, decays, send = ring_prefix(got, done)
+    send, mate_decay = ring_starts(
+        parents, part, decays, across(send, 1), across(send, 2), across(send, 3)
+    )
+    starts = around(send)
     near_queries, attended, stats, kept, states = attend(
         block_ends, gains, d_out, starts, first_term, within
     )
-    stats = everyone(stats, "head")
+    stats = everyone(stats)
     send = grads(block_ends, gains, stats, near_queries, d_out, attended)
-    got = everyone(send, "seq")
-    out, d_queries, d_keys, d_values, last_term, done = local_grads(
-        cum_rows, stats, gains, queries, keys, values, d_out, kept, states
-    )
-    far = everyone(backward_scan(got, decays, done), "seq")
+    got = around(send)
+    operands = (cum_rows, stats, gains, queries, keys, values, d_out, kept, states)
+    *partly, last_term, done = local_grads((0, 1), *operands)
+    part, later, mate_send, far_send = ring_suffix(parents, got, decays, done)
+    mate, same, cross = across(mate_send, 1), across(far_send, 2), across(far_send, 3)
+    out, d_queries, d_keys, d_values, done = local_grads((2,), *operands, *partly)
+    far = around(ring_ends(part, later, mate_decay, mate, same, cross, done))
     d_keys, d_values = far_grads(
         cum_rows, block_ends, far, scaled_keys, values, last_term, d_keys, d_values
     )

time: 116 us -> 122 us (1.052)
  blocking collectives: 48.8 us -> 42 us
  starting transfers between devices: 16 us -> 21.8 us
  Pallas kernels: 38.4 us -> 42.5 us
  waiting for transfers between devices: 9.56 us -> 13 us
    ppermute x0 -> x6, starting transfers between devices: none -> 8.36 us  [across(): return lax.ppermute(array, 'seq', pairs)]
    all_to_all x3, blocking collectives: 48.8 us -> 42 us  [the longest x2 32.2 us: around(): lax.all_to_all(array, 'seq', 0, 0, axis_index_groups=groups, tiled=True)]
    pallas_call x5 -> x8, Pallas kernels: 21.8 us -> 26.1 us  [the longest x2 17.2 us: local_grads(): call(functools.partial(local_grads_kernel, blocks), 'reply_grads' if part...]
    ppermute x0 -> x6, waiting for transfers between devices: none -> 4.14 us  [across(): return lax.ppermute(array, 'seq', pairs)]
    all_to_all x2, starting transfers between devices: 16 us -> 13.4 us  [around(): lax.all_to_all(array, 'seq', 0, 0, axis_index_groups=groups, tiled=True)]
  transfers between devices with their start and end apart: 2 -> 8, of which waited for: 2 -> 4; matrix products, arithmetic and copies ran while one was open for 0% -> 0% of each run, Pallas kernels for 19% -> 21%
where the time goes in v5:
time: 122 us; the launch traced here: 121 us
  Pallas kernels  42.5 us (35%)
  blocking collectives  42 us (34%)
  starting transfers between devices  21.8 us (18%)
  waiting for transfers between devices  13 us (11%)
    all_to_all x2, blocking collectives, around(): lax.all_to_all(array, 'seq', 0, 0, axis_index_groups=groups, tiled=True)  32.2 us
    pallas_call x2, Pallas kernels, local_grads(): call(functools.partial(local_grads_kernel, blocks), 'reply_grads' if part...  17.2 us
    all_to_all x2, starting transfers between devices, around(): lax.all_to_all(array, 'seq', 0, 0, axis_index_groups=groups, tiled=True)  13.4 us
    all_to_all x1, blocking collectives, everyone(): return lax.all_to_all(array, 'head', 0, 0, tiled=True)  9.89 us
    all_to_all x2, waiting for transfers between devices, around(): lax.all_to_all(array, 'seq', 0, 0, axis_index_groups=groups, tiled=True)  8.83 us
    ppermute x6, starting transfers between devices, across(): return lax.ppermute(array, 'seq', pairs)  8.36 us
    pallas_call x1, Pallas kernels, inside(): call(within_kernel, 'within', [VMEM] + [HBM] * 3, [(HBM, shape((FAR, ROWS...  8.28 us
    pallas_call x1, Pallas kernels, attend(): call(attend_kernel, 'attend', [VMEM] * 5 + [HBM], [(VMEM, shape(HEAD_ROWS...  4.18 us
  transfers between devices with their start and end apart: 8, of which 4 were waited for; matrix products, arithmetic and copies ran while one was open for 0% of the time, Pallas kernels for 21%

profile of v5, /device:TPU:32, one launch (start us, length us, event | category | flops | bytes accessed | tf_op | source)
XLA Modules:
  0.0 120.8 jit_solution(17157558185241819693)
XLA Ops:
  0.6 0.0 copy-start.3
  0.6 0.7 copy-done.3
  1.4 3.9 %summary.1 = (bf16[8,144,128]{2,1,0:T(8,128)(2,1)}, f32[8,128,128]{2,1,0:T(8,128)S(1)}, f32[8,768]{1,0:T(8,128)S(1)}, f32[8,8,128]{2,1,0:T(8,128)S(1)}) custom-call(f32[1,8,768]{2,1,0:T(8,128)S(1)} %bitcast.6, bf16[1,768,1024]{2,1,0:T(8,128)(2,1)} %keys_ref.7, bf16[1,768,1024]{2,1,0:T(8,128)(2,1)} %values_ref.9), custom_call_target="tpu_custom_call" | custom-call | flops 300000000 | bytes 4194304 | tf_op jit(solution)/shard_map/summary/pallas_call | solution.py:557
  5.2 8.6 %all-to-all-start = ((bf16[8,144,128]{2,1,0:T(8,128)(2,1)}), bf16[8,144,128]{2,1,0:T(8,128)(2,1)S(1)}, u32[]{:S(2)}, u32[]{:S(2)}) async-start(bf16[8,144,128]{2,1,0:T(8,128)(2,1)} %get-tuple-element.40), calls=%async_computation | async-start | bytes 589824 | tf_op jit(solution)/shard_map/all_to_all | solution.py:662
  13.8 0.0 copy-start.4
  13.8 8.3 %within.1 = (bf16[160,768,128]{2,1,0:T(8,128)(2,1)}, bf16[8,512,128]{2,1,0:T(8,128)(2,1)S(1)}, f32[8,128]{1,0:T(8,128)S(1)}) custom-call(f32[8,768]{1,0:T(8,128)S(1)} %get-tuple-element.38.cum_rows_ref, bf16[1,768,1024]{2,1,0:T(8,128)(2,1)} %queries_ref.5, bf16[1,768,1024]{2,1,0:T(8,128)(2,1)} %keys_ref.7, bf16[1,768,1024]{2,1,0:T(8,128)(2,1)} %values_ref.9), custom_call_target="tpu_custom_call" | custom-call | flops 4000000000 | bytes 16777216 | tf_op jit(solution)/shard_map/within/pallas_call | solution.py:568
  22.1 0.0 copy-start
  22.1 0.0 copy-start.2
  22.1 2.8 %all-to-all-done.got_ref = bf16[8,144,128]{2,1,0:T(8,128)(2,1)S(1)} async-done(((bf16[8,144,128]{2,1,0:T(8,128)(2,1)}), bf16[8,144,128]{2,1,0:T(8,128)(2,1)S(1)}, u32[]{:S(2)}, u32[]{:S(2)}) %all-to-all-start) | async-done | bytes 294944 | tf_op jit(solution)/shard_map/all_to_all | solution.py:662
  25.0 0.1 ring_prefix.1
  25.0 2.8 %collective-permute-start.2 = (bf16[144,128]{1,0:T(8,128)(2,1)S(1)}, bf16[144,128]{1,0:T(8,128)(2,1)S(1)}, u32[]{:S(2)}, u32[]{:S(2)}) collective-permute-start(bf16[144,128]{1,0:T(8,128)(2,1)S(1)} %get-tuple-element.44), channel_id=1, source_target_pairs={{0,192},{8,200},{16,208},{24,216},{32,224},{40,232},{48,240},{56,2... | collective-permute-start | bytes 110600 | tf_op jit(solution)/shard_map/ppermute | solution.py:667
  27.9 0.8 collective-permute-start.1
  28.7 0.5 collective-permute-start
  29.2 1.1 collective-permute-done.2.cross_ref
  30.3 3.1 %collective-permute-done.1.same_ref = bf16[144,128]{1,0:T(8,128)(2,1)S(1)} collective-permute-done((bf16[144,128]{1,0:T(8,128)(2,1)S(1)}, bf16[144,128]{1,0:T(8,128)(2,1)S(1)}, u32[]{:S(2)}, u32[]{:S(2)}) %collective-permute-start.1) | collective-permute-done | bytes 36896 | tf_op jit(solution)/shard_map/ppermute | solution.py:667
  33.3 0.0 collective-permute-done.mate_ref
  33.3 0.0 copy-done.4
  33.3 0.7 ring_starts.1
  34.0 18.3 %all_to_all.25.starts_ref = bf16[8,256,128]{2,1,0:T(8,128)(2,1)S(1)} all-to-all(bf16[8,256,128]{2,1,0:T(8,128)(2,1)S(1)} %get-tuple-element.45), channel_id=1, replica_groups={{0,8,16,24,32,40,48,56},{64,72,80,88,96,104,112,120},{128,136,144,152,1..., dimensions={0} | all-to-all | bytes 1048576 | tf_op jit(solution)/shard_map/all_to_all | solution.py:662
  52.3 0.0 copy-done
  52.3 0.0 copy-done.2
  52.3 4.2 %attend.1 = (bf16[8,768,128]{2,1,0:T(8,128)(2,1)S(1)}, bf16[8,768,128]{2,1,0:T(8,128)(2,1)S(1)}, f32[8,16,128]{2,1,0:T(8,128)S(1)}, bf16[160,768,128]{2,1,0:T(8,128)(2,1)}, bf16[960,128,128]{2,1,0:T(8,128)(2,1)}) custom-call(f32[8,8,128]{2,1,0:T(8,128)S(1)} %get-tuple-element.39.ends_ref, f32[8,128]{1,0:T(8,128)S(1)} %bitcast.2, ...), custom_call_target="tpu_custom_call" | custom-call | flops 300000000 | bytes 10485760 | tf_op jit(solution)/shard_map/attend/pallas_call | solution.py:616
  56.4 9.9 %all_to_all.26.stats_ref = f32[8,16,128]{2,1,0:T(8,128)S(1)} all-to-all(f32[8,16,128]{2,1,0:T(8,128)S(1)} %get-tuple-element.48), channel_id=1, replica_groups=mesh['seq'=32,'head'=8] {'head'}, dimensions={0} | all-to-all | bytes 131072 | tf_op jit(solution)/shard_map/all_to_all | solution.py:671
  66.3 3.6 %grad.1 = bf16[8,256,128]{2,1,0:T(8,128)(2,1)} custom-call(f32[8,8,128]{2,1,0:T(8,128)S(1)} %get-tuple-element.39.ends_ref, f32[8,128]{1,0:T(8,128)S(1)} %bitcast.3, f32[8,16,128]{2,1,0:T(8,128)S(1)} %all_to_all.26.stats_ref, bf16[8,768,128]{2,1,0:T(8,128)(2,1)S(1)} %get-tuple-element.57.queries_ref, bf16[1,768,1024]{2,1,0:T(8,128)(2,1)S(1)} %copy-done, ...), custom_call_target="tpu_custom_call" | custom-call | flops 300000000 | bytes 10485760 | tf_op jit(solution)/shard_map/grad/pallas_call | solution.py:629
  69.9 4.9 %all-to-all-start.3 = ((bf16[8,256,128]{2,1,0:T(8,128)(2,1)}), bf16[8,256,128]{2,1,0:T(8,128)(2,1)S(1)}, u32[]{:S(2)}, u32[]{:S(2)}) async-start(bf16[8,256,128]{2,1,0:T(8,128)(2,1)} %grad.1), calls=%async_computation.3 | async-start | bytes 1048576 | tf_op jit(solution)/shard_map/all_to_all | solution.py:662
  74.8 10.2 %local_grads.1 = (bf16[1,768,1024]{2,1,0:T(8,128)(2,1)}, bf16[1,768,1024]{2,1,0:T(8,128)(2,1)}, bf16[1,768,1024]{2,1,0:T(8,128)(2,1)}, bf16[1,768,1024]{2,1,0:T(...) custom-call(f32[8,768]{1,0:T(8,128)S(1)} %get-tuple-element.38.cum_rows_ref, ...), custom_call_target="tpu_custom_call" | custom-call | flops 4000000000 | bytes 16777216 | tf_op jit(solution)/shard_map/local_grads/pallas_call | solution.py:641
  85.0 6.0 %all-to-all-done.3.got_ref = bf16[8,256,128]{2,1,0:T(8,128)(2,1)S(1)} async-done(((bf16[8,256,128]{2,1,0:T(8,128)(2,1)}), bf16[8,256,128]{2,1,0:T(8,128)(2,1)S(1)}, u32[]{:S(2)}, u32[]{:S(2)}) %all-to-all-start.3) | async-done | bytes 524320 | tf_op jit(solution)/shard_map/all_to_all | solution.py:662
  91.0 0.7 ring_suffix.1
  91.7 1.5 %collective-permute-start.5 = (bf16[128,128]{1,0:T(8,128)(2,1)S(1)}, bf16[128,128]{1,0:T(8,128)(2,1)S(1)}, u32[]{:S(2)}, u32[]{:S(2)}) collective-permute-start(bf16[128,128]{1,0:T(8,128)(2,1)S(1)} %get-tuple-element.64), channel_id=1, source_target_pairs={{0,192},{8,200},{16,208},{24,216},{32,224},{40,232},{48,240},{56,2... | collective-permute-start | bytes 98312 | tf_op jit(solution)/shard_map/ppermute | solution.py:667
  93.2 0.9 collective-permute-start.4
  94.1 1.8 %collective-permute-start.3 = (bf16[256,128]{1,0:T(8,128)(2,1)S(1)}, bf16[256,128]{1,0:T(8,128)(2,1)S(1)}, u32[]{:S(2)}, u32[]{:S(2)}) collective-permute-start(bf16[256,128]{1,0:T(8,128)(2,1)S(1)} %get-tuple-element.63), channel_id=1, source_target_pairs={{0,64},{8,72},{16,80},{24,88},{32,96},{40,104},{48,112},{56,120},{... | collective-permute-start | bytes 196616 | tf_op jit(solution)/shard_map/ppermute | solution.py:667
  95.9 0.0 copy-start.1
  95.9 7.0 %reply_grads.1 = (bf16[1,768,1024]{2,1,0:T(8,128)(2,1)}, bf16[1,768,1024]{2,1,0:T(8,128)(2,1)}, bf16[1,768,1024]{2,1,0:T(8,128)(2,1)}, bf16[1,768,1024]{2,1,0:T(8,128)(2,1)}, f32[8,128]{1,0:T(8,128)S(1)}) custom-call(f32[8,768]{1,0:T(8,128)S(1)} %get-tuple-element.38.cum_rows_ref, ...), custom_call_target="tpu_custom_call", output_to_operand_aliasing={{0}: (9, {}), {1}: (10, {}), {2}: (11, {}), {3}: (12, {})} | custom-call | flops 2000000000 | bytes 8388608 | tf_op jit(solution)/shard_map/reply_grads/pallas_call | solution.py:641
  102.9 0.0 collective-permute-done.5.cross_ref
  102.9 0.0 collective-permute-done.4.same_ref
  102.9 0.0 collective-permute-done.3.mate_ref
  102.9 0.1 ring_ends.1
  103.0 13.9 %all_to_all.27.far_ref = bf16[8,128,128]{2,1,0:T(8,128)(2,1)S(1)} all-to-all(bf16[8,128,128]{2,1,0:T(8,128)(2,1)S(1)} %ring_ends.1), channel_id=1, replica_groups={{0,8,16,24,32,40,48,56},{64,72,80,88,96,104,112,120},{128,136,144,152,1..., dimensions={0} | all-to-all | bytes 524288 | tf_op jit(solution)/shard_map/all_to_all | solution.py:662
  116.9 0.0 copy-done.1
  116.9 3.9 %far_grads.1 = (bf16[1,768,1024]{2,1,0:T(8,128)(2,1)}, bf16[1,768,1024]{2,1,0:T(8,128)(2,1)}) custom-call(f32[8,768]{1,0:T(8,128)S(1)} %get-tuple-element.38.cum_rows_ref, f32[8,8,128]{2,1,0:T(8,128)S(1)} %get-tuple-element.39.ends_ref, bf16[8,128,128]{2,1,0:T(8,128)(2,1)S(1)} %all_to_all.27.far_ref, ...), custom_call_target="tpu_custom_call", output_to_operand_aliasing={{0}: (6, {}), {1}: (7, {})} | custom-call | flops 300000000 | bytes 10485760 | tf_op jit(solution)/shard_map/far_grads/pallas_call | solution.py:653
Async XLA Ops:
  0.6 0.7 copy-start.3
  5.2 19.7 %all-to-all-start = ((bf16[8,144,128]{2,1,0:T(8,128)(2,1)}), bf16[8,144,128]{2,1,0:T(8,128)(2,1)S(1)}, u32[]{:S(2)}, u32[]{:S(2)}) async-start(bf16[8,144,128]{2,1,0:T(8,128)(2,1)} %get-tuple-element.40), calls=%async_computation | async-start | bytes 589824 | tf_op jit(solution)/shard_map/all_to_all | solution.py:662
  13.8 19.5 %copy-start.4 = (s32[32]{0:T(128)S(1)}, s32[32]{0:T(128)}, u32[]{:S(2)}) copy-start(s32[32]{0:T(128)} %parents_ref.3) | copy-start | bytes 388
  22.1 30.1 %copy-start = (bf16[1,768,1024]{2,1,0:T(8,128)(2,1)S(1)}, bf16[1,768,1024]{2,1,0:T(8,128)(2,1)}, u32[]{:S(2)}) copy-start(bf16[1,768,1024]{2,1,0:T(8,128)(2,1)} %d_out_ref.7) | copy-start | bytes 4718596
  22.1 30.1 %copy-start.2 = (f32[1024]{0:T(1024)S(1)}, f32[1024]{0:T(1024)}, u32[]{:S(2)}) copy-start(f32[1024]{0:T(1024)} %param.11) | copy-start | bytes 12292
  25.0 5.3 %collective-permute-start.2 = (bf16[144,128]{1,0:T(8,128)(2,1)S(1)}, bf16[144,128]{1,0:T(8,128)(2,1)S(1)}, u32[]{:S(2)}, u32[]{:S(2)}) collective-permute-start(bf16[144,128]{1,0:T(8,128)(2,1)S(1)} %get-tuple-element.44), channel_id=1, source_target_pairs={{0,192},{8,200},{16,208},{24,216},{32,224},{40,232},{48,240},{56,2... | collective-permute-start | bytes 110600 | tf_op jit(solution)/shard_map/ppermute | solution.py:667
  27.9 5.5 %collective-permute-start.1 = (bf16[144,128]{1,0:T(8,128)(2,1)S(1)}, bf16[144,128]{1,0:T(8,128)(2,1)S(1)}, u32[]{:S(2)}, u32[]{:S(2)}) collective-permute-start(bf16[144,128]{1,0:T(8,128)(2,1)S(1)} %get-tuple-element.44), channel_id=1, source_target_pairs={{0,128},{8,136},{16,144},{24,152},{32,160},{40,168},{48,176},{56,1... | collective-permute-start | bytes 110600 | tf_op jit(solution)/shard_map/ppermute | solution.py:667
  28.7 4.7 %collective-permute-start = (bf16[144,128]{1,0:T(8,128)(2,1)S(1)}, bf16[144,128]{1,0:T(8,128)(2,1)S(1)}, u32[]{:S(2)}, u32[]{:S(2)}) collective-permute-start(bf16[144,128]{1,0:T(8,128)(2,1)S(1)} %get-tuple-element.44), channel_id=1, source_target_pairs={{0,64},{8,72},{16,80},{24,88},{32,96},{40,104},{48,112},{56,120},{... | collective-permute-start | bytes 110600 | tf_op jit(solution)/shard_map/ppermute | solution.py:667
  69.9 21.1 %all-to-all-start.3 = ((bf16[8,256,128]{2,1,0:T(8,128)(2,1)}), bf16[8,256,128]{2,1,0:T(8,128)(2,1)S(1)}, u32[]{:S(2)}, u32[]{:S(2)}) async-start(bf16[8,256,128]{2,1,0:T(8,128)(2,1)} %grad.1), calls=%async_computation.3 | async-start | bytes 1048576 | tf_op jit(solution)/shard_map/all_to_all | solution.py:662
  91.7 11.2 %collective-permute-start.5 = (bf16[128,128]{1,0:T(8,128)(2,1)S(1)}, bf16[128,128]{1,0:T(8,128)(2,1)S(1)}, u32[]{:S(2)}, u32[]{:S(2)}) collective-permute-start(bf16[128,128]{1,0:T(8,128)(2,1)S(1)} %get-tuple-element.64), channel_id=1, source_target_pairs={{0,192},{8,200},{16,208},{24,216},{32,224},{40,232},{48,240},{56,2... | collective-permute-start | bytes 98312 | tf_op jit(solution)/shard_map/ppermute | solution.py:667
  93.2 9.7 %collective-permute-start.4 = (bf16[128,128]{1,0:T(8,128)(2,1)S(1)}, bf16[128,128]{1,0:T(8,128)(2,1)S(1)}, u32[]{:S(2)}, u32[]{:S(2)}) collective-permute-start(bf16[128,128]{1,0:T(8,128)(2,1)S(1)} %get-tuple-element.64), channel_id=1, source_target_pairs={{0,128},{8,136},{16,144},{24,152},{32,160},{40,168},{48,176},{56,1... | collective-permute-start | bytes 98312 | tf_op jit(solution)/shard_map/ppermute | solution.py:667
  94.1 8.8 %collective-permute-start.3 = (bf16[256,128]{1,0:T(8,128)(2,1)S(1)}, bf16[256,128]{1,0:T(8,128)(2,1)S(1)}, u32[]{:S(2)}, u32[]{:S(2)}) collective-permute-start(bf16[256,128]{1,0:T(8,128)(2,1)S(1)} %get-tuple-element.63), channel_id=1, source_target_pairs={{0,64},{8,72},{16,80},{24,88},{32,96},{40,104},{48,112},{56,120},{... | collective-permute-start | bytes 196616 | tf_op jit(solution)/shard_map/ppermute | solution.py:667
  95.9 21.0 %copy-start.1 = (bf16[1,768,1024]{2,1,0:T(8,128)(2,1)S(1)}, bf16[1,768,1024]{2,1,0:T(8,128)(2,1)}, u32[]{:S(2)}) copy-start(bf16[1,768,1024]{2,1,0:T(8,128)(2,1)} %values_ref.9) | copy-start | bytes 4718596

commit v6 on v4

--- a/solution.py
+++ b/solution.py
@@ -20,6 +20,7 @@
 BLOCKS = ROWS // BLK
 TILES = ROWS // HD
 EPS = 1e-05
+GROUP = 2
 
 F32 = jnp.float32
 BF16 = jnp.bfloat16
@@ -91,25 +92,32 @@
         for copy in self.each(head):
             copy.start()
 
+    def begin(self):
+        for head in range(HL):
+            self.start(head)
+
     def wait(self, head):
         for copy in self.each(head):
             copy.wait()
 
 
-def over_heads(fetch, body, leave=None, started=False):
+def over_heads(fetch, body, leave=None, started=False, group=GROUP):
     if fetch is not None and not started:
-        for head in range(HL):
-            fetch.start(head)
-
-    def step(head, carry):
-        if fetch is not None:
-            fetch.wait(head)
-        body(head)
-        if leave is not None:
-            leave.start(head)
+        fetch.begin()
+
+    def step(number, carry):
+        heads = [number * group + place for place in range(group)]
+        for head in heads:
+            if fetch is not None:
+                fetch.wait(head)
+        for head in heads:
+            body(head)
+        for head in heads:
+            if leave is not None:
+                leave.start(head)
         return carry
 
-    lax.fori_loop(0, HL, step, 0)
+    lax.fori_loop(0, HL // group, step, 0)
     if leave is not None:
         for head in range(HL):
             leave.wait(head)
@@ -134,8 +142,7 @@
         ],
         in_sems,
     )
-    for head in range(HL):
-        fetch.start(head)
+    fetch.begin()
     before = lax.broadcasted_iota(jnp.int32, (BLK, BLK), 0)
     after = lax.broadcasted_iota(jnp.int32, (BLK, BLK), 1)
     upper = jnp.where(before <= after, 1.0, 0.0).astype(BF16)
@@ -171,12 +178,7 @@
             send_ref[at, 0:PIECE, :] = summary[piece * PIECE : (piece + 1) * PIECE].astype(BF16)
             send_ref[at, PIECE : PIECE + 16, :] = packed
 
-    def step(head, carry):
-        fetch.wait(head)
-        body(head)
-        return carry
-
-    lax.fori_loop(0, HL, step, 0)
+    over_heads(fetch, body, started=True, group=4)
 
 
 def within_kernel(
@@ -220,7 +222,7 @@
                 factor = down(jnp.exp(row[:, BLK - 1 : BLK] - row))
                 scaled_keys_buf[head, part, :] = rounded_product(keys, factor)
 
-    over_heads(fetch, body, leave)
+    over_heads(fetch, body, leave, group=4)
 
 
 def forward_scan_kernel(parents_ref, got_ref, _after, send_ref, decay_ref):
@@ -260,8 +262,7 @@
         ],
         out_sems,
     )
-    for head in range(HL):
-        fetch.start(head)
+    fetch.begin()
     squares_ref[...] = jnp.zeros_like(squares_ref)
     products_ref[...] = jnp.zeros_like(products_ref)
 
@@ -331,7 +332,7 @@
             send_ref[at, 0:PIECE, :] = local_sum[part].astype(BF16)
             send_ref[at, PIECE : 2 * PIECE, :] = terms[2][part].astype(BF16)
 
-    over_heads(None, body)
+    over_heads(None, body, group=HL)
 
 
 def backward_scan_kernel(got_ref, decay_ref, _after, send_ref):
@@ -377,8 +378,7 @@
         ],
         out_sems,
     )
-    for head in range(HL):
-        fetch.start(head)
+    fetch.begin()
     done_ref[...] = jnp.zeros_like(done_ref)
     row_factors(stats_ref, inverse_ref, slope_ref)
     row_ids = lax.broadcasted_iota(jnp.int32, (BLK, BLK), 0)

time: 116 us -> 113 us (0.974)
  Pallas kernels: 38.4 us -> 34.1 us
  waiting for transfers between devices: 9.56 us -> 11.2 us
    all_to_all x2, waiting for transfers between devices: 9.56 us -> 11.2 us  [everyone(): return lax.all_to_all(array, axis, 0, 0, tiled=True)]
    pallas_call x1, Pallas kernels: 8.4 us -> 6.82 us  [inside(): call(within_kernel, 'within', [VMEM] + [HBM] * 3, [(HBM, shape((FAR, ROWS...]
    pallas_call x1, Pallas kernels: 3.58 us -> 2.24 us  [grads(): call(grad_kernel, 'grad', [VMEM] * 6, [(VMEM, shape(TWO_PIECES, BF16))],...]
  transfers between devices with their start and end apart: 2 -> 2, of which waited for: 2 -> 2; matrix products, arithmetic and copies ran while one was open for 0% -> 0% of each run, Pallas kernels for 19% -> 18%
where the time goes in v6:
time: 113 us
  blocking collectives  48.7 us (43%)
  Pallas kernels  34.1 us (30%)
  starting transfers between devices  16.1 us (14%)
  waiting for transfers between devices  11.2 us (10%)
  local copies, waits for them, and re-layouts  1.74 us (2%)
    all_to_all x3, blocking collectives, everyone(): return lax.all_to_all(array, axis, 0, 0, tiled=True)  48.7 us
    all_to_all x2, starting transfers between devices, everyone(): return lax.all_to_all(array, axis, 0, 0, tiled=True)  16.1 us
    pallas_call x1, Pallas kernels, local_grads(): call(local_grads_kernel, 'local_grads', [VMEM] * 3 + [HBM] * 6, [(HBM, WI...  13.3 us
    all_to_all x2, waiting for transfers between devices, everyone(): return lax.all_to_all(array, axis, 0, 0, tiled=True)  11.2 us
    pallas_call x1, Pallas kernels, inside(): call(within_kernel, 'within', [VMEM] + [HBM] * 3, [(HBM, shape((FAR, ROWS...  6.82 us
    pallas_call x1, Pallas kernels, attend(): call(attend_kernel, 'attend', [VMEM] * 5 + [HBM], [(VMEM, shape(HEAD_ROWS...  4.15 us
    pallas_call x1, Pallas kernels, far_grads(): call(far_grads_kernel, 'far_grads', [VMEM] * 5 + [HBM] * 3, [(HBM, WIDE),...  3.59 us
    pallas_call x1, Pallas kernels, summarize(): call(summary_kernel, 'summary', [VMEM, HBM, HBM], [(VMEM, shape(SENT_PIEC...  3.01 us
  transfers between devices with their start and end apart: 2, of which 2 were waited for; matrix products, arithmetic and copies ran while one was open for 0% of the time, Pallas kernels for 18%

profile of v6, /device:TPU:32, one launch (start us, length us, event | category | flops | bytes accessed | tf_op | source)
XLA Modules:
  0.0 112.5 jit_solution(15996555555021927703)
XLA Ops:
  0.6 0.0 copy-start.5
  0.6 0.7 copy-done.5
  1.4 3.0 %summary.1 = (bf16[32,48,128]{2,1,0:T(8,128)(2,1)}, f32[8,128,128]{2,1,0:T(8,128)S(1)}, f32[8,768]{1,0:T(8,128)S(1)}, f32[8,8,128]{2,1,0:T(8,128)S(1)}) custom-call(f32[1,8,768]{2,1,0:T(8,128)S(1)} %bitcast.5, bf16[1,768,1024]{2,1,0:T(8,128)(2,1)} %keys_ref.5, bf16[1,768,1024]{2,1,0:T(8,128)(2,1)} %values_ref.7), custom_call_target="tpu_custom_call" | custom-call | flops 300000000 | bytes 4194304 | tf_op jit(solution)/shard_map/summary/pallas_call | solution.py:493
  4.4 11.2 %all-to-all-start = ((bf16[32,48,128]{2,1,0:T(8,128)(2,1)}), bf16[32,48,128]{2,1,0:T(8,128)(2,1)S(1)}, u32[]{:S(2)}, u32[]{:S(2)}) async-start(bf16[32,48,128]{2,1,0:T(8,128)(2,1)} %get-tuple-element.28), calls=%async_computation | async-start | bytes 786432 | tf_op jit(solution)/shard_map/all_to_all | solution.py:571
  15.6 0.0 copy-start.6
  15.6 0.0 copy-start.1
  15.6 0.0 copy-start.4
  15.6 6.8 %within.1 = (bf16[160,768,128]{2,1,0:T(8,128)(2,1)}, bf16[8,512,128]{2,1,0:T(8,128)(2,1)S(1)}, f32[8,128]{1,0:T(8,128)S(1)}) custom-call(f32[8,768]{1,0:T(8,128)S(1)} %get-tuple-element.26.cum_rows_ref, bf16[1,768,1024]{2,1,0:T(8,128)(2,1)} %queries_ref.3, bf16[1,768,1024]{2,1,0:T(8,128)(2,1)} %keys_ref.5, bf16[1,768,1024]{2,1,0:T(8,128)(2,1)} %values_ref.7), custom_call_target="tpu_custom_call" | custom-call | flops 4000000000 | bytes 16777216 | tf_op jit(solution)/shard_map/within/pallas_call | solution.py:504
  22.4 0.0 copy-start.2
  22.5 1.0 copy-done.2
  23.4 7.0 %all-to-all-done.got_ref = bf16[32,48,128]{2,1,0:T(8,128)(2,1)S(1)} async-done(((bf16[32,48,128]{2,1,0:T(8,128)(2,1)}), bf16[32,48,128]{2,1,0:T(8,128)(2,1)S(1)}, u32[]{:S(2)}, u32[]{:S(2)}) %all-to-all-start) | async-done | bytes 393248 | tf_op jit(solution)/shard_map/all_to_all | solution.py:571
  30.5 0.0 copy-done.6
  30.5 0.7 forward_scan.1
  31.2 21.7 %all_to_all.25.starts_ref = bf16[32,64,128]{2,1,0:T(8,128)(2,1)S(1)} all-to-all(bf16[32,64,128]{2,1,0:T(8,128)(2,1)S(1)} %get-tuple-element.30), channel_id=1, replica_groups=mesh['seq'=32,'head'=8] {'seq'}, dimensions={0} | all-to-all | bytes 1048576 | tf_op jit(solution)/shard_map/all_to_all | solution.py:571
  52.9 0.0 copy-done.1
  52.9 0.0 copy-done.4
  52.9 4.2 %attend.1 = (bf16[8,768,128]{2,1,0:T(8,128)(2,1)S(1)}, bf16[8,768,128]{2,1,0:T(8,128)(2,1)S(1)}, f32[8,16,128]{2,1,0:T(8,128)S(1)}, bf16[160,768,128]{2,1,0:T(8,128)(2,1)}, bf16[960,128,128]{2,1,0:T(8,128)(2,1)}) custom-call(f32[8,8,128]{2,1,0:T(8,128)S(1)} %get-tuple-element.27.ends_ref, f32[8,128]{1,0:T(8,128)S(1)} %bitcast.2, ...), custom_call_target="tpu_custom_call" | custom-call | flops 300000000 | bytes 10485760 | tf_op jit(solution)/shard_map/attend/pallas_call | solution.py:523
  57.0 9.9 %all_to_all.26.stats_ref = f32[8,16,128]{2,1,0:T(8,128)S(1)} all-to-all(f32[8,16,128]{2,1,0:T(8,128)S(1)} %get-tuple-element.33), channel_id=1, replica_groups=mesh['seq'=32,'head'=8] {'head'}, dimensions={0} | all-to-all | bytes 131072 | tf_op jit(solution)/shard_map/all_to_all | solution.py:571
  66.9 2.2 %grad.1 = bf16[32,64,128]{2,1,0:T(8,128)(2,1)} custom-call(f32[8,8,128]{2,1,0:T(8,128)S(1)} %get-tuple-element.27.ends_ref, f32[8,128]{1,0:T(8,128)S(1)} %bitcast.3, f32[8,16,128]{2,1,0:T(8,128)S(1)} %all_to_all.26.stats_ref, bf16[8,768,128]{2,1,0:T(8,128)(2,1)S(1)} %get-tuple-element.38.queries_ref, bf16[1,768,1024]{2,1,0:T(8,128)(2,1)S(1)} %copy-done.1, ...), custom_call_target="tpu_custom_call" | custom-call | flops 300000000 | bytes 10485760 | tf_op jit(solution)/shard_map/grad/pallas_call | solution.py:536
  69.1 4.9 %all-to-all-start.3 = ((bf16[32,64,128]{2,1,0:T(8,128)(2,1)}), bf16[32,64,128]{2,1,0:T(8,128)(2,1)S(1)}, u32[]{:S(2)}, u32[]{:S(2)}) async-start(bf16[32,64,128]{2,1,0:T(8,128)(2,1)} %grad.1), calls=%async_computation.3 | async-start | bytes 1048576 | tf_op jit(solution)/shard_map/all_to_all | solution.py:571
  74.0 0.0 copy-start
  74.0 13.3 %local_grads.1 = (bf16[1,768,1024]{2,1,0:T(8,128)(2,1)}, bf16[1,768,1024]{2,1,0:T(8,128)(2,1)}, bf16[1,768,1024]{2,1,0:T(8,128)(2,1)}, bf16[1,768,1024]{2,1,0:T(...) custom-call(f32[8,768]{1,0:T(8,128)S(1)} %get-tuple-element.26.cum_rows_ref, ...), custom_call_target="tpu_custom_call" | custom-call | flops 6000000000 | bytes 25165824 | tf_op jit(solution)/shard_map/local_grads/pallas_call | solution.py:543
  87.3 0.0 copy-start.3
  87.3 4.2 %all-to-all-done.3.got_ref = bf16[32,64,128]{2,1,0:T(8,128)(2,1)S(1)} async-done(((bf16[32,64,128]{2,1,0:T(8,128)(2,1)}), bf16[32,64,128]{2,1,0:T(8,128)(2,1)S(1)}, u32[]{:S(2)}, u32[]{:S(2)}) %all-to-all-start.3) | async-done | bytes 524320 | tf_op jit(solution)/shard_map/all_to_all | solution.py:571
  91.5 0.2 backward_scan.1
  91.8 17.1 %all_to_all.27.far_ref = bf16[32,32,128]{2,1,0:T(8,128)(2,1)S(1)} all-to-all(bf16[32,32,128]{2,1,0:T(8,128)(2,1)S(1)} %backward_scan.1), channel_id=1, replica_groups=mesh['seq'=32,'head'=8] {'seq'}, dimensions={0} | all-to-all | bytes 524288 | tf_op jit(solution)/shard_map/all_to_all | solution.py:571
  108.9 0.0 copy-done
  108.9 0.0 copy-done.3
  108.9 3.6 %far_grads.1 = (bf16[1,768,1024]{2,1,0:T(8,128)(2,1)}, bf16[1,768,1024]{2,1,0:T(8,128)(2,1)}) custom-call(f32[8,768]{1,0:T(8,128)S(1)} %get-tuple-element.26.cum_rows_ref, f32[8,8,128]{2,1,0:T(8,128)S(1)} %get-tuple-element.27.ends_ref, bf16[32,32,128]{2,1,0:T(8,128)(2,1)S(1)} %all_to_all.27.far_ref, ...), custom_call_target="tpu_custom_call", output_to_operand_aliasing={{0}: (6, {}), {1}: (7, {})} | custom-call | flops 300000000 | bytes 10485760 | tf_op jit(solution)/shard_map/far_grads/pallas_call | solution.py:556
Async XLA Ops:
  0.6 0.7 copy-start.5
  4.4 26.1 %all-to-all-start = ((bf16[32,48,128]{2,1,0:T(8,128)(2,1)}), bf16[32,48,128]{2,1,0:T(8,128)(2,1)S(1)}, u32[]{:S(2)}, u32[]{:S(2)}) async-start(bf16[32,48,128]{2,1,0:T(8,128)(2,1)} %get-tuple-element.28), calls=%async_computation | async-start | bytes 786432 | tf_op jit(solution)/shard_map/all_to_all | solution.py:571
  15.6 14.9 %copy-start.6 = (s32[32]{0:T(128)S(1)}, s32[32]{0:T(128)}, u32[]{:S(2)}) copy-start(s32[32]{0:T(128)} %parents_ref.1) | copy-start | bytes 388
  15.6 37.3 %copy-start.1 = (bf16[1,768,1024]{2,1,0:T(8,128)(2,1)S(1)}, bf16[1,768,1024]{2,1,0:T(8,128)(2,1)}, u32[]{:S(2)}) copy-start(bf16[1,768,1024]{2,1,0:T(8,128)(2,1)} %d_out_ref.5) | copy-start | bytes 4718596
  15.6 37.3 %copy-start.4 = (f32[1024]{0:T(1024)S(1)}, f32[1024]{0:T(1024)}, u32[]{:S(2)}) copy-start(f32[1024]{0:T(1024)} %param.11) | copy-start | bytes 12292
  22.4 1.0 copy-start.2
  69.1 22.4 %all-to-all-start.3 = ((bf16[32,64,128]{2,1,0:T(8,128)(2,1)}), bf16[32,64,128]{2,1,0:T(8,128)(2,1)S(1)}, u32[]{:S(2)}, u32[]{:S(2)}) async-start(bf16[32,64,128]{2,1,0:T(8,128)(2,1)} %grad.1), calls=%async_computation.3 | async-start | bytes 1048576 | tf_op jit(solution)/shard_map/all_to_all | solution.py:571
  74.0 34.9 %copy-start = (bf16[1,768,1024]{2,1,0:T(8,128)(2,1)S(1)}, bf16[1,768,1024]{2,1,0:T(8,128)(2,1)}, u32[]{:S(2)}) copy-start(bf16[1,768,1024]{2,1,0:T(8,128)(2,1)} %values_ref.7) | copy-start | bytes 4718596
  87.3 21.6 %copy-start.3 = (bf16[8,512,128]{2,1,0:T(8,128)(2,1)S(1)}, bf16[8,512,128]{2,1,0:T(8,128)(2,1)}, u32[]{:S(2)}) copy-start(bf16[8,512,128]{2,1,0:T(8,128)(2,1)} %copy-done.2) | copy-start | bytes 3145732

commit v7 on v6

--- a/solution.py
+++ b/solution.py
@@ -17,6 +17,7 @@
 COLS = HL * HD
 PIECE = HL * HD // N_SEQ
 PARTS = HD // PIECE
+PACK = 16
 BLOCKS = ROWS // BLK
 TILES = ROWS // HD
 EPS = 1e-05
@@ -133,7 +134,7 @@
 def summary_kernel(
     decay_ref, keys_ref, values_ref,
     send_ref, term_ref, cum_rows_ref, ends_ref,
-    keys_buf, values_buf, in_sems,
+    keys_buf, values_buf, decay_buf, send_buf, in_sems, out_sems, decay_sem,
 ):
     fetch = Copies(
         [
@@ -142,12 +143,16 @@
         ],
         in_sems,
     )
+    leave = Copies([(of_lead(send_buf, PARTS), of_lead(send_ref, PARTS))], out_sems)
+    decay_copy = pltpu.make_async_copy(decay_ref, decay_buf, decay_sem.at[0, 0])
+    decay_copy.start()
     fetch.begin()
     before = lax.broadcasted_iota(jnp.int32, (BLK, BLK), 0)
     after = lax.broadcasted_iota(jnp.int32, (BLK, BLK), 1)
     upper = jnp.where(before <= after, 1.0, 0.0).astype(BF16)
+    decay_copy.wait()
     stacked = jnp.concatenate(
-        [decay_ref[0, :, rows(number)] for number in range(BLOCKS)], axis=0
+        [decay_buf[0, :, rows(number)] for number in range(BLOCKS)], axis=0
     )
     coarse, middle, fine = (mm(part, upper) for part in split(stacked))
     cumulative = (fine + middle) + coarse
@@ -155,7 +160,7 @@
         total = cumulative[number * HL : (number + 1) * HL]
         cum_rows_ref[:, rows(number)] = total
         ends_ref[:, number, :] = jnp.broadcast_to(jnp.exp(total[:, BLK - 1 : BLK]), (HL, HD))
-    row_ids = lax.broadcasted_iota(jnp.int32, (16, HD), 0)
+    row_ids = lax.broadcasted_iota(jnp.int32, (PACK, HD), 0)
 
     def body(head):
         terms = []
@@ -168,24 +173,24 @@
         term_ref[head] = terms[0]
         end_decays = ends_ref[head]
         summary = end_decays[1:2, :] * terms[0] + terms[1]
-        decay = jnp.broadcast_to(end_decays[0:1, :] * end_decays[1:2, :], (16, HD))
+        decay = jnp.broadcast_to(end_decays[0:1, :] * end_decays[1:2, :], (PACK, HD))
         coarse, middle, _ = split(decay)
         packed = jnp.where(
             row_ids == 0, coarse.astype(F32), jnp.where(row_ids == 1, middle.astype(F32), 0.0)
         ).astype(BF16)
         for piece in range(PARTS):
             at = head * PARTS + piece
-            send_ref[at, 0:PIECE, :] = summary[piece * PIECE : (piece + 1) * PIECE].astype(BF16)
-            send_ref[at, PIECE : PIECE + 16, :] = packed
-
-    over_heads(fetch, body, started=True, group=4)
+            send_buf[at, 0:PIECE, :] = summary[piece * PIECE : (piece + 1) * PIECE].astype(BF16)
+            send_buf[at, PIECE : PIECE + PACK, :] = packed
+
+    over_heads(fetch, body, leave, started=True, group=4)
 
 
 def within_kernel(
     cum_rows_ref, queries_ref, keys_ref, values_ref,
-    within_ref, scaled_keys_ref, done_ref,
+    within_ref, scaled_keys_ref, weights_ref, done_ref,
     queries_buf, keys_buf, values_buf, within_buf, scaled_queries_buf, scaled_keys_buf,
-    in_sems, out_sems,
+    weights_buf, in_sems, out_sems,
 ):
     fetch = Copies(
         [
@@ -200,6 +205,7 @@
             (of_lead(within_buf), of_lead(within_ref)),
             (of_lead(scaled_queries_buf), of_lead(within_ref, first=HL)),
             (of_lead(scaled_keys_buf), of_lead(scaled_keys_ref)),
+            (of_lead(weights_buf), of_lead(weights_ref)),
         ],
         out_sems,
     )
@@ -213,10 +219,11 @@
             queries = queries_buf[head, part, :]
             keys = keys_buf[head, part, :]
             row = cum_rows_ref[pl.ds(head, 1), part]
-            gaps = twice(down(row)) - row
-            mask = jnp.where(row_ids >= col_ids, jnp.exp(gaps), 0.0)
-            weights = (mm_nt(queries, keys) * mask).astype(BF16)
-            within_buf[head, part, :] = mm(weights, values_buf[head, part, :]).astype(BF16)
+            gaps = row - twice(down(row))
+            mask = jnp.where(col_ids >= row_ids, jnp.exp(gaps), 0.0)
+            weights = (mm_nt(keys, queries) * mask).astype(BF16)
+            weights_buf[head, part, :] = weights
+            within_buf[head, part, :] = mm_tn(weights, values_buf[head, part, :]).astype(BF16)
             scaled_queries_buf[head, part, :] = rounded_product(queries, down(jnp.exp(row)))
             if number < 2:
                 factor = down(jnp.exp(row[:, BLK - 1 : BLK] - row))
@@ -230,7 +237,7 @@
     for prompt in range(PROMPTS):
         carry = jnp.zeros((PIECE, HD), F32)
         for index in range(prompt * SPAN, (prompt + 1) * SPAN):
-            packed = got_ref[index, PIECE : PIECE + 16, :].astype(F32)
+            packed = got_ref[index, PIECE : PIECE + PACK, :].astype(F32)
             decay = packed[0:1, :] + packed[1:2, :]
             decay_ref[index : index + 1, :] = decay
             send_ref[index, 0:PIECE, :] = carry.astype(BF16)
@@ -351,9 +358,9 @@
 
 def local_grads_kernel(
     cum_rows_ref, stats_ref, gain_ref,
-    queries_ref, keys_ref, values_ref, d_out_ref, attended_ref, states_ref,
+    queries_ref, keys_ref, values_ref, d_out_ref, attended_ref, states_ref, weights_ref,
     out_ref, d_queries_ref, d_keys_ref, d_values_ref, term_ref, done_ref,
-    queries_buf, keys_buf, values_buf, d_out_buf, attended_buf, states_buf,
+    queries_buf, keys_buf, values_buf, d_out_buf, attended_buf, states_buf, weights_buf,
     out_buf, d_queries_buf, d_keys_buf, d_values_buf, term_buf,
     inverse_ref, slope_ref, in_sems, out_sems,
 ):
@@ -365,6 +372,7 @@
             (of_rows(keys_ref), of_lead(keys_buf)),
             (of_rows(values_ref), of_lead(values_buf)),
             (of_lead(states_ref, BLOCKS), of_lead(states_buf, BLOCKS)),
+            (of_lead(weights_ref), of_lead(weights_buf)),
         ],
         in_sems,
     )
@@ -399,7 +407,7 @@
             row = cum_rows_ref[pl.ds(head, 1), part]
             gaps = row - twice(down(row))
             mask = jnp.where(col_ids >= row_ids, jnp.exp(gaps), 0.0)
-            weights = (mm_nt(keys, queries) * mask).astype(BF16)
+            weights = weights_buf[head, part, :]
             score_grad = (mm_nt(values, grad) * mask).astype(BF16)
             growth = down(jnp.exp(row))
             start = states_buf[head * BLOCKS + number]
@@ -467,9 +475,9 @@
 STATE = (HL, HD, HD)
 PIECES = (N_SEQ, PIECE, HD)
 TWO_PIECES = (N_SEQ, 2 * PIECE, HD)
-SENT_PIECES = (N_SEQ, PIECE + 16, HD)
+SENT_PIECES = (N_SEQ, PIECE + PACK, HD)
 CUM = (ROWS, HD)
-FAR = 160
+FAR = 100
 
 
 def call(kernel, name, in_specs, outs, scratch, semaphores, mib, flops, moved, aliases=None):
@@ -491,12 +499,13 @@
 
 def summarize(decay_rows, keys, values):
     return call(
-        summary_kernel, "summary", [VMEM, HBM, HBM],
-        [
-            (VMEM, shape(SENT_PIECES, BF16)), (VMEM, shape(STATE, F32)),
+        summary_kernel, "summary", [HBM, HBM, HBM],
+        [
+            (HBM, shape(SENT_PIECES, BF16)), (VMEM, shape(STATE, F32)),
             (VMEM, shape((HL, ROWS), F32)), (VMEM, shape((HL, 8, HD), F32)),
         ],
-        [(HEAD_PROMPT, BF16), (HEAD_PROMPT, BF16)], [2], 52, 3e8, 4,
+        [(HEAD_PROMPT, BF16), (HEAD_PROMPT, BF16), ((1, HL, ROWS), F32), (SENT_PIECES, BF16)],
+        [2, 1, 1], 52, 3e8, 4,
     )(decay_rows, keys, values)
 
 
@@ -505,9 +514,10 @@
         within_kernel, "within", [VMEM] + [HBM] * 3,
         [
             (HBM, shape((FAR, ROWS, HD), BF16)), (HBM, shape(HEAD_PROMPT, BF16)),
-            (VMEM, shape((8, HD), F32)),
-        ],
-        [(HEAD_ROWS, BF16)] * 5 + [(HEAD_PROMPT, BF16)], [3, 3], 52, 4e9, 16,
+            (HBM, shape((FAR // 2, ROWS, BLK), BF16)), (VMEM, shape((8, HD), F32)),
+        ],
+        [(HEAD_ROWS, BF16)] * 5 + [(HEAD_PROMPT, BF16), ((HL, ROWS, BLK), BF16)],
+        [3, 4], 52, 4e9, 16,
     )(cum_rows, queries, keys, values)
 
 
@@ -528,7 +538,7 @@
             (HBM, shape((6 * FAR, HD, HD), BF16)),
         ],
         [(HEAD_ROWS, BF16), ((HL * BLOCKS, HD, HD), BF16), (CUM, F32), (CUM, F32)],
-        [2, 2], 36, 3e8, 10,
+        [2, 2], 46, 3e8, 10,
     )(ends, gains, d_out, starts, term, within)
 
 
@@ -539,24 +549,27 @@
     )(ends, gains, stats, scaled_queries, d_out, attended)[0]
 
 
-def local_grads(cum_rows, stats, gains, queries, keys, values, d_out, attended, states):
-    return call(
-        local_grads_kernel, "local_grads", [VMEM] * 3 + [HBM] * 6,
+def local_grads(
+    cum_rows, stats, gains, queries, keys, values, d_out, attended, states, weights
+):
+    return call(
+        local_grads_kernel, "local_grads", [VMEM] * 3 + [HBM] * 7,
         [
             (HBM, WIDE), (HBM, WIDE), (HBM, WIDE), (HBM, WIDE),
             (HBM, shape((4 * FAR, HD, HD), F32)), (VMEM, shape((8, HD), F32)),
         ],
-        [(HEAD_ROWS, BF16)] * 5 + [((HL * BLOCKS, HD, HD), BF16)] + [(HEAD_ROWS, BF16)] * 4
+        [(HEAD_ROWS, BF16)] * 5 + [((HL * BLOCKS, HD, HD), BF16), ((HL, ROWS, BLK), BF16)]
+        + [(HEAD_ROWS, BF16)] * 4
         + [(STATE, F32), (CUM, F32), (CUM, F32)],
-        [6, 5], 53, 6e9, 24,
-    )(cum_rows, stats, gains, queries, keys, values, d_out, attended, states)
+        [7, 5], 53, 6e9, 24,
+    )(cum_rows, stats, gains, queries, keys, values, d_out, attended, states, weights)
 
 
 def far_grads(cum_rows, ends, far, scaled_keys, values, term, near_keys, near_values):
     return call(
         far_grads_kernel, "far_grads", [VMEM] * 5 + [HBM] * 3,
         [(HBM, WIDE), (HBM, WIDE)],
-        [(STATE, F32)] + [(HEAD_PROMPT, BF16)] * 4, [3, 2], 36, 3e8, 10, {6: 0, 7: 1},
+        [(STATE, F32)] + [(HEAD_PROMPT, BF16)] * 4, [3, 2], 44, 3e8, 10, {6: 0, 7: 1},
     )(cum_rows, ends, far, scaled_keys, values, term, near_keys, near_values)
 
 
@@ -576,7 +589,7 @@
     decay_rows = jnp.swapaxes(log_decay, 1, 2)
     send, first_term, cum_rows, block_ends = summarize(decay_rows, keys, values)
     got = everyone(send, "seq")
-    within, scaled_keys, done = inside(cum_rows, queries, keys, values)
+    within, scaled_keys, weights, done = inside(cum_rows, queries, keys, values)
     send, decays = forward_scan(parents, got, done)
     starts = everyone(send, "seq")
     near_queries, attended, stats, kept, states = attend(
@@ -586,7 +599,7 @@
     send = grads(block_ends, gains, stats, near_queries, d_out, attended)
     got = everyone(send, "seq")
     out, d_queries, d_keys, d_values, last_term, done = local_grads(
-        cum_rows, stats, gains, queries, keys, values, d_out, kept, states
+        cum_rows, stats, gains, queries, keys, values, d_out, kept, states, weights
     )
     far = everyone(backward_scan(got, decays, done), "seq")
     d_keys, d_values = far_grads(

time: 113 us -> 113 us (level)
    pallas_call x1, Pallas kernels: 6.82 us -> 9.65 us  [inside(): call(within_kernel, 'within', [VMEM] + [HBM] * 3, [(HBM, shape((FAR, ROWS...]
    pallas_call x2, Pallas kernels: 16.3 us -> 13.9 us  [the longest x1 10.9 us: local_grads(): call(local_grads_kernel, 'local_grads', [VMEM] * 3 + [HBM] * 7, [(HBM, WI...]
where the time goes in v7:
time: 113 us; the launch traced here: 112 us
  blocking collectives  48.6 us (43%)
  Pallas kernels  34.5 us (31%)
  starting transfers between devices  16.1 us (14%)
  waiting for transfers between devices  10.8 us (10%)
  local copies, waits for them, and re-layouts  1.74 us (2%)
    all_to_all x3, blocking collectives, everyone(): return lax.all_to_all(array, axis, 0, 0, tiled=True)  48.6 us
    all_to_all x2, starting transfers between devices, everyone(): return lax.all_to_all(array, axis, 0, 0, tiled=True)  16.1 us
    pallas_call x1, Pallas kernels, local_grads(): call(local_grads_kernel, 'local_grads', [VMEM] * 3 + [HBM] * 7, [(HBM, WI...  10.9 us
    all_to_all x2, waiting for transfers between devices, everyone(): return lax.all_to_all(array, axis, 0, 0, tiled=True)  10.8 us
    pallas_call x1, Pallas kernels, inside(): call(within_kernel, 'within', [VMEM] + [HBM] * 3, [(HBM, shape((FAR, ROWS...  9.65 us
    pallas_call x1, Pallas kernels, attend(): call(attend_kernel, 'attend', [VMEM] * 5 + [HBM], [(VMEM, shape(HEAD_ROWS...  4.14 us
    pallas_call x1, Pallas kernels, far_grads(): call(far_grads_kernel, 'far_grads', [VMEM] * 5 + [HBM] * 3, [(HBM, WIDE),...  3.6 us
    pallas_call x1, Pallas kernels, summarize(): call(summary_kernel, 'summary', [HBM, HBM, HBM], [(HBM, shape(SENT_PIECES...  3.08 us
  transfers between devices with their start and end apart: 2, of which 2 were waited for; matrix products, arithmetic and copies ran while one was open for 0% of the time, Pallas kernels for 18%

profile of v7, /device:TPU:32, one launch (start us, length us, event | category | flops | bytes accessed | tf_op | source)
XLA Modules:
  0.0 112.5 jit_solution(12748389346131616428)
XLA Ops:
  0.6 0.0 copy-start.5
  0.6 0.7 copy-done.5
  1.4 3.1 %summary.1 = (bf16[32,48,128]{2,1,0:T(8,128)(2,1)}, f32[8,128,128]{2,1,0:T(8,128)S(1)}, f32[8,768]{1,0:T(8,128)S(1)}, f32[8,8,128]{2,1,0:T(8,128)S(1)}) custom-call(f32[1,8,768]{2,1,0:T(8,128)S(1)} %bitcast.5, bf16[1,768,1024]{2,1,0:T(8,128)(2,1)} %keys_ref.5, bf16[1,768,1024]{2,1,0:T(8,128)(2,1)} %values_ref.7), custom_call_target="tpu_custom_call" | custom-call | flops 300000000 | bytes 4194304 | tf_op jit(solution)/shard_map/summary/pallas_call | solution.py:501
  4.5 11.2 %all-to-all-start = ((bf16[32,48,128]{2,1,0:T(8,128)(2,1)}), bf16[32,48,128]{2,1,0:T(8,128)(2,1)S(1)}, u32[]{:S(2)}, u32[]{:S(2)}) async-start(bf16[32,48,128]{2,1,0:T(8,128)(2,1)} %get-tuple-element.29), calls=%async_computation | async-start | bytes 786432 | tf_op jit(solution)/shard_map/all_to_all | solution.py:584
  15.7 0.0 copy-start.6
  15.7 0.0 copy-start.1
  15.7 0.0 copy-start.4
  15.7 9.6 %within.1 = (bf16[100,768,128]{2,1,0:T(8,128)(2,1)}, bf16[8,512,128]{2,1,0:T(8,128)(2,1)S(1)}, bf16[50,768,256]{2,1,0:T(8,128)(2,1)}, f32[8,128]{1,0:T(8,128)S(1)}) custom-call(f32[8,768]{1,0:T(8,128)S(1)} %get-tuple-element.27.cum_rows_ref, bf16[1,768,1024]{2,1,0:T(8,128)(2,1)} %queries_ref.3, bf16[1,768,1024]{2,1,0:T(8,128)(2,1)} %keys_ref.5, ...), custom_call_target="tpu_custom_call" | custom-call | flops 4000000000 | bytes 16777216 | tf_op jit(solution)/shard_map/within/pallas_call | solution.py:513
  25.3 0.0 copy-start.2
  25.4 1.0 copy-done.2
  26.3 4.2 %all-to-all-done.got_ref = bf16[32,48,128]{2,1,0:T(8,128)(2,1)S(1)} async-done(((bf16[32,48,128]{2,1,0:T(8,128)(2,1)}), bf16[32,48,128]{2,1,0:T(8,128)(2,1)S(1)}, u32[]{:S(2)}, u32[]{:S(2)}) %all-to-all-start) | async-done | bytes 393248 | tf_op jit(solution)/shard_map/all_to_all | solution.py:584
  30.5 0.0 copy-done.6
  30.5 0.7 forward_scan.1
  31.3 22.5 %all_to_all.25.starts_ref = bf16[32,64,128]{2,1,0:T(8,128)(2,1)S(1)} all-to-all(bf16[32,64,128]{2,1,0:T(8,128)(2,1)S(1)} %get-tuple-element.31), channel_id=1, replica_groups=mesh['seq'=32,'head'=8] {'seq'}, dimensions={0} | all-to-all | bytes 1048576 | tf_op jit(solution)/shard_map/all_to_all | solution.py:584
  53.7 0.0 copy-done.1
  53.7 0.0 copy-done.4
  53.7 4.1 %attend.1 = (bf16[8,768,128]{2,1,0:T(8,128)(2,1)S(1)}, bf16[8,768,128]{2,1,0:T(8,128)(2,1)S(1)}, f32[8,16,128]{2,1,0:T(8,128)S(1)}, bf16[100,768,128]{2,1,0:T(8,128)(2,1)}, bf16[600,128,128]{2,1,0:T(8,128)(2,1)}) custom-call(f32[8,8,128]{2,1,0:T(8,128)S(1)} %get-tuple-element.28.ends_ref, f32[8,128]{1,0:T(8,128)S(1)} %bitcast.2, ...), custom_call_target="tpu_custom_call" | custom-call | flops 300000000 | bytes 10485760 | tf_op jit(solution)/shard_map/attend/pallas_call | solution.py:533
  57.9 9.9 %all_to_all.26.stats_ref = f32[8,16,128]{2,1,0:T(8,128)S(1)} all-to-all(f32[8,16,128]{2,1,0:T(8,128)S(1)} %get-tuple-element.34), channel_id=1, replica_groups=mesh['seq'=32,'head'=8] {'head'}, dimensions={0} | all-to-all | bytes 131072 | tf_op jit(solution)/shard_map/all_to_all | solution.py:584
  67.8 2.2 %grad.1 = bf16[32,64,128]{2,1,0:T(8,128)(2,1)} custom-call(f32[8,8,128]{2,1,0:T(8,128)S(1)} %get-tuple-element.28.ends_ref, f32[8,128]{1,0:T(8,128)S(1)} %bitcast.3, f32[8,16,128]{2,1,0:T(8,128)S(1)} %all_to_all.26.stats_ref, bf16[8,768,128]{2,1,0:T(8,128)(2,1)S(1)} %get-tuple-element.40.queries_ref, bf16[1,768,1024]{2,1,0:T(8,128)(2,1)S(1)} %copy-done.1, ...), custom_call_target="tpu_custom_call" | custom-call | flops 300000000 | bytes 10485760 | tf_op jit(solution)/shard_map/grad/pallas_call | solution.py:546
  70.0 4.9 %all-to-all-start.3 = ((bf16[32,64,128]{2,1,0:T(8,128)(2,1)}), bf16[32,64,128]{2,1,0:T(8,128)(2,1)S(1)}, u32[]{:S(2)}, u32[]{:S(2)}) async-start(bf16[32,64,128]{2,1,0:T(8,128)(2,1)} %grad.1), calls=%async_computation.3 | async-start | bytes 1048576 | tf_op jit(solution)/shard_map/all_to_all | solution.py:584
  74.9 0.0 copy-start
  74.9 10.9 %local_grads.1 = (bf16[1,768,1024]{2,1,0:T(8,128)(2,1)}, bf16[1,768,1024]{2,1,0:T(8,128)(2,1)}, bf16[1,768,1024]{2,1,0:T(8,128)(2,1)}, bf16[1,768,1024]{2,1,0:T(...) custom-call(f32[8,768]{1,0:T(8,128)S(1)} %get-tuple-element.27.cum_rows_ref, ...), custom_call_target="tpu_custom_call" | custom-call | flops 6000000000 | bytes 25165824 | tf_op jit(solution)/shard_map/local_grads/pallas_call | solution.py:555
  85.8 0.0 copy-start.3
  85.8 6.6 %all-to-all-done.3.got_ref = bf16[32,64,128]{2,1,0:T(8,128)(2,1)S(1)} async-done(((bf16[32,64,128]{2,1,0:T(8,128)(2,1)}), bf16[32,64,128]{2,1,0:T(8,128)(2,1)S(1)}, u32[]{:S(2)}, u32[]{:S(2)}) %all-to-all-start.3) | async-done | bytes 524320 | tf_op jit(solution)/shard_map/all_to_all | solution.py:584
  92.4 0.2 backward_scan.1
  92.7 16.2 %all_to_all.27.far_ref = bf16[32,32,128]{2,1,0:T(8,128)(2,1)S(1)} all-to-all(bf16[32,32,128]{2,1,0:T(8,128)(2,1)S(1)} %backward_scan.1), channel_id=1, replica_groups=mesh['seq'=32,'head'=8] {'seq'}, dimensions={0} | all-to-all | bytes 524288 | tf_op jit(solution)/shard_map/all_to_all | solution.py:584
  108.9 0.0 copy-done
  108.9 0.0 copy-done.3
  108.9 3.6 %far_grads.1 = (bf16[1,768,1024]{2,1,0:T(8,128)(2,1)}, bf16[1,768,1024]{2,1,0:T(8,128)(2,1)}) custom-call(f32[8,768]{1,0:T(8,128)S(1)} %get-tuple-element.27.cum_rows_ref, f32[8,8,128]{2,1,0:T(8,128)S(1)} %get-tuple-element.28.ends_ref, bf16[32,32,128]{2,1,0:T(8,128)(2,1)S(1)} %all_to_all.27.far_ref, ...), custom_call_target="tpu_custom_call", output_to_operand_aliasing={{0}: (6, {}), {1}: (7, {})} | custom-call | flops 300000000 | bytes 10485760 | tf_op jit(solution)/shard_map/far_grads/pallas_call | solution.py:569
Async XLA Ops:
  0.6 0.7 copy-start.5
  4.5 26.1 %all-to-all-start = ((bf16[32,48,128]{2,1,0:T(8,128)(2,1)}), bf16[32,48,128]{2,1,0:T(8,128)(2,1)S(1)}, u32[]{:S(2)}, u32[]{:S(2)}) async-start(bf16[32,48,128]{2,1,0:T(8,128)(2,1)} %get-tuple-element.29), calls=%async_computation | async-start | bytes 786432 | tf_op jit(solution)/shard_map/all_to_all | solution.py:584
  15.7 14.9 %copy-start.6 = (s32[32]{0:T(128)S(1)}, s32[32]{0:T(128)}, u32[]{:S(2)}) copy-start(s32[32]{0:T(128)} %parents_ref.1) | copy-start | bytes 388
  15.7 38.1 %copy-start.1 = (bf16[1,768,1024]{2,1,0:T(8,128)(2,1)S(1)}, bf16[1,768,1024]{2,1,0:T(8,128)(2,1)}, u32[]{:S(2)}) copy-start(bf16[1,768,1024]{2,1,0:T(8,128)(2,1)} %d_out_ref.5) | copy-start | bytes 4718596
  15.7 38.1 %copy-start.4 = (f32[1024]{0:T(1024)S(1)}, f32[1024]{0:T(1024)}, u32[]{:S(2)}) copy-start(f32[1024]{0:T(1024)} %param.11) | copy-start | bytes 12292
  25.3 1.0 copy-start.2
  70.0 22.4 %all-to-all-start.3 = ((bf16[32,64,128]{2,1,0:T(8,128)(2,1)}), bf16[32,64,128]{2,1,0:T(8,128)(2,1)S(1)}, u32[]{:S(2)}, u32[]{:S(2)}) async-start(bf16[32,64,128]{2,1,0:T(8,128)(2,1)} %grad.1), calls=%async_computation.3 | async-start | bytes 1048576 | tf_op jit(solution)/shard_map/all_to_all | solution.py:584
  74.9 34.0 %copy-start = (bf16[1,768,1024]{2,1,0:T(8,128)(2,1)S(1)}, bf16[1,768,1024]{2,1,0:T(8,128)(2,1)}, u32[]{:S(2)}) copy-start(bf16[1,768,1024]{2,1,0:T(8,128)(2,1)} %values_ref.7) | copy-start | bytes 4718596
  85.8 23.1 %copy-start.3 = (bf16[8,512,128]{2,1,0:T(8,128)(2,1)S(1)}, bf16[8,512,128]{2,1,0:T(8,128)(2,1)}, u32[]{:S(2)}) copy-start(bf16[8,512,128]{2,1,0:T(8,128)(2,1)} %copy-done.2) | copy-start | bytes 3145732

commit v8 on v7

--- a/solution.py
+++ b/solution.py
@@ -188,9 +188,8 @@
 
 def within_kernel(
     cum_rows_ref, queries_ref, keys_ref, values_ref,
-    within_ref, scaled_keys_ref, weights_ref, done_ref,
-    queries_buf, keys_buf, values_buf, within_buf, scaled_queries_buf, scaled_keys_buf,
-    weights_buf, in_sems, out_sems,
+    within_ref, weights_ref, done_ref,
+    queries_buf, keys_buf, values_buf, within_buf, scaled_queries_buf, weights_buf, in_sems, out_sems,
 ):
     fetch = Copies(
         [
@@ -204,7 +203,6 @@
         [
             (of_lead(within_buf), of_lead(within_ref)),
             (of_lead(scaled_queries_buf), of_lead(within_ref, first=HL)),
-            (of_lead(scaled_keys_buf), of_lead(scaled_keys_ref)),
             (of_lead(weights_buf), of_lead(weights_ref)),
         ],
         out_sems,
@@ -225,11 +223,26 @@
             weights_buf[head, part, :] = weights
             within_buf[head, part, :] = mm_tn(weights, values_buf[head, part, :]).astype(BF16)
             scaled_queries_buf[head, part, :] = rounded_product(queries, down(jnp.exp(row)))
-            if number < 2:
-                factor = down(jnp.exp(row[:, BLK - 1 : BLK] - row))
-                scaled_keys_buf[head, part, :] = rounded_product(keys, factor)
 
     over_heads(fetch, body, leave, group=4)
+
+
+def scaled_keys_kernel(
+    cum_rows_ref, keys_ref, _after, scaled_keys_ref, done_ref,
+    keys_buf, scaled_keys_buf, in_sems, out_sems,
+):
+    fetch = Copies([(of_rows(keys_ref, P_DEV), of_lead(keys_buf))], in_sems)
+    leave = Copies([(of_lead(scaled_keys_buf), of_lead(scaled_keys_ref))], out_sems)
+    done_ref[...] = jnp.zeros_like(done_ref)
+
+    def body(head):
+        for number in range(2):
+            part = rows(number)
+            row = cum_rows_ref[pl.ds(head, 1), part]
+            factor = down(jnp.exp(row[:, BLK - 1 : BLK] - row))
+            scaled_keys_buf[head, part, :] = rounded_product(keys_buf[head, part, :], factor)
+
+    over_heads(fetch, body, leave)
 
 
 def forward_scan_kernel(parents_ref, got_ref, _after, send_ref, decay_ref):
@@ -251,7 +264,7 @@
 
 
 def attend_kernel(
-    ends_ref, gain_ref, d_out_ref, starts_ref, term_ref, within_ref,
+    ends_ref, gain_ref, d_out_ref, starts_ref, term_ref, within_ref, _after,
     queries_ref, attended_ref, stats_ref, kept_ref, states_ref,
     within_buf, states_buf, squares_ref, products_ref, in_sems, out_sems,
 ):
@@ -513,12 +526,19 @@
     return call(
         within_kernel, "within", [VMEM] + [HBM] * 3,
         [
-            (HBM, shape((FAR, ROWS, HD), BF16)), (HBM, shape(HEAD_PROMPT, BF16)),
-            (HBM, shape((FAR // 2, ROWS, BLK), BF16)), (VMEM, shape((8, HD), F32)),
-        ],
-        [(HEAD_ROWS, BF16)] * 5 + [(HEAD_PROMPT, BF16), ((HL, ROWS, BLK), BF16)],
-        [3, 4], 52, 4e9, 16,
+            (HBM, shape((FAR, ROWS, HD), BF16)), (HBM, shape((FAR // 2, ROWS, BLK), BF16)),
+            (VMEM, shape((8, HD), F32)),
+        ],
+        [(HEAD_ROWS, BF16)] * 5 + [((HL, ROWS, BLK), BF16)], [3, 3], 53, 4e9, 16,
     )(cum_rows, queries, keys, values)
+
+
+def scale_keys(cum_rows, keys, after):
+    return call(
+        scaled_keys_kernel, "scaled_keys", [VMEM, HBM, HBM],
+        [(HBM, shape(HEAD_PROMPT, BF16)), (VMEM, shape((8, HD), F32))],
+        [(HEAD_PROMPT, BF16)] * 2, [1, 1], 53, 2e9, 8,
+    )(cum_rows, keys, after)
 
 
 def forward_scan(parents, got, after):
@@ -529,9 +549,9 @@
     )(parents, got, after)
 
 
-def attend(ends, gains, d_out, starts, term, within):
-    return call(
-        attend_kernel, "attend", [VMEM] * 5 + [HBM],
+def attend(ends, gains, d_out, starts, term, within, after):
+    return call(
+        attend_kernel, "attend", [VMEM] * 5 + [HBM] * 2,
         [
             (VMEM, shape(HEAD_ROWS, BF16)), (VMEM, shape(HEAD_ROWS, BF16)),
             (VMEM, shape((HL, 16, HD), F32)), (HBM, shape((FAR, ROWS, HD), BF16)),
@@ -539,7 +559,7 @@
         ],
         [(HEAD_ROWS, BF16), ((HL * BLOCKS, HD, HD), BF16), (CUM, F32), (CUM, F32)],
         [2, 2], 46, 3e8, 10,
-    )(ends, gains, d_out, starts, term, within)
+    )(ends, gains, d_out, starts, term, within, after)
 
 
 def grads(ends, gains, stats, scaled_queries, d_out, attended):
@@ -589,11 +609,12 @@
     decay_rows = jnp.swapaxes(log_decay, 1, 2)
     send, first_term, cum_rows, block_ends = summarize(decay_rows, keys, values)
     got = everyone(send, "seq")
-    within, scaled_keys, weights, done = inside(cum_rows, queries, keys, values)
+    within, weights, done = inside(cum_rows, queries, keys, values)
     send, decays = forward_scan(parents, got, done)
     starts = everyone(send, "seq")
+    scaled_keys, done = scale_keys(cum_rows, keys, decays)
     near_queries, attended, stats, kept, states = attend(
-        block_ends, gains, d_out, starts, first_term, within
+        block_ends, gains, d_out, starts, first_term, within, done
     )
     stats = everyone(stats, "head")
     send = grads(block_ends, gains, stats, near_queries, d_out, attended)

time: 113 us -> 113 us (level)
  blocking collectives: 48.6 us -> 26.1 us
  waiting for transfers between devices: 10.8 us -> 28.2 us
  starting transfers between devices: 16.1 us -> 20.8 us
  Pallas kernels: 34.5 us -> 36 us
    all_to_all x3 -> x2, blocking collectives: 48.6 us -> 26.1 us  [everyone(): return lax.all_to_all(array, axis, 0, 0, tiled=True)]
    all_to_all x2 -> x3, waiting for transfers between devices: 10.8 us -> 28.2 us  [everyone(): return lax.all_to_all(array, axis, 0, 0, tiled=True)]
    all_to_all x2 -> x3, starting transfers between devices: 16.1 us -> 20.8 us  [everyone(): return lax.all_to_all(array, axis, 0, 0, tiled=True)]
    pallas_call x1 -> x2, Pallas kernels: 4.14 us -> 7.22 us  [the longest x1 4.13 us: attend(): call(attend_kernel, 'attend', [VMEM] * 5 + [HBM] * 2, [(VMEM, shape(HEAD_...]
    pallas_call x1, Pallas kernels: 9.65 us -> 7.22 us  [inside(): call(within_kernel, 'within', [VMEM] + [HBM] * 3, [(HBM, shape((FAR, ROWS...]
  transfers between devices with their start and end apart: 2 -> 3, of which waited for: 2 -> 3; matrix products, arithmetic and copies ran while one was open for 0% -> 0% of each run, Pallas kernels for 18% -> 19%
where the time goes in v8:
time: 113 us
  Pallas kernels  36 us (32%)
  waiting for transfers between devices  28.2 us (25%)
  blocking collectives  26.1 us (23%)
  starting transfers between devices  20.8 us (18%)
    all_to_all x3, waiting for transfers between devices, everyone(): return lax.all_to_all(array, axis, 0, 0, tiled=True)  28.2 us
    all_to_all x2, blocking collectives, everyone(): return lax.all_to_all(array, axis, 0, 0, tiled=True)  26.1 us
    all_to_all x3, starting transfers between devices, everyone(): return lax.all_to_all(array, axis, 0, 0, tiled=True)  20.8 us
    pallas_call x1, Pallas kernels, local_grads(): call(local_grads_kernel, 'local_grads', [VMEM] * 3 + [HBM] * 7, [(HBM, WI...  10.9 us
    pallas_call x1, Pallas kernels, inside(): call(within_kernel, 'within', [VMEM] + [HBM] * 3, [(HBM, shape((FAR, ROWS...  7.22 us
    pallas_call x1, Pallas kernels, attend(): call(attend_kernel, 'attend', [VMEM] * 5 + [HBM] * 2, [(VMEM, shape(HEAD_...  4.13 us
    pallas_call x1, Pallas kernels, far_grads(): call(far_grads_kernel, 'far_grads', [VMEM] * 5 + [HBM] * 3, [(HBM, WIDE),...  3.59 us
    pallas_call x1, Pallas kernels, scale_keys(): call(scaled_keys_kernel, 'scaled_keys', [VMEM, HBM, HBM], [(HBM, shape(HE...  3.09 us
  transfers between devices with their start and end apart: 3, of which 3 were waited for; matrix products, arithmetic and copies ran while one was open for 0% of the time, Pallas kernels for 19%

profile of v8, /device:TPU:32, one launch (start us, length us, event | category | flops | bytes accessed | tf_op | source)
XLA Modules:
  0.0 112.6 jit_solution(16127557002932919945)
XLA Ops:
  0.6 0.0 copy-start.4
  0.6 0.7 copy-done.4
  1.4 3.1 %summary.1 = (bf16[32,48,128]{2,1,0:T(8,128)(2,1)}, f32[8,128,128]{2,1,0:T(8,128)S(1)}, f32[8,768]{1,0:T(8,128)S(1)}, f32[8,8,128]{2,1,0:T(8,128)S(1)}) custom-call(f32[1,8,768]{2,1,0:T(8,128)S(1)} %bitcast.5, bf16[1,768,1024]{2,1,0:T(8,128)(2,1)} %keys_ref.7, bf16[1,768,1024]{2,1,0:T(8,128)(2,1)} %values_ref.7), custom_call_target="tpu_custom_call" | custom-call | flops 300000000 | bytes 4194304 | tf_op jit(solution)/shard_map/summary/pallas_call | solution.py:514
  4.5 11.2 %all-to-all-start = ((bf16[32,48,128]{2,1,0:T(8,128)(2,1)}), bf16[32,48,128]{2,1,0:T(8,128)(2,1)S(1)}, u32[]{:S(2)}, u32[]{:S(2)}) async-start(bf16[32,48,128]{2,1,0:T(8,128)(2,1)} %get-tuple-element.30), calls=%async_computation | async-start | bytes 786432 | tf_op jit(solution)/shard_map/all_to_all | solution.py:604
  15.7 0.0 copy-start.5
  15.7 7.2 %within.1 = (bf16[100,768,128]{2,1,0:T(8,128)(2,1)}, bf16[50,768,256]{2,1,0:T(8,128)(2,1)}, f32[8,128]{1,0:T(8,128)S(1)}) custom-call(f32[8,768]{1,0:T(8,128)S(1)} %get-tuple-element.28.cum_rows_ref, bf16[1,768,1024]{2,1,0:T(8,128)(2,1)} %queries_ref.3, bf16[1,768,1024]{2,1,0:T(8,128)(2,1)} %keys_ref.7, bf16[1,768,1024]{2,1,0:T(8,128)(2,1)} %values_ref.7), custom_call_target="tpu_custom_call" | custom-call | flops 4000000000 | bytes 16777216 | tf_op jit(solution)/shard_map/within/pallas_call | solution.py:526
  22.9 7.6 %all-to-all-done.got_ref = bf16[32,48,128]{2,1,0:T(8,128)(2,1)S(1)} async-done(((bf16[32,48,128]{2,1,0:T(8,128)(2,1)}), bf16[32,48,128]{2,1,0:T(8,128)(2,1)S(1)}, u32[]{:S(2)}, u32[]{:S(2)}) %all-to-all-start) | async-done | bytes 393248 | tf_op jit(solution)/shard_map/all_to_all | solution.py:604
  30.5 0.0 copy-done.5
  30.5 1.5 %forward_scan.1 = (bf16[32,64,128]{2,1,0:T(8,128)(2,1)}, f32[64,128]{1,0:T(8,128)S(1)}) custom-call(s32[32]{0:T(128)S(1)} %copy-done.5, bf16[32,48,128]{2,1,0:T(8,128)(2,1)S(1)} %all-to-all-done.got_ref, f32[8,128]{1,0:T(8,128)S(1)} %get-tuple-element.31._after), custom_call_target="tpu_custom_call" | custom-call | flops 1000000 | bytes 1048576 | tf_op jit(solution)/shard_map/forward_scan/pallas_call | solution.py:545
  32.1 4.8 %all-to-all-start.1 = ((bf16[32,64,128]{2,1,0:T(8,128)(2,1)}), bf16[32,64,128]{2,1,0:T(8,128)(2,1)S(1)}, u32[]{:S(2)}, u32[]{:S(2)}) async-start(bf16[32,64,128]{2,1,0:T(8,128)(2,1)} %get-tuple-element.32), calls=%async_computation.1 | async-start | bytes 1048576 | tf_op jit(solution)/shard_map/all_to_all | solution.py:604
  36.9 0.0 copy-start.1
  36.9 0.0 copy-start.3
  36.9 3.1 %scaled_keys.1 = (bf16[8,512,128]{2,1,0:T(8,128)(2,1)}, f32[8,128]{1,0:T(8,128)S(1)}) custom-call(f32[8,768]{1,0:T(8,128)S(1)} %get-tuple-element.28.cum_rows_ref, bf16[1,768,1024]{2,1,0:T(8,128)(2,1)} %keys_ref.7, f32[64,128]{1,0:T(8,128)S(1)} %get-tuple-element.35._after.decay_ref), custom_call_target="tpu_custom_call" | custom-call | flops 2000000000 | bytes 8388608 | tf_op jit(solution)/shard_map/scaled_keys/pallas_call | solution.py:537
  40.0 14.0 %all-to-all-done.1.starts_ref = bf16[32,64,128]{2,1,0:T(8,128)(2,1)S(1)} async-done(((bf16[32,64,128]{2,1,0:T(8,128)(2,1)}), bf16[32,64,128]{2,1,0:T(8,128)(2,1)S(1)}, u32[]{:S(2)}, u32[]{:S(2)}) %all-to-all-start.1) | async-done | bytes 524320 | tf_op jit(solution)/shard_map/all_to_all | solution.py:604
  53.9 0.0 copy-done.1
  53.9 0.0 copy-done.3
  53.9 4.1 %attend.1 = (bf16[8,768,128]{2,1,0:T(8,128)(2,1)S(1)}, bf16[8,768,128]{2,1,0:T(8,128)(2,1)S(1)}, f32[8,16,128]{2,1,0:T(8,128)S(1)}, bf16[100,768,128]{2,1,0:T(8,128)(2,1)}, bf16[600,128,128]{2,1,0:T(8,128)(2,1)}) custom-call(f32[8,8,128]{2,1,0:T(8,128)S(1)} %get-tuple-element.29.ends_ref, f32[8,128]{1,0:T(8,128)S(1)} %bitcast.2, ...), custom_call_target="tpu_custom_call" | custom-call | flops 300000000 | bytes 10485760 | tf_op jit(solution)/shard_map/attend/pallas_call | solution.py:553
  58.1 9.9 %all_to_all.25.stats_ref = f32[8,16,128]{2,1,0:T(8,128)S(1)} all-to-all(f32[8,16,128]{2,1,0:T(8,128)S(1)} %get-tuple-element.37), channel_id=1, replica_groups=mesh['seq'=32,'head'=8] {'head'}, dimensions={0} | all-to-all | bytes 131072 | tf_op jit(solution)/shard_map/all_to_all | solution.py:604
  68.0 2.2 %grad.1 = bf16[32,64,128]{2,1,0:T(8,128)(2,1)} custom-call(f32[8,8,128]{2,1,0:T(8,128)S(1)} %get-tuple-element.29.ends_ref, f32[8,128]{1,0:T(8,128)S(1)} %bitcast.3, f32[8,16,128]{2,1,0:T(8,128)S(1)} %all_to_all.25.stats_ref, bf16[8,768,128]{2,1,0:T(8,128)(2,1)S(1)} %get-tuple-element.43.queries_ref, bf16[1,768,1024]{2,1,0:T(8,128)(2,1)S(1)} %copy-done.1, ...), custom_call_target="tpu_custom_call" | custom-call | flops 300000000 | bytes 10485760 | tf_op jit(solution)/shard_map/grad/pallas_call | solution.py:566
  70.2 4.9 %all-to-all-start.3 = ((bf16[32,64,128]{2,1,0:T(8,128)(2,1)}), bf16[32,64,128]{2,1,0:T(8,128)(2,1)S(1)}, u32[]{:S(2)}, u32[]{:S(2)}) async-start(bf16[32,64,128]{2,1,0:T(8,128)(2,1)} %grad.1), calls=%async_computation.3 | async-start | bytes 1048576 | tf_op jit(solution)/shard_map/all_to_all | solution.py:604
  75.1 0.0 copy-start
  75.1 10.9 %local_grads.1 = (bf16[1,768,1024]{2,1,0:T(8,128)(2,1)}, bf16[1,768,1024]{2,1,0:T(8,128)(2,1)}, bf16[1,768,1024]{2,1,0:T(8,128)(2,1)}, bf16[1,768,1024]{2,1,0:T(...) custom-call(f32[8,768]{1,0:T(8,128)S(1)} %get-tuple-element.28.cum_rows_ref, ...), custom_call_target="tpu_custom_call" | custom-call | flops 6000000000 | bytes 25165824 | tf_op jit(solution)/shard_map/local_grads/pallas_call | solution.py:575
  86.0 0.0 copy-start.2
  86.0 6.6 %all-to-all-done.3.got_ref = bf16[32,64,128]{2,1,0:T(8,128)(2,1)S(1)} async-done(((bf16[32,64,128]{2,1,0:T(8,128)(2,1)}), bf16[32,64,128]{2,1,0:T(8,128)(2,1)S(1)}, u32[]{:S(2)}, u32[]{:S(2)}) %all-to-all-start.3) | async-done | bytes 524320 | tf_op jit(solution)/shard_map/all_to_all | solution.py:604
  92.6 0.2 backward_scan.1
  92.8 16.2 %all_to_all.26.far_ref = bf16[32,32,128]{2,1,0:T(8,128)(2,1)S(1)} all-to-all(bf16[32,32,128]{2,1,0:T(8,128)(2,1)S(1)} %backward_scan.1), channel_id=1, replica_groups=mesh['seq'=32,'head'=8] {'seq'}, dimensions={0} | all-to-all | bytes 524288 | tf_op jit(solution)/shard_map/all_to_all | solution.py:604
  109.0 0.0 copy-done
  109.0 0.0 copy-done.2
  109.0 3.6 %far_grads.1 = (bf16[1,768,1024]{2,1,0:T(8,128)(2,1)}, bf16[1,768,1024]{2,1,0:T(8,128)(2,1)}) custom-call(f32[8,768]{1,0:T(8,128)S(1)} %get-tuple-element.28.cum_rows_ref, f32[8,8,128]{2,1,0:T(8,128)S(1)} %get-tuple-element.29.ends_ref, bf16[32,32,128]{2,1,0:T(8,128)(2,1)S(1)} %all_to_all.26.far_ref, ...), custom_call_target="tpu_custom_call", output_to_operand_aliasing={{0}: (6, {}), {1}: (7, {})} | custom-call | flops 300000000 | bytes 10485760 | tf_op jit(solution)/shard_map/far_grads/pallas_call | solution.py:589
Async XLA Ops:
  0.6 0.7 copy-start.4
  4.5 26.1 %all-to-all-start = ((bf16[32,48,128]{2,1,0:T(8,128)(2,1)}), bf16[32,48,128]{2,1,0:T(8,128)(2,1)S(1)}, u32[]{:S(2)}, u32[]{:S(2)}) async-start(bf16[32,48,128]{2,1,0:T(8,128)(2,1)} %get-tuple-element.30), calls=%async_computation | async-start | bytes 786432 | tf_op jit(solution)/shard_map/all_to_all | solution.py:604
  15.7 14.9 %copy-start.5 = (s32[32]{0:T(128)S(1)}, s32[32]{0:T(128)}, u32[]{:S(2)}) copy-start(s32[32]{0:T(128)} %parents_ref.1) | copy-start | bytes 388
  32.1 21.9 %all-to-all-start.1 = ((bf16[32,64,128]{2,1,0:T(8,128)(2,1)}), bf16[32,64,128]{2,1,0:T(8,128)(2,1)S(1)}, u32[]{:S(2)}, u32[]{:S(2)}) async-start(bf16[32,64,128]{2,1,0:T(8,128)(2,1)} %get-tuple-element.32), calls=%async_computation.1 | async-start | bytes 1048576 | tf_op jit(solution)/shard_map/all_to_all | solution.py:604
  36.9 17.1 %copy-start.1 = (bf16[1,768,1024]{2,1,0:T(8,128)(2,1)S(1)}, bf16[1,768,1024]{2,1,0:T(8,128)(2,1)}, u32[]{:S(2)}) copy-start(bf16[1,768,1024]{2,1,0:T(8,128)(2,1)} %d_out_ref.5) | copy-start | bytes 4718596
  36.9 17.1 %copy-start.3 = (f32[1024]{0:T(1024)S(1)}, f32[1024]{0:T(1024)}, u32[]{:S(2)}) copy-start(f32[1024]{0:T(1024)} %param.11) | copy-start | bytes 12292
  70.2 22.4 %all-to-all-start.3 = ((bf16[32,64,128]{2,1,0:T(8,128)(2,1)}), bf16[32,64,128]{2,1,0:T(8,128)(2,1)S(1)}, u32[]{:S(2)}, u32[]{:S(2)}) async-start(bf16[32,64,128]{2,1,0:T(8,128)(2,1)} %grad.1), calls=%async_computation.3 | async-start | bytes 1048576 | tf_op jit(solution)/shard_map/all_to_all | solution.py:604
  75.1 34.0 %copy-start = (bf16[1,768,1024]{2,1,0:T(8,128)(2,1)S(1)}, bf16[1,768,1024]{2,1,0:T(8,128)(2,1)}, u32[]{:S(2)}) copy-start(bf16[1,768,1024]{2,1,0:T(8,128)(2,1)} %values_ref.7) | copy-start | bytes 4718596
  86.0 23.1 %copy-start.2 = (bf16[8,512,128]{2,1,0:T(8,128)(2,1)S(1)}, bf16[8,512,128]{2,1,0:T(8,128)(2,1)}, u32[]{:S(2)}) copy-start(bf16[8,512,128]{2,1,0:T(8,128)(2,1)} %get-tuple-element.46.scaled_keys_ref) | copy-start | bytes 3145732

commit v9 on v7

--- a/solution.py
+++ b/solution.py
@@ -17,7 +17,7 @@
 COLS = HL * HD
 PIECE = HL * HD // N_SEQ
 PARTS = HD // PIECE
-PACK = 16
+PACK = 8
 BLOCKS = ROWS // BLK
 TILES = ROWS // HD
 EPS = 1e-05

time: 113 us -> 113 us (level)
  waiting for transfers between devices: 10.8 us -> 9.54 us
  blocking collectives: 48.6 us -> 49.8 us
    all_to_all x2, waiting for transfers between devices: 10.8 us -> 9.54 us  [everyone(): return lax.all_to_all(array, axis, 0, 0, tiled=True)]
    all_to_all x3, blocking collectives: 48.6 us -> 49.8 us  [everyone(): return lax.all_to_all(array, axis, 0, 0, tiled=True)]
where the time goes in v9:
time: 113 us; the launch traced here: 112 us
  blocking collectives  49.8 us (44%)
  Pallas kernels  34.5 us (31%)
  starting transfers between devices  16.1 us (14%)
  waiting for transfers between devices  9.54 us (8%)
  local copies, waits for them, and re-layouts  1.74 us (2%)
    all_to_all x3, blocking collectives, everyone(): return lax.all_to_all(array, axis, 0, 0, tiled=True)  49.8 us
    all_to_all x2, starting transfers between devices, everyone(): return lax.all_to_all(array, axis, 0, 0, tiled=True)  16.1 us
    pallas_call x1, Pallas kernels, local_grads(): call(local_grads_kernel, 'local_grads', [VMEM] * 3 + [HBM] * 7, [(HBM, WI...  10.9 us
    pallas_call x1, Pallas kernels, inside(): call(within_kernel, 'within', [VMEM] + [HBM] * 3, [(HBM, shape((FAR, ROWS...  9.65 us
    all_to_all x2, waiting for transfers between devices, everyone(): return lax.all_to_all(array, axis, 0, 0, tiled=True)  9.54 us
    pallas_call x1, Pallas kernels, attend(): call(attend_kernel, 'attend', [VMEM] * 5 + [HBM], [(VMEM, shape(HEAD_ROWS...  4.14 us
    pallas_call x1, Pallas kernels, far_grads(): call(far_grads_kernel, 'far_grads', [VMEM] * 5 + [HBM] * 3, [(HBM, WIDE),...  3.6 us
    pallas_call x1, Pallas kernels, summarize(): call(summary_kernel, 'summary', [HBM, HBM, HBM], [(HBM, shape(SENT_PIECES...  3.07 us
  transfers between devices with their start and end apart: 2, of which 2 were waited for; matrix products, arithmetic and copies ran while one was open for 0% of the time, Pallas kernels for 18%

profile of v9, /device:TPU:32, one launch (start us, length us, event | category | flops | bytes accessed | tf_op | source)
XLA Modules:
  0.0 112.5 jit_solution(9668602159392934886)
XLA Ops:
  0.6 0.0 copy-start.5
  0.6 0.7 copy-done.5
  1.4 3.1 %summary.1 = (bf16[32,40,128]{2,1,0:T(8,128)(2,1)}, f32[8,128,128]{2,1,0:T(8,128)S(1)}, f32[8,768]{1,0:T(8,128)S(1)}, f32[8,8,128]{2,1,0:T(8,128)S(1)}) custom-call(f32[1,8,768]{2,1,0:T(8,128)S(1)} %bitcast.5, bf16[1,768,1024]{2,1,0:T(8,128)(2,1)} %keys_ref.5, bf16[1,768,1024]{2,1,0:T(8,128)(2,1)} %values_ref.7), custom_call_target="tpu_custom_call" | custom-call | flops 300000000 | bytes 4194304 | tf_op jit(solution)/shard_map/summary/pallas_call | solution.py:501
  4.4 11.2 %all-to-all-start = ((bf16[32,40,128]{2,1,0:T(8,128)(2,1)}), bf16[32,40,128]{2,1,0:T(8,128)(2,1)S(1)}, u32[]{:S(2)}, u32[]{:S(2)}) async-start(bf16[32,40,128]{2,1,0:T(8,128)(2,1)} %get-tuple-element.29), calls=%async_computation | async-start | bytes 655360 | tf_op jit(solution)/shard_map/all_to_all | solution.py:584
  15.6 0.0 copy-start.6
  15.7 0.0 copy-start.1
  15.7 0.0 copy-start.4
  15.7 9.7 %within.1 = (bf16[100,768,128]{2,1,0:T(8,128)(2,1)}, bf16[8,512,128]{2,1,0:T(8,128)(2,1)S(1)}, bf16[50,768,256]{2,1,0:T(8,128)(2,1)}, f32[8,128]{1,0:T(8,128)S(1)}) custom-call(f32[8,768]{1,0:T(8,128)S(1)} %get-tuple-element.27.cum_rows_ref, bf16[1,768,1024]{2,1,0:T(8,128)(2,1)} %queries_ref.3, bf16[1,768,1024]{2,1,0:T(8,128)(2,1)} %keys_ref.5, ...), custom_call_target="tpu_custom_call" | custom-call | flops 4000000000 | bytes 16777216 | tf_op jit(solution)/shard_map/within/pallas_call | solution.py:513
  25.3 0.0 copy-start.2
  25.4 1.0 copy-done.2
  26.3 2.9 %all-to-all-done.got_ref = bf16[32,40,128]{2,1,0:T(8,128)(2,1)S(1)} async-done(((bf16[32,40,128]{2,1,0:T(8,128)(2,1)}), bf16[32,40,128]{2,1,0:T(8,128)(2,1)S(1)}, u32[]{:S(2)}, u32[]{:S(2)}) %all-to-all-start) | async-done | bytes 327712 | tf_op jit(solution)/shard_map/all_to_all | solution.py:584
  29.2 0.0 copy-done.6
  29.2 0.7 forward_scan.1
  30.0 23.7 %all_to_all.25.starts_ref = bf16[32,64,128]{2,1,0:T(8,128)(2,1)S(1)} all-to-all(bf16[32,64,128]{2,1,0:T(8,128)(2,1)S(1)} %get-tuple-element.31), channel_id=1, replica_groups=mesh['seq'=32,'head'=8] {'seq'}, dimensions={0} | all-to-all | bytes 1048576 | tf_op jit(solution)/shard_map/all_to_all | solution.py:584
  53.7 0.0 copy-done.1
  53.7 0.0 copy-done.4
  53.7 4.1 %attend.1 = (bf16[8,768,128]{2,1,0:T(8,128)(2,1)S(1)}, bf16[8,768,128]{2,1,0:T(8,128)(2,1)S(1)}, f32[8,16,128]{2,1,0:T(8,128)S(1)}, bf16[100,768,128]{2,1,0:T(8,128)(2,1)}, bf16[600,128,128]{2,1,0:T(8,128)(2,1)}) custom-call(f32[8,8,128]{2,1,0:T(8,128)S(1)} %get-tuple-element.28.ends_ref, f32[8,128]{1,0:T(8,128)S(1)} %bitcast.2, ...), custom_call_target="tpu_custom_call" | custom-call | flops 300000000 | bytes 10485760 | tf_op jit(solution)/shard_map/attend/pallas_call | solution.py:533
  57.9 9.9 %all_to_all.26.stats_ref = f32[8,16,128]{2,1,0:T(8,128)S(1)} all-to-all(f32[8,16,128]{2,1,0:T(8,128)S(1)} %get-tuple-element.34), channel_id=1, replica_groups=mesh['seq'=32,'head'=8] {'head'}, dimensions={0} | all-to-all | bytes 131072 | tf_op jit(solution)/shard_map/all_to_all | solution.py:584
  67.8 2.2 %grad.1 = bf16[32,64,128]{2,1,0:T(8,128)(2,1)} custom-call(f32[8,8,128]{2,1,0:T(8,128)S(1)} %get-tuple-element.28.ends_ref, f32[8,128]{1,0:T(8,128)S(1)} %bitcast.3, f32[8,16,128]{2,1,0:T(8,128)S(1)} %all_to_all.26.stats_ref, bf16[8,768,128]{2,1,0:T(8,128)(2,1)S(1)} %get-tuple-element.40.queries_ref, bf16[1,768,1024]{2,1,0:T(8,128)(2,1)S(1)} %copy-done.1, ...), custom_call_target="tpu_custom_call" | custom-call | flops 300000000 | bytes 10485760 | tf_op jit(solution)/shard_map/grad/pallas_call | solution.py:546
  70.0 4.9 %all-to-all-start.3 = ((bf16[32,64,128]{2,1,0:T(8,128)(2,1)}), bf16[32,64,128]{2,1,0:T(8,128)(2,1)S(1)}, u32[]{:S(2)}, u32[]{:S(2)}) async-start(bf16[32,64,128]{2,1,0:T(8,128)(2,1)} %grad.1), calls=%async_computation.3 | async-start | bytes 1048576 | tf_op jit(solution)/shard_map/all_to_all | solution.py:584
  74.9 0.0 copy-start
  74.9 10.9 %local_grads.1 = (bf16[1,768,1024]{2,1,0:T(8,128)(2,1)}, bf16[1,768,1024]{2,1,0:T(8,128)(2,1)}, bf16[1,768,1024]{2,1,0:T(8,128)(2,1)}, bf16[1,768,1024]{2,1,0:T(...) custom-call(f32[8,768]{1,0:T(8,128)S(1)} %get-tuple-element.27.cum_rows_ref, ...), custom_call_target="tpu_custom_call" | custom-call | flops 6000000000 | bytes 25165824 | tf_op jit(solution)/shard_map/local_grads/pallas_call | solution.py:555
  85.8 0.0 copy-start.3
  85.8 6.6 %all-to-all-done.3.got_ref = bf16[32,64,128]{2,1,0:T(8,128)(2,1)S(1)} async-done(((bf16[32,64,128]{2,1,0:T(8,128)(2,1)}), bf16[32,64,128]{2,1,0:T(8,128)(2,1)S(1)}, u32[]{:S(2)}, u32[]{:S(2)}) %all-to-all-start.3) | async-done | bytes 524320 | tf_op jit(solution)/shard_map/all_to_all | solution.py:584
  92.4 0.2 backward_scan.1
  92.6 16.2 %all_to_all.27.far_ref = bf16[32,32,128]{2,1,0:T(8,128)(2,1)S(1)} all-to-all(bf16[32,32,128]{2,1,0:T(8,128)(2,1)S(1)} %backward_scan.1), channel_id=1, replica_groups=mesh['seq'=32,'head'=8] {'seq'}, dimensions={0} | all-to-all | bytes 524288 | tf_op jit(solution)/shard_map/all_to_all | solution.py:584
  108.9 0.0 copy-done
  108.9 0.0 copy-done.3
  108.9 3.6 %far_grads.1 = (bf16[1,768,1024]{2,1,0:T(8,128)(2,1)}, bf16[1,768,1024]{2,1,0:T(8,128)(2,1)}) custom-call(f32[8,768]{1,0:T(8,128)S(1)} %get-tuple-element.27.cum_rows_ref, f32[8,8,128]{2,1,0:T(8,128)S(1)} %get-tuple-element.28.ends_ref, bf16[32,32,128]{2,1,0:T(8,128)(2,1)S(1)} %all_to_all.27.far_ref, ...), custom_call_target="tpu_custom_call", output_to_operand_aliasing={{0}: (6, {}), {1}: (7, {})} | custom-call | flops 300000000 | bytes 10485760 | tf_op jit(solution)/shard_map/far_grads/pallas_call | solution.py:569
Async XLA Ops:
  0.6 0.7 copy-start.5
  4.4 24.8 %all-to-all-start = ((bf16[32,40,128]{2,1,0:T(8,128)(2,1)}), bf16[32,40,128]{2,1,0:T(8,128)(2,1)S(1)}, u32[]{:S(2)}, u32[]{:S(2)}) async-start(bf16[32,40,128]{2,1,0:T(8,128)(2,1)} %get-tuple-element.29), calls=%async_computation | async-start | bytes 655360 | tf_op jit(solution)/shard_map/all_to_all | solution.py:584
  15.6 13.6 %copy-start.6 = (s32[32]{0:T(128)S(1)}, s32[32]{0:T(128)}, u32[]{:S(2)}) copy-start(s32[32]{0:T(128)} %parents_ref.1) | copy-start | bytes 388
  15.7 38.1 %copy-start.1 = (bf16[1,768,1024]{2,1,0:T(8,128)(2,1)S(1)}, bf16[1,768,1024]{2,1,0:T(8,128)(2,1)}, u32[]{:S(2)}) copy-start(bf16[1,768,1024]{2,1,0:T(8,128)(2,1)} %d_out_ref.5) | copy-start | bytes 4718596
  15.7 38.0 %copy-start.4 = (f32[1024]{0:T(1024)S(1)}, f32[1024]{0:T(1024)}, u32[]{:S(2)}) copy-start(f32[1024]{0:T(1024)} %param.11) | copy-start | bytes 12292
  25.3 1.0 copy-start.2
  70.0 22.4 %all-to-all-start.3 = ((bf16[32,64,128]{2,1,0:T(8,128)(2,1)}), bf16[32,64,128]{2,1,0:T(8,128)(2,1)S(1)}, u32[]{:S(2)}, u32[]{:S(2)}) async-start(bf16[32,64,128]{2,1,0:T(8,128)(2,1)} %grad.1), calls=%async_computation.3 | async-start | bytes 1048576 | tf_op jit(solution)/shard_map/all_to_all | solution.py:584
  74.9 34.0 %copy-start = (bf16[1,768,1024]{2,1,0:T(8,128)(2,1)S(1)}, bf16[1,768,1024]{2,1,0:T(8,128)(2,1)}, u32[]{:S(2)}) copy-start(bf16[1,768,1024]{2,1,0:T(8,128)(2,1)} %values_ref.7) | copy-start | bytes 4718596
  85.8 23.1 %copy-start.3 = (bf16[8,512,128]{2,1,0:T(8,128)(2,1)S(1)}, bf16[8,512,128]{2,1,0:T(8,128)(2,1)}, u32[]{:S(2)}) copy-start(bf16[8,512,128]{2,1,0:T(8,128)(2,1)} %copy-done.2) | copy-start | bytes 3145732

commit v10 on v9

--- a/solution.py
+++ b/solution.py
@@ -219,11 +219,19 @@
             queries = queries_buf[head, part, :]
             keys = keys_buf[head, part, :]
             row = cum_rows_ref[pl.ds(head, 1), part]
-            gaps = row - twice(down(row))
-            mask = jnp.where(col_ids >= row_ids, jnp.exp(gaps), 0.0)
-            weights = (mm_nt(keys, queries) * mask).astype(BF16)
-            weights_buf[head, part, :] = weights
-            within_buf[head, part, :] = mm_tn(weights, values_buf[head, part, :]).astype(BF16)
+            values = values_buf[head, part, :]
+            if number < 2:
+                gaps = twice(down(row)) - row
+                mask = jnp.where(row_ids >= col_ids, jnp.exp(gaps), 0.0)
+                weights = (mm_nt(queries, keys) * mask).astype(BF16)
+                within = mm(weights, values)
+            else:
+                gaps = row - twice(down(row))
+                mask = jnp.where(col_ids >= row_ids, jnp.exp(gaps), 0.0)
+                weights = (mm_nt(keys, queries) * mask).astype(BF16)
+                weights_buf[head] = weights
+                within = mm_tn(weights, values)
+            within_buf[head, part, :] = within.astype(BF16)
             scaled_queries_buf[head, part, :] = rounded_product(queries, down(jnp.exp(row)))
             if number < 2:
                 factor = down(jnp.exp(row[:, BLK - 1 : BLK] - row))
@@ -407,7 +415,10 @@
             row = cum_rows_ref[pl.ds(head, 1), part]
             gaps = row - twice(down(row))
             mask = jnp.where(col_ids >= row_ids, jnp.exp(gaps), 0.0)
-            weights = weights_buf[head, part, :]
+            if number < 2:
+                weights = (mm_nt(keys, queries) * mask).astype(BF16)
+            else:
+                weights = weights_buf[head]
             score_grad = (mm_nt(values, grad) * mask).astype(BF16)
             growth = down(jnp.exp(row))
             start = states_buf[head * BLOCKS + number]
@@ -514,9 +525,9 @@
         within_kernel, "within", [VMEM] + [HBM] * 3,
         [
             (HBM, shape((FAR, ROWS, HD), BF16)), (HBM, shape(HEAD_PROMPT, BF16)),
-            (HBM, shape((FAR // 2, ROWS, BLK), BF16)), (VMEM, shape((8, HD), F32)),
-        ],
-        [(HEAD_ROWS, BF16)] * 5 + [(HEAD_PROMPT, BF16), ((HL, ROWS, BLK), BF16)],
+            (HBM, shape((FAR * 3 // 2, BLK, BLK), BF16)), (VMEM, shape((8, HD), F32)),
+        ],
+        [(HEAD_ROWS, BF16)] * 5 + [(HEAD_PROMPT, BF16), ((HL, BLK, BLK), BF16)],
         [3, 4], 52, 4e9, 16,
     )(cum_rows, queries, keys, values)
 
@@ -558,7 +569,7 @@
             (HBM, WIDE), (HBM, WIDE), (HBM, WIDE), (HBM, WIDE),
             (HBM, shape((4 * FAR, HD, HD), F32)), (VMEM, shape((8, HD), F32)),
         ],
-        [(HEAD_ROWS, BF16)] * 5 + [((HL * BLOCKS, HD, HD), BF16), ((HL, ROWS, BLK), BF16)]
+        [(HEAD_ROWS, BF16)] * 5 + [((HL * BLOCKS, HD, HD), BF16), ((HL, BLK, BLK), BF16)]
         + [(HEAD_ROWS, BF16)] * 4
         + [(STATE, F32), (CUM, F32), (CUM, F32)],
         [7, 5], 53, 6e9, 24,

time: 113 us -> 111 us (0.982)
  blocking collectives: 49.8 us -> 48.2 us
    all_to_all x3, blocking collectives: 49.8 us -> 48.2 us  [everyone(): return lax.all_to_all(array, axis, 0, 0, tiled=True)]
    pallas_call x1, Pallas kernels: 9.65 us -> 8.03 us  [inside(): call(within_kernel, 'within', [VMEM] + [HBM] * 3, [(HBM, shape((FAR, ROWS...]
    pallas_call x1, Pallas kernels: 10.9 us -> 12.1 us  [local_grads(): call(local_grads_kernel, 'local_grads', [VMEM] * 3 + [HBM] * 7, [(HBM, WI...]
where the time goes in v10:
time: 111 us
  blocking collectives  48.2 us (43%)
  Pallas kernels  34.1 us (31%)
  starting transfers between devices  16.1 us (15%)
  waiting for transfers between devices  9.95 us (9%)
  local copies, waits for them, and re-layouts  1.74 us (2%)
    all_to_all x3, blocking collectives, everyone(): return lax.all_to_all(array, axis, 0, 0, tiled=True)  48.2 us
    all_to_all x2, starting transfers between devices, everyone(): return lax.all_to_all(array, axis, 0, 0, tiled=True)  16.1 us
    pallas_call x1, Pallas kernels, local_grads(): call(local_grads_kernel, 'local_grads', [VMEM] * 3 + [HBM] * 7, [(HBM, WI...  12.1 us
    all_to_all x2, waiting for transfers between devices, everyone(): return lax.all_to_all(array, axis, 0, 0, tiled=True)  9.95 us
    pallas_call x1, Pallas kernels, inside(): call(within_kernel, 'within', [VMEM] + [HBM] * 3, [(HBM, shape((FAR, ROWS...  8.03 us
    pallas_call x1, Pallas kernels, attend(): call(attend_kernel, 'attend', [VMEM] * 5 + [HBM], [(VMEM, shape(HEAD_ROWS...  4.14 us
    pallas_call x1, Pallas kernels, far_grads(): call(far_grads_kernel, 'far_grads', [VMEM] * 5 + [HBM] * 3, [(HBM, WIDE),...  3.59 us
    pallas_call x1, Pallas kernels, summarize(): call(summary_kernel, 'summary', [HBM, HBM, HBM], [(HBM, shape(SENT_PIECES...  3.07 us
  transfers between devices with their start and end apart: 2, of which 2 were waited for; matrix products, arithmetic and copies ran while one was open for 0% of the time, Pallas kernels for 18%

profile of v10, /device:TPU:32, one launch (start us, length us, event | category | flops | bytes accessed | tf_op | source)
XLA Modules:
  0.0 110.8 jit_solution(5044539444362632045)
XLA Ops:
  0.6 0.0 copy-start.5
  0.6 0.7 copy-done.5
  1.4 3.1 %summary.1 = (bf16[32,40,128]{2,1,0:T(8,128)(2,1)}, f32[8,128,128]{2,1,0:T(8,128)S(1)}, f32[8,768]{1,0:T(8,128)S(1)}, f32[8,8,128]{2,1,0:T(8,128)S(1)}) custom-call(f32[1,8,768]{2,1,0:T(8,128)S(1)} %bitcast.5, bf16[1,768,1024]{2,1,0:T(8,128)(2,1)} %keys_ref.5, bf16[1,768,1024]{2,1,0:T(8,128)(2,1)} %values_ref.7), custom_call_target="tpu_custom_call" | custom-call | flops 300000000 | bytes 4194304 | tf_op jit(solution)/shard_map/summary/pallas_call | solution.py:512
  4.4 11.2 %all-to-all-start = ((bf16[32,40,128]{2,1,0:T(8,128)(2,1)}), bf16[32,40,128]{2,1,0:T(8,128)(2,1)S(1)}, u32[]{:S(2)}, u32[]{:S(2)}) async-start(bf16[32,40,128]{2,1,0:T(8,128)(2,1)} %get-tuple-element.29), calls=%async_computation | async-start | bytes 655360 | tf_op jit(solution)/shard_map/all_to_all | solution.py:595
  15.6 0.0 copy-start.6
  15.7 0.0 copy-start.1
  15.7 0.0 copy-start.4
  15.7 8.0 %within.1 = (bf16[100,768,128]{2,1,0:T(8,128)(2,1)}, bf16[8,512,128]{2,1,0:T(8,128)(2,1)S(1)}, bf16[150,256,256]{2,1,0:T(8,128)(2,1)}, f32[8,128]{1,0:T(8,128)S(1)}) custom-call(f32[8,768]{1,0:T(8,128)S(1)} %get-tuple-element.27.cum_rows_ref, bf16[1,768,1024]{2,1,0:T(8,128)(2,1)} %queries_ref.3, bf16[1,768,1024]{2,1,0:T(8,128)(2,1)} %keys_ref.5, ...), custom_call_target="tpu_custom_call" | custom-call | flops 4000000000 | bytes 16777216 | tf_op jit(solution)/shard_map/within/pallas_call | solution.py:524
  23.7 0.0 copy-start.2
  23.7 1.0 copy-done.2
  24.7 4.5 %all-to-all-done.got_ref = bf16[32,40,128]{2,1,0:T(8,128)(2,1)S(1)} async-done(((bf16[32,40,128]{2,1,0:T(8,128)(2,1)}), bf16[32,40,128]{2,1,0:T(8,128)(2,1)S(1)}, u32[]{:S(2)}, u32[]{:S(2)}) %all-to-all-start) | async-done | bytes 327712 | tf_op jit(solution)/shard_map/all_to_all | solution.py:595
  29.2 0.0 copy-done.6
  29.2 0.7 forward_scan.1
  30.0 22.1 %all_to_all.25.starts_ref = bf16[32,64,128]{2,1,0:T(8,128)(2,1)S(1)} all-to-all(bf16[32,64,128]{2,1,0:T(8,128)(2,1)S(1)} %get-tuple-element.31), channel_id=1, replica_groups=mesh['seq'=32,'head'=8] {'seq'}, dimensions={0} | all-to-all | bytes 1048576 | tf_op jit(solution)/shard_map/all_to_all | solution.py:595
  52.1 0.0 copy-done.1
  52.1 0.0 copy-done.4
  52.1 4.1 %attend.1 = (bf16[8,768,128]{2,1,0:T(8,128)(2,1)S(1)}, bf16[8,768,128]{2,1,0:T(8,128)(2,1)S(1)}, f32[8,16,128]{2,1,0:T(8,128)S(1)}, bf16[100,768,128]{2,1,0:T(8,128)(2,1)}, bf16[600,128,128]{2,1,0:T(8,128)(2,1)}) custom-call(f32[8,8,128]{2,1,0:T(8,128)S(1)} %get-tuple-element.28.ends_ref, f32[8,128]{1,0:T(8,128)S(1)} %bitcast.2, ...), custom_call_target="tpu_custom_call" | custom-call | flops 300000000 | bytes 10485760 | tf_op jit(solution)/shard_map/attend/pallas_call | solution.py:544
  56.2 9.9 %all_to_all.26.stats_ref = f32[8,16,128]{2,1,0:T(8,128)S(1)} all-to-all(f32[8,16,128]{2,1,0:T(8,128)S(1)} %get-tuple-element.34), channel_id=1, replica_groups=mesh['seq'=32,'head'=8] {'head'}, dimensions={0} | all-to-all | bytes 131072 | tf_op jit(solution)/shard_map/all_to_all | solution.py:595
  66.1 2.2 %grad.1 = bf16[32,64,128]{2,1,0:T(8,128)(2,1)} custom-call(f32[8,8,128]{2,1,0:T(8,128)S(1)} %get-tuple-element.28.ends_ref, f32[8,128]{1,0:T(8,128)S(1)} %bitcast.3, f32[8,16,128]{2,1,0:T(8,128)S(1)} %all_to_all.26.stats_ref, bf16[8,768,128]{2,1,0:T(8,128)(2,1)S(1)} %get-tuple-element.40.queries_ref, bf16[1,768,1024]{2,1,0:T(8,128)(2,1)S(1)} %copy-done.1, ...), custom_call_target="tpu_custom_call" | custom-call | flops 300000000 | bytes 10485760 | tf_op jit(solution)/shard_map/grad/pallas_call | solution.py:557
  68.4 4.9 %all-to-all-start.3 = ((bf16[32,64,128]{2,1,0:T(8,128)(2,1)}), bf16[32,64,128]{2,1,0:T(8,128)(2,1)S(1)}, u32[]{:S(2)}, u32[]{:S(2)}) async-start(bf16[32,64,128]{2,1,0:T(8,128)(2,1)} %grad.1), calls=%async_computation.3 | async-start | bytes 1048576 | tf_op jit(solution)/shard_map/all_to_all | solution.py:595
  73.3 0.0 copy-start
  73.3 12.1 %local_grads.1 = (bf16[1,768,1024]{2,1,0:T(8,128)(2,1)}, bf16[1,768,1024]{2,1,0:T(8,128)(2,1)}, bf16[1,768,1024]{2,1,0:T(8,128)(2,1)}, bf16[1,768,1024]{2,1,0:T(...) custom-call(f32[8,768]{1,0:T(8,128)S(1)} %get-tuple-element.27.cum_rows_ref, ...), custom_call_target="tpu_custom_call" | custom-call | flops 6000000000 | bytes 25165824 | tf_op jit(solution)/shard_map/local_grads/pallas_call | solution.py:566
  85.4 0.0 copy-start.3
  85.4 5.4 %all-to-all-done.3.got_ref = bf16[32,64,128]{2,1,0:T(8,128)(2,1)S(1)} async-done(((bf16[32,64,128]{2,1,0:T(8,128)(2,1)}), bf16[32,64,128]{2,1,0:T(8,128)(2,1)S(1)}, u32[]{:S(2)}, u32[]{:S(2)}) %all-to-all-start.3) | async-done | bytes 524320 | tf_op jit(solution)/shard_map/all_to_all | solution.py:595
  90.8 0.2 backward_scan.1
  91.0 16.2 %all_to_all.27.far_ref = bf16[32,32,128]{2,1,0:T(8,128)(2,1)S(1)} all-to-all(bf16[32,32,128]{2,1,0:T(8,128)(2,1)S(1)} %backward_scan.1), channel_id=1, replica_groups=mesh['seq'=32,'head'=8] {'seq'}, dimensions={0} | all-to-all | bytes 524288 | tf_op jit(solution)/shard_map/all_to_all | solution.py:595
  107.2 0.0 copy-done
  107.2 0.0 copy-done.3
  107.2 3.6 %far_grads.1 = (bf16[1,768,1024]{2,1,0:T(8,128)(2,1)}, bf16[1,768,1024]{2,1,0:T(8,128)(2,1)}) custom-call(f32[8,768]{1,0:T(8,128)S(1)} %get-tuple-element.27.cum_rows_ref, f32[8,8,128]{2,1,0:T(8,128)S(1)} %get-tuple-element.28.ends_ref, bf16[32,32,128]{2,1,0:T(8,128)(2,1)S(1)} %all_to_all.27.far_ref, ...), custom_call_target="tpu_custom_call", output_to_operand_aliasing={{0}: (6, {}), {1}: (7, {})} | custom-call | flops 300000000 | bytes 10485760 | tf_op jit(solution)/shard_map/far_grads/pallas_call | solution.py:580
Async XLA Ops:
  0.6 0.7 copy-start.5
  4.4 24.8 %all-to-all-start = ((bf16[32,40,128]{2,1,0:T(8,128)(2,1)}), bf16[32,40,128]{2,1,0:T(8,128)(2,1)S(1)}, u32[]{:S(2)}, u32[]{:S(2)}) async-start(bf16[32,40,128]{2,1,0:T(8,128)(2,1)} %get-tuple-element.29), calls=%async_computation | async-start | bytes 655360 | tf_op jit(solution)/shard_map/all_to_all | solution.py:595
  15.6 13.6 %copy-start.6 = (s32[32]{0:T(128)S(1)}, s32[32]{0:T(128)}, u32[]{:S(2)}) copy-start(s32[32]{0:T(128)} %parents_ref.1) | copy-start | bytes 388
  15.7 36.4 %copy-start.1 = (bf16[1,768,1024]{2,1,0:T(8,128)(2,1)S(1)}, bf16[1,768,1024]{2,1,0:T(8,128)(2,1)}, u32[]{:S(2)}) copy-start(bf16[1,768,1024]{2,1,0:T(8,128)(2,1)} %d_out_ref.5) | copy-start | bytes 4718596
  15.7 36.4 %copy-start.4 = (f32[1024]{0:T(1024)S(1)}, f32[1024]{0:T(1024)}, u32[]{:S(2)}) copy-start(f32[1024]{0:T(1024)} %param.11) | copy-start | bytes 12292
  23.7 1.0 copy-start.2
  68.4 22.4 %all-to-all-start.3 = ((bf16[32,64,128]{2,1,0:T(8,128)(2,1)}), bf16[32,64,128]{2,1,0:T(8,128)(2,1)S(1)}, u32[]{:S(2)}, u32[]{:S(2)}) async-start(bf16[32,64,128]{2,1,0:T(8,128)(2,1)} %grad.1), calls=%async_computation.3 | async-start | bytes 1048576 | tf_op jit(solution)/shard_map/all_to_all | solution.py:595
  73.3 34.0 %copy-start = (bf16[1,768,1024]{2,1,0:T(8,128)(2,1)S(1)}, bf16[1,768,1024]{2,1,0:T(8,128)(2,1)}, u32[]{:S(2)}) copy-start(bf16[1,768,1024]{2,1,0:T(8,128)(2,1)} %values_ref.7) | copy-start | bytes 4718596
  85.4 21.9 %copy-start.3 = (bf16[8,512,128]{2,1,0:T(8,128)(2,1)S(1)}, bf16[8,512,128]{2,1,0:T(8,128)(2,1)}, u32[]{:S(2)}) copy-start(bf16[8,512,128]{2,1,0:T(8,128)(2,1)} %copy-done.2) | copy-start | bytes 3145732

commit v11 on v10

--- a/solution.py
+++ b/solution.py
@@ -528,7 +528,7 @@
             (HBM, shape((FAR * 3 // 2, BLK, BLK), BF16)), (VMEM, shape((8, HD), F32)),
         ],
         [(HEAD_ROWS, BF16)] * 5 + [(HEAD_PROMPT, BF16), ((HL, BLK, BLK), BF16)],
-        [3, 4], 52, 4e9, 16,
+        [3, 4], 53, 4e9, 16,
     )(cum_rows, queries, keys, values)
 
 

time: 111 us -> 110 us (level)
  waiting for transfers between devices: 9.95 us -> 11.5 us
    all_to_all x2, waiting for transfers between devices: 9.95 us -> 11.5 us  [everyone(): return lax.all_to_all(array, axis, 0, 0, tiled=True)]
where the time goes in v11:
time: 110 us
  blocking collectives  47.4 us (43%)
  Pallas kernels  33.6 us (31%)
  starting transfers between devices  16.1 us (15%)
  waiting for transfers between devices  11.5 us (10%)
    all_to_all x3, blocking collectives, everyone(): return lax.all_to_all(array, axis, 0, 0, tiled=True)  47.4 us
    all_to_all x2, starting transfers between devices, everyone(): return lax.all_to_all(array, axis, 0, 0, tiled=True)  16.1 us
    pallas_call x1, Pallas kernels, local_grads(): call(local_grads_kernel, 'local_grads', [VMEM] * 3 + [HBM] * 7, [(HBM, WI...  12.1 us
    all_to_all x2, waiting for transfers between devices, everyone(): return lax.all_to_all(array, axis, 0, 0, tiled=True)  11.5 us
    pallas_call x1, Pallas kernels, inside(): call(within_kernel, 'within', [VMEM] + [HBM] * 3, [(HBM, shape((FAR, ROWS...  7.47 us
    pallas_call x1, Pallas kernels, attend(): call(attend_kernel, 'attend', [VMEM] * 5 + [HBM], [(VMEM, shape(HEAD_ROWS...  4.14 us
    pallas_call x1, Pallas kernels, far_grads(): call(far_grads_kernel, 'far_grads', [VMEM] * 5 + [HBM] * 3, [(HBM, WIDE),...  3.59 us
    pallas_call x1, Pallas kernels, summarize(): call(summary_kernel, 'summary', [HBM, HBM, HBM], [(HBM, shape(SENT_PIECES...  3.07 us
  transfers between devices with their start and end apart: 2, of which 2 were waited for; matrix products, arithmetic and copies ran while one was open for 0% of the time, Pallas kernels for 18%

profile of v11, /device:TPU:32, one launch (start us, length us, event | category | flops | bytes accessed | tf_op | source)
XLA Modules:
  0.0 110.0 jit_solution(10734673158601909274)
XLA Ops:
  0.6 0.0 copy-start.4
  0.6 0.7 copy-done.4
  1.4 3.1 %summary.1 = (bf16[32,40,128]{2,1,0:T(8,128)(2,1)}, f32[8,128,128]{2,1,0:T(8,128)S(1)}, f32[8,768]{1,0:T(8,128)S(1)}, f32[8,8,128]{2,1,0:T(8,128)S(1)}) custom-call(f32[1,8,768]{2,1,0:T(8,128)S(1)} %bitcast.5, bf16[1,768,1024]{2,1,0:T(8,128)(2,1)} %keys_ref.5, bf16[1,768,1024]{2,1,0:T(8,128)(2,1)} %values_ref.7), custom_call_target="tpu_custom_call" | custom-call | flops 300000000 | bytes 4194304 | tf_op jit(solution)/shard_map/summary/pallas_call | solution.py:512
  4.4 11.2 %all-to-all-start = ((bf16[32,40,128]{2,1,0:T(8,128)(2,1)}), bf16[32,40,128]{2,1,0:T(8,128)(2,1)S(1)}, u32[]{:S(2)}, u32[]{:S(2)}) async-start(bf16[32,40,128]{2,1,0:T(8,128)(2,1)} %get-tuple-element.29), calls=%async_computation | async-start | bytes 655360 | tf_op jit(solution)/shard_map/all_to_all | solution.py:595
  15.6 0.0 copy-start.5
  15.7 0.0 copy-start.1
  15.7 0.0 copy-start.3
  15.7 7.5 %within.1 = (bf16[100,768,128]{2,1,0:T(8,128)(2,1)}, bf16[8,512,128]{2,1,0:T(8,128)(2,1)}, bf16[150,256,256]{2,1,0:T(8,128)(2,1)}, f32[8,128]{1,0:T(8,128)S(1)}) custom-call(f32[8,768]{1,0:T(8,128)S(1)} %get-tuple-element.27.cum_rows_ref, bf16[1,768,1024]{2,1,0:T(8,128)(2,1)} %queries_ref.3, bf16[1,768,1024]{2,1,0:T(8,128)(2,1)} %keys_ref.5, ...), custom_call_target="tpu_custom_call" | custom-call | flops 4000000000 | bytes 16777216 | tf_op jit(solution)/shard_map/within/pallas_call | solution.py:524
  23.2 6.1 %all-to-all-done.got_ref = bf16[32,40,128]{2,1,0:T(8,128)(2,1)S(1)} async-done(((bf16[32,40,128]{2,1,0:T(8,128)(2,1)}), bf16[32,40,128]{2,1,0:T(8,128)(2,1)S(1)}, u32[]{:S(2)}, u32[]{:S(2)}) %all-to-all-start) | async-done | bytes 327712 | tf_op jit(solution)/shard_map/all_to_all | solution.py:595
  29.2 0.0 copy-done.5
  29.2 0.7 forward_scan.1
  30.0 21.2 %all_to_all.25.starts_ref = bf16[32,64,128]{2,1,0:T(8,128)(2,1)S(1)} all-to-all(bf16[32,64,128]{2,1,0:T(8,128)(2,1)S(1)} %get-tuple-element.31), channel_id=1, replica_groups=mesh['seq'=32,'head'=8] {'seq'}, dimensions={0} | all-to-all | bytes 1048576 | tf_op jit(solution)/shard_map/all_to_all | solution.py:595
  51.2 0.0 copy-done.1
  51.2 0.0 copy-done.3
  51.2 4.1 %attend.1 = (bf16[8,768,128]{2,1,0:T(8,128)(2,1)S(1)}, bf16[8,768,128]{2,1,0:T(8,128)(2,1)S(1)}, f32[8,16,128]{2,1,0:T(8,128)S(1)}, bf16[100,768,128]{2,1,0:T(8,128)(2,1)}, bf16[600,128,128]{2,1,0:T(8,128)(2,1)}) custom-call(f32[8,8,128]{2,1,0:T(8,128)S(1)} %get-tuple-element.28.ends_ref, f32[8,128]{1,0:T(8,128)S(1)} %bitcast.2, ...), custom_call_target="tpu_custom_call" | custom-call | flops 300000000 | bytes 10485760 | tf_op jit(solution)/shard_map/attend/pallas_call | solution.py:544
  55.4 9.9 %all_to_all.26.stats_ref = f32[8,16,128]{2,1,0:T(8,128)S(1)} all-to-all(f32[8,16,128]{2,1,0:T(8,128)S(1)} %get-tuple-element.34), channel_id=1, replica_groups=mesh['seq'=32,'head'=8] {'head'}, dimensions={0} | all-to-all | bytes 131072 | tf_op jit(solution)/shard_map/all_to_all | solution.py:595
  65.3 2.2 %grad.1 = bf16[32,64,128]{2,1,0:T(8,128)(2,1)} custom-call(f32[8,8,128]{2,1,0:T(8,128)S(1)} %get-tuple-element.28.ends_ref, f32[8,128]{1,0:T(8,128)S(1)} %bitcast.3, f32[8,16,128]{2,1,0:T(8,128)S(1)} %all_to_all.26.stats_ref, bf16[8,768,128]{2,1,0:T(8,128)(2,1)S(1)} %get-tuple-element.40.queries_ref, bf16[1,768,1024]{2,1,0:T(8,128)(2,1)S(1)} %copy-done.1, ...), custom_call_target="tpu_custom_call" | custom-call | flops 300000000 | bytes 10485760 | tf_op jit(solution)/shard_map/grad/pallas_call | solution.py:557
  67.5 4.9 %all-to-all-start.3 = ((bf16[32,64,128]{2,1,0:T(8,128)(2,1)}), bf16[32,64,128]{2,1,0:T(8,128)(2,1)S(1)}, u32[]{:S(2)}, u32[]{:S(2)}) async-start(bf16[32,64,128]{2,1,0:T(8,128)(2,1)} %grad.1), calls=%async_computation.3 | async-start | bytes 1048576 | tf_op jit(solution)/shard_map/all_to_all | solution.py:595
  72.4 0.0 copy-start
  72.4 12.1 %local_grads.1 = (bf16[1,768,1024]{2,1,0:T(8,128)(2,1)}, bf16[1,768,1024]{2,1,0:T(8,128)(2,1)}, bf16[1,768,1024]{2,1,0:T(8,128)(2,1)}, bf16[1,768,1024]{2,1,0:T(...) custom-call(f32[8,768]{1,0:T(8,128)S(1)} %get-tuple-element.27.cum_rows_ref, ...), custom_call_target="tpu_custom_call" | custom-call | flops 6000000000 | bytes 25165824 | tf_op jit(solution)/shard_map/local_grads/pallas_call | solution.py:566
  84.5 0.0 copy-start.2
  84.5 5.4 %all-to-all-done.3.got_ref = bf16[32,64,128]{2,1,0:T(8,128)(2,1)S(1)} async-done(((bf16[32,64,128]{2,1,0:T(8,128)(2,1)}), bf16[32,64,128]{2,1,0:T(8,128)(2,1)S(1)}, u32[]{:S(2)}, u32[]{:S(2)}) %all-to-all-start.3) | async-done | bytes 524320 | tf_op jit(solution)/shard_map/all_to_all | solution.py:595
  89.9 0.2 backward_scan.1
  90.2 16.2 %all_to_all.27.far_ref = bf16[32,32,128]{2,1,0:T(8,128)(2,1)S(1)} all-to-all(bf16[32,32,128]{2,1,0:T(8,128)(2,1)S(1)} %backward_scan.1), channel_id=1, replica_groups=mesh['seq'=32,'head'=8] {'seq'}, dimensions={0} | all-to-all | bytes 524288 | tf_op jit(solution)/shard_map/all_to_all | solution.py:595
  106.4 0.0 copy-done
  106.4 0.0 copy-done.2
  106.4 3.6 %far_grads.1 = (bf16[1,768,1024]{2,1,0:T(8,128)(2,1)}, bf16[1,768,1024]{2,1,0:T(8,128)(2,1)}) custom-call(f32[8,768]{1,0:T(8,128)S(1)} %get-tuple-element.27.cum_rows_ref, f32[8,8,128]{2,1,0:T(8,128)S(1)} %get-tuple-element.28.ends_ref, bf16[32,32,128]{2,1,0:T(8,128)(2,1)S(1)} %all_to_all.27.far_ref, ...), custom_call_target="tpu_custom_call", output_to_operand_aliasing={{0}: (6, {}), {1}: (7, {})} | custom-call | flops 300000000 | bytes 10485760 | tf_op jit(solution)/shard_map/far_grads/pallas_call | solution.py:580
Async XLA Ops:
  0.6 0.7 copy-start.4
  4.4 24.8 %all-to-all-start = ((bf16[32,40,128]{2,1,0:T(8,128)(2,1)}), bf16[32,40,128]{2,1,0:T(8,128)(2,1)S(1)}, u32[]{:S(2)}, u32[]{:S(2)}) async-start(bf16[32,40,128]{2,1,0:T(8,128)(2,1)} %get-tuple-element.29), calls=%async_computation | async-start | bytes 655360 | tf_op jit(solution)/shard_map/all_to_all | solution.py:595
  15.6 13.6 %copy-start.5 = (s32[32]{0:T(128)S(1)}, s32[32]{0:T(128)}, u32[]{:S(2)}) copy-start(s32[32]{0:T(128)} %parents_ref.1) | copy-start | bytes 388
  15.7 35.6 %copy-start.1 = (bf16[1,768,1024]{2,1,0:T(8,128)(2,1)S(1)}, bf16[1,768,1024]{2,1,0:T(8,128)(2,1)}, u32[]{:S(2)}) copy-start(bf16[1,768,1024]{2,1,0:T(8,128)(2,1)} %d_out_ref.5) | copy-start | bytes 4718596
  15.7 35.6 %copy-start.3 = (f32[1024]{0:T(1024)S(1)}, f32[1024]{0:T(1024)}, u32[]{:S(2)}) copy-start(f32[1024]{0:T(1024)} %param.11) | copy-start | bytes 12292
  67.5 22.4 %all-to-all-start.3 = ((bf16[32,64,128]{2,1,0:T(8,128)(2,1)}), bf16[32,64,128]{2,1,0:T(8,128)(2,1)S(1)}, u32[]{:S(2)}, u32[]{:S(2)}) async-start(bf16[32,64,128]{2,1,0:T(8,128)(2,1)} %grad.1), calls=%async_computation.3 | async-start | bytes 1048576 | tf_op jit(solution)/shard_map/all_to_all | solution.py:595
  72.4 34.0 %copy-start = (bf16[1,768,1024]{2,1,0:T(8,128)(2,1)S(1)}, bf16[1,768,1024]{2,1,0:T(8,128)(2,1)}, u32[]{:S(2)}) copy-start(bf16[1,768,1024]{2,1,0:T(8,128)(2,1)} %values_ref.7) | copy-start | bytes 4718596
  84.5 21.9 %copy-start.2 = (bf16[8,512,128]{2,1,0:T(8,128)(2,1)S(1)}, bf16[8,512,128]{2,1,0:T(8,128)(2,1)}, u32[]{:S(2)}) copy-start(bf16[8,512,128]{2,1,0:T(8,128)(2,1)} %get-tuple-element.44.scaled_keys_ref) | copy-start | bytes 3145732

commit v12 on v11

--- a/solution.py
+++ b/solution.py
@@ -425,7 +425,7 @@
             grad_queries = mm_tn(score_grad, keys) + growth * mm_nt(grad, start)
             d_queries_buf[head, part, :] = grad_queries.astype(BF16)
             if number == 1:
-                term_buf[head] = mm_tn(rounded_product(queries, growth), grad)
+                term_buf[head] = mm_tn(rounded_product(queries, growth), grad).astype(BF16)
             d_keys_buf[head, part, :] = mm(score_grad, queries).astype(BF16)
             d_values_buf[head, part, :] = mm(weights, grad).astype(BF16)
 
@@ -455,7 +455,7 @@
 
     def body(head):
         second = far_ref[pl.ds(head * PARTS, PARTS)].reshape(HD, HD)
-        first = (ends_ref[head][1:2, :] * second.astype(F32) + term_buf[head]).astype(BF16)
+        first = (ends_ref[head][1:2, :] * second.astype(F32) + term_buf[head].astype(F32)).astype(BF16)
         for number, end_grad in enumerate((first, second)):
             part = rows(number)
             row = cum_rows_ref[pl.ds(head, 1), part]
@@ -567,11 +567,11 @@
         local_grads_kernel, "local_grads", [VMEM] * 3 + [HBM] * 7,
         [
             (HBM, WIDE), (HBM, WIDE), (HBM, WIDE), (HBM, WIDE),
-            (HBM, shape((4 * FAR, HD, HD), F32)), (VMEM, shape((8, HD), F32)),
+            (HBM, shape((8 * FAR, HD, HD), BF16)), (VMEM, shape((8, HD), F32)),
         ],
         [(HEAD_ROWS, BF16)] * 5 + [((HL * BLOCKS, HD, HD), BF16), ((HL, BLK, BLK), BF16)]
         + [(HEAD_ROWS, BF16)] * 4
-        + [(STATE, F32), (CUM, F32), (CUM, F32)],
+        + [(STATE, BF16), (CUM, F32), (CUM, F32)],
         [7, 5], 53, 6e9, 24,
     )(cum_rows, stats, gains, queries, keys, values, d_out, attended, states, weights)
 
@@ -580,7 +580,7 @@
     return call(
         far_grads_kernel, "far_grads", [VMEM] * 5 + [HBM] * 3,
         [(HBM, WIDE), (HBM, WIDE)],
-        [(STATE, F32)] + [(HEAD_PROMPT, BF16)] * 4, [3, 2], 44, 3e8, 10, {6: 0, 7: 1},
+        [(STATE, BF16)] + [(HEAD_PROMPT, BF16)] * 4, [3, 2], 44, 3e8, 10, {6: 0, 7: 1},
     )(cum_rows, ends, far, scaled_keys, values, term, near_keys, near_values)
 
 

time: 110 us -> 110 us (level)
  no operation moved by 1% of the time
where the time goes in v12:
time: 110 us
  blocking collectives  47.4 us (43%)
  Pallas kernels  33.5 us (30%)
  starting transfers between devices  16.1 us (15%)
  waiting for transfers between devices  11.5 us (10%)
    all_to_all x3, blocking collectives, everyone(): return lax.all_to_all(array, axis, 0, 0, tiled=True)  47.4 us
    all_to_all x2, starting transfers between devices, everyone(): return lax.all_to_all(array, axis, 0, 0, tiled=True)  16.1 us
    pallas_call x1, Pallas kernels, local_grads(): call(local_grads_kernel, 'local_grads', [VMEM] * 3 + [HBM] * 7, [(HBM, WI...  12.1 us
    all_to_all x2, waiting for transfers between devices, everyone(): return lax.all_to_all(array, axis, 0, 0, tiled=True)  11.5 us
    pallas_call x1, Pallas kernels, inside(): call(within_kernel, 'within', [VMEM] + [HBM] * 3, [(HBM, shape((FAR, ROWS...  7.47 us
    pallas_call x1, Pallas kernels, attend(): call(attend_kernel, 'attend', [VMEM] * 5 + [HBM], [(VMEM, shape(HEAD_ROWS...  4.14 us
    pallas_call x1, Pallas kernels, far_grads(): call(far_grads_kernel, 'far_grads', [VMEM] * 5 + [HBM] * 3, [(HBM, WIDE),...  3.52 us
    pallas_call x1, Pallas kernels, summarize(): call(summary_kernel, 'summary', [HBM, HBM, HBM], [(HBM, shape(SENT_PIECES...  3.07 us
  transfers between devices with their start and end apart: 2, of which 2 were waited for; matrix products, arithmetic and copies ran while one was open for 0% of the time, Pallas kernels for 18%

profile of v12, /device:TPU:32, one launch (start us, length us, event | category | flops | bytes accessed | tf_op | source)
XLA Modules:
  0.0 109.9 jit_solution(13409740465105698102)
XLA Ops:
  0.6 0.0 copy-start.4
  0.6 0.7 copy-done.4
  1.4 3.1 %summary.1 = (bf16[32,40,128]{2,1,0:T(8,128)(2,1)}, f32[8,128,128]{2,1,0:T(8,128)S(1)}, f32[8,768]{1,0:T(8,128)S(1)}, f32[8,8,128]{2,1,0:T(8,128)S(1)}) custom-call(f32[1,8,768]{2,1,0:T(8,128)S(1)} %bitcast.5, bf16[1,768,1024]{2,1,0:T(8,128)(2,1)} %keys_ref.5, bf16[1,768,1024]{2,1,0:T(8,128)(2,1)} %values_ref.7), custom_call_target="tpu_custom_call" | custom-call | flops 300000000 | bytes 4194304 | tf_op jit(solution)/shard_map/summary/pallas_call | solution.py:512
  4.4 11.2 %all-to-all-start = ((bf16[32,40,128]{2,1,0:T(8,128)(2,1)}), bf16[32,40,128]{2,1,0:T(8,128)(2,1)S(1)}, u32[]{:S(2)}, u32[]{:S(2)}) async-start(bf16[32,40,128]{2,1,0:T(8,128)(2,1)} %get-tuple-element.29), calls=%async_computation | async-start | bytes 655360 | tf_op jit(solution)/shard_map/all_to_all | solution.py:595
  15.6 0.0 copy-start.5
  15.7 0.0 copy-start.1
  15.7 0.0 copy-start.3
  15.7 7.5 %within.1 = (bf16[100,768,128]{2,1,0:T(8,128)(2,1)}, bf16[8,512,128]{2,1,0:T(8,128)(2,1)}, bf16[150,256,256]{2,1,0:T(8,128)(2,1)}, f32[8,128]{1,0:T(8,128)S(1)}) custom-call(f32[8,768]{1,0:T(8,128)S(1)} %get-tuple-element.27.cum_rows_ref, bf16[1,768,1024]{2,1,0:T(8,128)(2,1)} %queries_ref.3, bf16[1,768,1024]{2,1,0:T(8,128)(2,1)} %keys_ref.5, ...), custom_call_target="tpu_custom_call" | custom-call | flops 4000000000 | bytes 16777216 | tf_op jit(solution)/shard_map/within/pallas_call | solution.py:524
  23.2 6.1 %all-to-all-done.got_ref = bf16[32,40,128]{2,1,0:T(8,128)(2,1)S(1)} async-done(((bf16[32,40,128]{2,1,0:T(8,128)(2,1)}), bf16[32,40,128]{2,1,0:T(8,128)(2,1)S(1)}, u32[]{:S(2)}, u32[]{:S(2)}) %all-to-all-start) | async-done | bytes 327712 | tf_op jit(solution)/shard_map/all_to_all | solution.py:595
  29.2 0.0 copy-done.5
  29.2 0.7 forward_scan.1
  30.0 21.2 %all_to_all.25.starts_ref = bf16[32,64,128]{2,1,0:T(8,128)(2,1)S(1)} all-to-all(bf16[32,64,128]{2,1,0:T(8,128)(2,1)S(1)} %get-tuple-element.31), channel_id=1, replica_groups=mesh['seq'=32,'head'=8] {'seq'}, dimensions={0} | all-to-all | bytes 1048576 | tf_op jit(solution)/shard_map/all_to_all | solution.py:595
  51.2 0.0 copy-done.1
  51.2 0.0 copy-done.3
  51.2 4.1 %attend.1 = (bf16[8,768,128]{2,1,0:T(8,128)(2,1)S(1)}, bf16[8,768,128]{2,1,0:T(8,128)(2,1)S(1)}, f32[8,16,128]{2,1,0:T(8,128)S(1)}, bf16[100,768,128]{2,1,0:T(8,128)(2,1)}, bf16[600,128,128]{2,1,0:T(8,128)(2,1)}) custom-call(f32[8,8,128]{2,1,0:T(8,128)S(1)} %get-tuple-element.28.ends_ref, f32[8,128]{1,0:T(8,128)S(1)} %bitcast.2, ...), custom_call_target="tpu_custom_call" | custom-call | flops 300000000 | bytes 10485760 | tf_op jit(solution)/shard_map/attend/pallas_call | solution.py:544
  55.4 9.9 %all_to_all.26.stats_ref = f32[8,16,128]{2,1,0:T(8,128)S(1)} all-to-all(f32[8,16,128]{2,1,0:T(8,128)S(1)} %get-tuple-element.34), channel_id=1, replica_groups=mesh['seq'=32,'head'=8] {'head'}, dimensions={0} | all-to-all | bytes 131072 | tf_op jit(solution)/shard_map/all_to_all | solution.py:595
  65.3 2.2 %grad.1 = bf16[32,64,128]{2,1,0:T(8,128)(2,1)} custom-call(f32[8,8,128]{2,1,0:T(8,128)S(1)} %get-tuple-element.28.ends_ref, f32[8,128]{1,0:T(8,128)S(1)} %bitcast.3, f32[8,16,128]{2,1,0:T(8,128)S(1)} %all_to_all.26.stats_ref, bf16[8,768,128]{2,1,0:T(8,128)(2,1)S(1)} %get-tuple-element.40.queries_ref, bf16[1,768,1024]{2,1,0:T(8,128)(2,1)S(1)} %copy-done.1, ...), custom_call_target="tpu_custom_call" | custom-call | flops 300000000 | bytes 10485760 | tf_op jit(solution)/shard_map/grad/pallas_call | solution.py:557
  67.5 4.9 %all-to-all-start.3 = ((bf16[32,64,128]{2,1,0:T(8,128)(2,1)}), bf16[32,64,128]{2,1,0:T(8,128)(2,1)S(1)}, u32[]{:S(2)}, u32[]{:S(2)}) async-start(bf16[32,64,128]{2,1,0:T(8,128)(2,1)} %grad.1), calls=%async_computation.3 | async-start | bytes 1048576 | tf_op jit(solution)/shard_map/all_to_all | solution.py:595
  72.4 0.0 copy-start
  72.4 12.1 %local_grads.1 = (bf16[1,768,1024]{2,1,0:T(8,128)(2,1)}, bf16[1,768,1024]{2,1,0:T(8,128)(2,1)}, bf16[1,768,1024]{2,1,0:T(8,128)(2,1)}, bf16[1,768,1024]{2,1,0:T(...) custom-call(f32[8,768]{1,0:T(8,128)S(1)} %get-tuple-element.27.cum_rows_ref, ...), custom_call_target="tpu_custom_call" | custom-call | flops 6000000000 | bytes 25165824 | tf_op jit(solution)/shard_map/local_grads/pallas_call | solution.py:566
  84.5 0.0 copy-start.2
  84.5 5.4 %all-to-all-done.3.got_ref = bf16[32,64,128]{2,1,0:T(8,128)(2,1)S(1)} async-done(((bf16[32,64,128]{2,1,0:T(8,128)(2,1)}), bf16[32,64,128]{2,1,0:T(8,128)(2,1)S(1)}, u32[]{:S(2)}, u32[]{:S(2)}) %all-to-all-start.3) | async-done | bytes 524320 | tf_op jit(solution)/shard_map/all_to_all | solution.py:595
  89.9 0.2 backward_scan.1
  90.2 16.2 %all_to_all.27.far_ref = bf16[32,32,128]{2,1,0:T(8,128)(2,1)S(1)} all-to-all(bf16[32,32,128]{2,1,0:T(8,128)(2,1)S(1)} %backward_scan.1), channel_id=1, replica_groups=mesh['seq'=32,'head'=8] {'seq'}, dimensions={0} | all-to-all | bytes 524288 | tf_op jit(solution)/shard_map/all_to_all | solution.py:595
  106.4 0.0 copy-done
  106.4 0.0 copy-done.2
  106.4 3.5 %far_grads.1 = (bf16[1,768,1024]{2,1,0:T(8,128)(2,1)}, bf16[1,768,1024]{2,1,0:T(8,128)(2,1)}) custom-call(f32[8,768]{1,0:T(8,128)S(1)} %get-tuple-element.27.cum_rows_ref, f32[8,8,128]{2,1,0:T(8,128)S(1)} %get-tuple-element.28.ends_ref, bf16[32,32,128]{2,1,0:T(8,128)(2,1)S(1)} %all_to_all.27.far_ref, ...), custom_call_target="tpu_custom_call", output_to_operand_aliasing={{0}: (6, {}), {1}: (7, {})} | custom-call | flops 300000000 | bytes 10485760 | tf_op jit(solution)/shard_map/far_grads/pallas_call | solution.py:580
Async XLA Ops:
  0.6 0.7 copy-start.4
  4.4 24.8 %all-to-all-start = ((bf16[32,40,128]{2,1,0:T(8,128)(2,1)}), bf16[32,40,128]{2,1,0:T(8,128)(2,1)S(1)}, u32[]{:S(2)}, u32[]{:S(2)}) async-start(bf16[32,40,128]{2,1,0:T(8,128)(2,1)} %get-tuple-element.29), calls=%async_computation | async-start | bytes 655360 | tf_op jit(solution)/shard_map/all_to_all | solution.py:595
  15.6 13.6 %copy-start.5 = (s32[32]{0:T(128)S(1)}, s32[32]{0:T(128)}, u32[]{:S(2)}) copy-start(s32[32]{0:T(128)} %parents_ref.1) | copy-start | bytes 388
  15.7 35.6 %copy-start.1 = (bf16[1,768,1024]{2,1,0:T(8,128)(2,1)S(1)}, bf16[1,768,1024]{2,1,0:T(8,128)(2,1)}, u32[]{:S(2)}) copy-start(bf16[1,768,1024]{2,1,0:T(8,128)(2,1)} %d_out_ref.5) | copy-start | bytes 4718596
  15.7 35.6 %copy-start.3 = (f32[1024]{0:T(1024)S(1)}, f32[1024]{0:T(1024)}, u32[]{:S(2)}) copy-start(f32[1024]{0:T(1024)} %param.11) | copy-start | bytes 12292
  67.5 22.4 %all-to-all-start.3 = ((bf16[32,64,128]{2,1,0:T(8,128)(2,1)}), bf16[32,64,128]{2,1,0:T(8,128)(2,1)S(1)}, u32[]{:S(2)}, u32[]{:S(2)}) async-start(bf16[32,64,128]{2,1,0:T(8,128)(2,1)} %grad.1), calls=%async_computation.3 | async-start | bytes 1048576 | tf_op jit(solution)/shard_map/all_to_all | solution.py:595
  72.4 34.0 %copy-start = (bf16[1,768,1024]{2,1,0:T(8,128)(2,1)S(1)}, bf16[1,768,1024]{2,1,0:T(8,128)(2,1)}, u32[]{:S(2)}) copy-start(bf16[1,768,1024]{2,1,0:T(8,128)(2,1)} %values_ref.7) | copy-start | bytes 4718596
  84.5 21.9 %copy-start.2 = (bf16[8,512,128]{2,1,0:T(8,128)(2,1)S(1)}, bf16[8,512,128]{2,1,0:T(8,128)(2,1)}, u32[]{:S(2)}) copy-start(bf16[8,512,128]{2,1,0:T(8,128)(2,1)} %get-tuple-element.44.scaled_keys_ref) | copy-start | bytes 3145732
